TPU v7x, 32 devices: a whole 2x2x4 slice. The times are simulated.
32 devices in a mesh: dp: 16 (over z, x, core), seq: 2 (over y).
Axes of the slice: x: 2, y: 2, z: 4, core: 2. Of those that a mesh axis runs over, the one named last changes fastest.
Arguments:
- tokens: bfloat16 [32, 256, 768], P('dp', 'seq'), may hold values from -6 to 6
- pair: bfloat16 [32, 256, 256, 256], P('dp', 'seq'), may hold values from -6 to 6
- cath_class: int32 [32], P('dp'), may hold values from 0 to 4
- cath_arch: int32 [32], P('dp'), may hold values from 0 to 42
- cath_topo: int32 [32], P('dp'), may hold values from 0 to 1471
- times: float32 [32], P('dp'), may hold values from 0.02 to 1
- out_grad: bfloat16 [32, 256, 768], P('dp', 'seq'), may hold values from -6 to 6
- emb_class: bfloat16 [5, 768], P(None, ('dp', 'seq')), may hold values from -4 to 4
- emb_arch: bfloat16 [43, 768], P(None, ('dp', 'seq')), may hold values from -4 to 4
- emb_topo: bfloat16 [1472, 768], P(None, ('dp', 'seq')), may hold values from -4 to 4
- w_time: bfloat16 [256, 768], P(('dp', 'seq')), may hold values from -0.375 to 0.375
- w_ada: bfloat16 [768, 4608], P(('dp', 'seq')), may hold values from -0.21875 to 0.21875
- w_qkv: bfloat16 [768, 2304], P(('dp', 'seq')), may hold values from -0.21875 to 0.21875
- w_gate: bfloat16 [768, 768], P(('dp', 'seq')), may hold values from -0.21875 to 0.21875
- w_out: bfloat16 [768, 768], P(('dp', 'seq')), may hold values from -0.875 to 0.875
- w_pair: bfloat16 [256, 12], P(('dp', 'seq')), may hold values from -0.375 to 0.375
- w_ffgate: bfloat16 [768, 3072], P(('dp', 'seq')), may hold values from -0.21875 to 0.21875
- w_ffup: bfloat16 [768, 3072], P(('dp', 'seq')), may hold values from -0.21875 to 0.21875
- w_ffdown: bfloat16 [3072, 768], P(('dp', 'seq')), may hold values from -0.109375 to 0.109375
Outputs:
- output: bfloat16 [32, 256, 768], P('dp', 'seq')
- input_grad: bfloat16 [32, 256, 768], P('dp', 'seq')
- pair_grad: bfloat16 [32, 256, 256, 256], P('dp', 'seq')
- grad_emb_class: float32 [5, 768], P(None, ('dp', 'seq'))
- grad_emb_arch: float32 [43, 768], P(None, ('dp', 'seq'))
- grad_emb_topo: float32 [1472, 768], P(None, ('dp', 'seq'))
- grad_w_time: float32 [256, 768], P(('dp', 'seq'))
- grad_w_ada: float32 [768, 4608], P(('dp', 'seq'))
- grad_w_qkv: float32 [768, 2304], P(('dp', 'seq'))
- grad_w_gate: float32 [768, 768], P(('dp', 'seq'))
- grad_w_out: float32 [768, 768], P(('dp', 'seq'))
- grad_w_pair: float32 [256, 12], P(('dp', 'seq'))
- grad_w_ffgate: float32 [768, 3072], P(('dp', 'seq'))
- grad_w_ffup: float32 [768, 3072], P(('dp', 'seq'))
- grad_w_ffdown: float32 [3072, 768], P(('dp', 'seq'))
All inputs are finite; a program needn't handle non-finite values.
Results may differ from a plain program's by a relative error of at most 0.017.
The roundings to bfloat16 on the way count: a program that leaves them out, or rounds other values in their place, can miss the bound.
Values may be sent and summed in bfloat16 or wider, within the bound.
No kernel may reach another device: no remote copies, remote signals or barrier semaphores. Data moves between devices by JAX's collectives and lax.ppermute only.
A program may use at most 256 MiB of HBM per device.

v0:
```python
import math

import jax
import jax.numpy as jnp
from jax import lax
from jax.sharding import PartitionSpec as P

EPSILON = 1e-06
TIME_SCALE = 100.0


def modulate(rows, shift, scale):
    centre = rows - jnp.mean(rows, axis=-1, keepdims=True)
    spread = jnp.mean(centre * centre, axis=-1, keepdims=True)
    return centre * lax.rsqrt(spread + EPSILON) * (1.0 + scale) + shift


def swiglu(gate_part, up_part):
    return jax.nn.silu(gate_part) * up_part


def time_features(moment, width):
    half_width = width // 2
    frequency = jnp.exp(-math.log(10000.0) * jnp.arange(half_width, dtype=jnp.float32) / half_width)
    angles = TIME_SCALE * moment[:, None] * frequency[None, :]
    return jnp.concatenate([jnp.sin(angles), jnp.cos(angles)], axis=-1)


def outer_sum(left, right):
    return jnp.dot(left.astype(jnp.float32).T, right, precision=lax.Precision.HIGHEST)


def chain_step(weights, rows_in, pair_rows, label_class, label_arch, label_topo, moment, cotangent):
    (
        emb_class,
        emb_arch,
        emb_topo,
        w_time,
        w_ada,
        w_qkv,
        w_gate,
        w_out,
        w_pair,
        w_ffgate,
        w_ffup,
        w_ffdown,
    ) = weights
    f32 = jnp.float32
    bf16 = jnp.bfloat16
    width = rows_in.shape[-1]
    local_rows = rows_in.shape[0]
    length = pair_rows.shape[1]
    heads = w_pair.shape[1]
    head_size = width // heads
    factor = head_size ** (-0.5)
    features = time_features(moment[None], w_time.shape[0]).astype(bf16)
    hot_class = (jnp.arange(emb_class.shape[0], dtype=jnp.int32) == label_class).astype(bf16)[
        None, :
    ]
    hot_arch = (jnp.arange(emb_arch.shape[0], dtype=jnp.int32) == label_arch).astype(bf16)[None, :]
    hot_topo = (jnp.arange(emb_topo.shape[0], dtype=jnp.int32) == label_topo).astype(bf16)[None, :]
    before = (
        jnp.dot(hot_class, emb_class, preferred_element_type=f32)
        + jnp.dot(hot_arch, emb_arch, preferred_element_type=f32)
        + jnp.dot(hot_topo, emb_topo, preferred_element_type=f32)
        + jnp.dot(features, w_time, preferred_element_type=f32)
    )
    condition, silu_back = jax.vjp(jax.nn.silu, before)
    condition_low = condition.astype(bf16)
    modes = jnp.dot(condition_low, w_ada, preferred_element_type=f32)
    shift_one, scale_one, gate_one, shift_two, scale_two, gate_two = jnp.split(modes, 6, axis=-1)
    rows = rows_in.astype(f32)
    modulated_one, norm_one_back = jax.vjp(modulate, rows, shift_one, scale_one)
    normed_one = modulated_one.astype(bf16)
    projected = jnp.dot(normed_one, w_qkv, preferred_element_type=f32).astype(bf16)
    gate_logits = jnp.dot(normed_one, w_gate, preferred_element_type=f32)
    queries = projected[:, :width].reshape(local_rows, heads, head_size)
    gathered = lax.all_gather(projected[:, width:], "seq", axis=0, tiled=True)
    keys = gathered[:, :width].reshape(length, heads, head_size)
    values = gathered[:, width:].reshape(length, heads, head_size)
    bias = jnp.einsum("ijc,ch->hij", pair_rows, w_pair, preferred_element_type=f32)
    scores = jnp.einsum("ihd,jhd->hij", queries, keys, preferred_element_type=f32) * factor + bias
    probs = jax.nn.softmax(scores, axis=-1)
    probs_low = probs.astype(bf16)
    attended = jnp.einsum("hij,jhd->ihd", probs_low, values, preferred_element_type=f32).reshape(
        local_rows, width
    )
    sigmoid_gate = jax.nn.sigmoid(gate_logits)
    gated = (attended * sigmoid_gate).astype(bf16)
    branch_one = jnp.dot(gated, w_out, preferred_element_type=f32)
    middle = rows + gate_one * branch_one
    modulated_two, norm_two_back = jax.vjp(modulate, middle, shift_two, scale_two)
    normed_two = modulated_two.astype(bf16)
    ff_gate = jnp.dot(normed_two, w_ffgate, preferred_element_type=f32)
    ff_up = jnp.dot(normed_two, w_ffup, preferred_element_type=f32)
    activated, swiglu_back = jax.vjp(swiglu, ff_gate, ff_up)
    hidden = activated.astype(bf16)
    branch_two = jnp.dot(hidden, w_ffdown, preferred_element_type=f32)
    result = (middle + gate_two * branch_two).astype(bf16)
    upstream = cotangent.astype(f32)
    branch_two_grad = (gate_two * upstream).astype(bf16)
    gate_two_grad = jnp.sum(upstream * branch_two, axis=0, keepdims=True)
    grad_w_ffdown = jnp.einsum("rf,rd->fd", hidden, branch_two_grad, preferred_element_type=f32)
    hidden_grad = jnp.einsum("rd,fd->rf", branch_two_grad, w_ffdown, preferred_element_type=f32)
    ff_gate_full, ff_up_full = swiglu_back(hidden_grad)
    ff_gate_grad = ff_gate_full.astype(bf16)
    ff_up_grad = ff_up_full.astype(bf16)
    grad_w_ffgate = jnp.einsum("rd,rf->df", normed_two, ff_gate_grad, preferred_element_type=f32)
    grad_w_ffup = jnp.einsum("rd,rf->df", normed_two, ff_up_grad, preferred_element_type=f32)
    normed_two_grad = jnp.einsum(
        "rf,df->rd", ff_gate_grad, w_ffgate, preferred_element_type=f32
    ) + jnp.einsum("rf,df->rd", ff_up_grad, w_ffup, preferred_element_type=f32)
    middle_part, shift_two_grad, scale_two_grad = norm_two_back(normed_two_grad)
    middle_grad = upstream + middle_part
    gate_one_grad = jnp.sum(middle_grad * branch_one, axis=0, keepdims=True)
    branch_one_grad = (gate_one * middle_grad).astype(bf16)
    grad_w_out = jnp.einsum("rk,rd->kd", gated, branch_one_grad, preferred_element_type=f32)
    gated_grad = jnp.einsum("rd,kd->rk", branch_one_grad, w_out, preferred_element_type=f32)
    attended_grad = (gated_grad * sigmoid_gate).astype(bf16).reshape(local_rows, heads, head_size)
    logits_grad = (gated_grad * attended * (sigmoid_gate * (1.0 - sigmoid_gate))).astype(bf16)
    value_grad = jnp.einsum("hij,ihd->jhd", probs_low, attended_grad, preferred_element_type=f32)
    probs_grad = jnp.einsum("ihd,jhd->hij", attended_grad, values, preferred_element_type=f32)
    scores_grad = (
        probs * (probs_grad - jnp.sum(probs_grad * probs, axis=-1, keepdims=True))
    ).astype(bf16)
    query_grad = (
        (jnp.einsum("hij,jhd->ihd", scores_grad, keys, preferred_element_type=f32) * factor)
        .reshape(local_rows, width)
        .astype(bf16)
    )
    key_grad = jnp.einsum("hij,ihd->jhd", scores_grad, queries, preferred_element_type=f32) * factor
    joined = jnp.concatenate(
        [key_grad.reshape(length, width), value_grad.reshape(length, width)], axis=1
    )
    owned = (
        lax.psum_scatter(joined.astype(jnp.bfloat16), "seq", scatter_dimension=0, tiled=True)
        .astype(jnp.float32)
        .astype(bf16)
    )
    projected_grad = jnp.concatenate([query_grad, owned], axis=1)
    pairs_grad = jnp.einsum("hij,ch->ijc", scores_grad, w_pair, preferred_element_type=f32).astype(
        bf16
    )
    grad_w_pair = jnp.einsum("ijc,hij->ch", pair_rows, scores_grad, preferred_element_type=f32)
    grad_w_qkv = jnp.einsum("rd,rk->dk", normed_one, projected_grad, preferred_element_type=f32)
    grad_w_gate = jnp.einsum("rd,rk->dk", normed_one, logits_grad, preferred_element_type=f32)
    normed_one_grad = jnp.einsum(
        "rk,dk->rd", projected_grad, w_qkv, preferred_element_type=f32
    ) + jnp.einsum("rk,dk->rd", logits_grad, w_gate, preferred_element_type=f32)
    rows_part, shift_one_grad, scale_one_grad = norm_one_back(normed_one_grad)
    tokens_grad = (middle_grad + rows_part).astype(bf16)
    modes_grad = jnp.concatenate(
        [
            shift_one_grad,
            scale_one_grad,
            gate_one_grad,
            shift_two_grad,
            scale_two_grad,
            gate_two_grad,
        ],
        axis=-1,
    )
    grad_w_ada = outer_sum(condition_low, modes_grad)
    condition_grad = jnp.dot(modes_grad, w_ada.astype(f32).T, precision=lax.Precision.HIGHEST)
    (before_grad,) = silu_back(condition_grad)
    grad_emb_class = outer_sum(hot_class, before_grad)
    grad_emb_arch = outer_sum(hot_arch, before_grad)
    grad_emb_topo = outer_sum(hot_topo, before_grad)
    grad_w_time = outer_sum(features, before_grad)
    grads = (
        grad_emb_class,
        grad_emb_arch,
        grad_emb_topo,
        grad_w_time,
        grad_w_ada,
        grad_w_qkv,
        grad_w_gate,
        grad_w_out,
        grad_w_pair,
        grad_w_ffgate,
        grad_w_ffup,
        grad_w_ffdown,
    )
    return (result, tokens_grad, pairs_grad, grads)


def on_device(
    tokens,
    pair,
    cath_class,
    cath_arch,
    cath_topo,
    times,
    out_grad,
    emb_class,
    emb_arch,
    emb_topo,
    w_time,
    w_ada,
    w_qkv,
    w_gate,
    w_out,
    w_pair,
    w_ffgate,
    w_ffup,
    w_ffdown,
):
    shards = (
        emb_class,
        emb_arch,
        emb_topo,
        w_time,
        w_ada,
        w_qkv,
        w_gate,
        w_out,
        w_pair,
        w_ffgate,
        w_ffup,
        w_ffdown,
    )

    def weights_now():
        return (
            lax.all_gather(emb_class, ("dp", "seq"), axis=1, tiled=True),
            lax.all_gather(emb_arch, ("dp", "seq"), axis=1, tiled=True),
            lax.all_gather(emb_topo, ("dp", "seq"), axis=1, tiled=True),
            lax.all_gather(w_time, ("dp", "seq"), axis=0, tiled=True),
            lax.all_gather(w_ada, ("dp", "seq"), axis=0, tiled=True),
            lax.all_gather(w_qkv, ("dp", "seq"), axis=0, tiled=True),
            lax.all_gather(w_gate, ("dp", "seq"), axis=0, tiled=True),
            lax.all_gather(w_out, ("dp", "seq"), axis=0, tiled=True),
            lax.all_gather(w_pair, ("dp", "seq"), axis=0, tiled=True),
            lax.all_gather(w_ffgate, ("dp", "seq"), axis=0, tiled=True),
            lax.all_gather(w_ffup, ("dp", "seq"), axis=0, tiled=True),
            lax.all_gather(w_ffdown, ("dp", "seq"), axis=0, tiled=True),
        )

    entries = (tokens, pair, cath_class, cath_arch, cath_topo, times, out_grad)

    def advance(totals, entry):
        result, tokens_grad, pairs_grad, grads = chain_step(weights_now(), *entry)
        (
            grad_a,
            grad_b,
            grad_c,
            grad_d,
            grad_e,
            grad_f,
            grad_g,
            grad_h,
            grad_i,
            grad_j,
            grad_k,
            grad_l,
        ) = grads
        shares = (
            lax.psum_scatter(grad_a, ("dp", "seq"), scatter_dimension=1, tiled=True),
            lax.psum_scatter(grad_b, ("dp", "seq"), scatter_dimension=1, tiled=True),
            lax.psum_scatter(grad_c, ("dp", "seq"), scatter_dimension=1, tiled=True),
            lax.psum_scatter(grad_d, ("dp", "seq"), scatter_dimension=0, tiled=True),
            lax.psum_scatter(grad_e, ("dp", "seq"), scatter_dimension=0, tiled=True),
            lax.psum_scatter(grad_f, ("dp", "seq"), scatter_dimension=0, tiled=True),
            lax.psum_scatter(grad_g, ("dp", "seq"), scatter_dimension=0, tiled=True),
            lax.psum_scatter(grad_h, ("dp", "seq"), scatter_dimension=0, tiled=True),
            lax.psum_scatter(grad_i, ("dp", "seq"), scatter_dimension=0, tiled=True),
            lax.psum_scatter(grad_j, ("dp", "seq"), scatter_dimension=0, tiled=True),
            lax.psum_scatter(grad_k, ("dp", "seq"), scatter_dimension=0, tiled=True),
            lax.psum_scatter(grad_l, ("dp", "seq"), scatter_dimension=0, tiled=True),
        )
        return (jax.tree.map(jnp.add, totals, tuple(shares)), (result, tokens_grad, pairs_grad))

    start = tuple((jnp.zeros(shard.shape, jnp.float32) for shard in shards))
    totals, (results, tokens_grads, pairs_grads) = lax.scan(advance, start, entries)
    return (
        results,
        tokens_grads,
        pairs_grads,
        totals[0],
        totals[1],
        totals[2],
        totals[3],
        totals[4],
        totals[5],
        totals[6],
        totals[7],
        totals[8],
        totals[9],
        totals[10],
        totals[11],
    )


def solution(mesh):
    in_specs = (
        P("dp", "seq", None),
        P("dp", "seq", None, None),
        P("dp"),
        P("dp"),
        P("dp"),
        P("dp"),
        P("dp", "seq", None),
        P(None, ("dp", "seq")),
        P(None, ("dp", "seq")),
        P(None, ("dp", "seq")),
        P(("dp", "seq"), None),
        P(("dp", "seq"), None),
        P(("dp", "seq"), None),
        P(("dp", "seq"), None),
        P(("dp", "seq"), None),
        P(("dp", "seq"), None),
        P(("dp", "seq"), None),
        P(("dp", "seq"), None),
        P(("dp", "seq"), None),
    )
    out_specs = (
        P("dp", "seq", None),
        P("dp", "seq", None),
        P("dp", "seq", None, None),
        P(None, ("dp", "seq")),
        P(None, ("dp", "seq")),
        P(None, ("dp", "seq")),
        P(("dp", "seq"), None),
        P(("dp", "seq"), None),
        P(("dp", "seq"), None),
        P(("dp", "seq"), None),
        P(("dp", "seq"), None),
        P(("dp", "seq"), None),
        P(("dp", "seq"), None),
        P(("dp", "seq"), None),
        P(("dp", "seq"), None),
    )
    return jax.shard_map(
        on_device, mesh=mesh, in_specs=in_specs, out_specs=out_specs, check_vma=False
    )
```

profile of v0, /device:TPU:0, one launch (start us, length us, event | category | flops | bytes accessed | tf_op | source)
XLA Modules:
  0.0 3611.1 jit_solution(7783661159276091485)
XLA Ops:
  7.3 3597.0 %while.42 = (s32[]{:T(128)}, f32[5,24]{1,0:T(8,128)}, f32[43,24]{0,1:T(8,128)}, f32[1472,24]{0,1:T(8,128)}, f32[8,768]{1,0:T(8,128)}, /*index=5*/f32[24,4608]{1,...) while((s32[]{:T(128)}, f32[5,24]{1,0:T(8,128)}, ...), condition=%wide.region_31.32_spmd.clone, body=%wide.region_0.31_spmd.clone.sunk | while | flops 8703712256 | bytes 632607104 | solution.py:274
  17.9 70.5 %all-gather.3 = bf16[32,24,5]{1,2,0:T(8,128)(2,1)S(1)} all-gather(bf16[1,24,5]{1,2,0:T(8,128)(2,1)} %bitcast.354), channel_id=1, replica_groups=mesh['dp'=16,'seq'=2] {'dp','seq'}, dimensions={0}, use_global_device_ids=true | all-gather | bytes 7920 | tf_op jit(solution)/shard_map/while/body/eval_jaxpr/all_gather | solution.py:225
  91.1 64.9 %all_gather.121 = bf16[256,12]{1,0:T(8,128)(2,1)S(1)} all-gather(bf16[8,12]{1,0:T(8,128)(2,1)} %get-tuple-element.1181), channel_id=1, replica_groups=mesh['dp'=16,'seq'=2] {'dp','seq'}, dimensions={0}, use_global_device_ids=true | all-gather | bytes 6336 | tf_op jit(solution)/shard_map/while/body/eval_jaxpr/all_gather | solution.py:233
  157.0 67.3 %all_gather.117 = bf16[43,768]{0,1:T(8,128)(2,1)S(1)} all-gather(bf16[43,24]{0,1:T(8,128)(2,1)} %get-tuple-element.1173), channel_id=1, replica_groups=mesh['dp'=16,'seq'=2] {'dp','seq'}, dimensions={1}, use_global_device_ids=true | all-gather | bytes 68112 | tf_op jit(solution)/shard_map/while/body/eval_jaxpr/all_gather | solution.py:226
  226.2 66.0 %all_gather.115 = bf16[256,768]{1,0:T(8,128)(2,1)S(1)} all-gather(bf16[8,768]{1,0:T(8,128)(2,1)S(1)} %copy-done.71), channel_id=1, replica_groups=mesh['dp'=16,'seq'=2] {'dp','seq'}, dimensions={0}, use_global_device_ids=true | all-gather | bytes 405504 | tf_op jit(solution)/shard_map/while/body/eval_jaxpr/all_gather | solution.py:228
  390.9 60.2 %all-gather.23.cloned.1.call-done = bf16[768,3072]{1,0:T(8,128)(2,1)} async-done(((bf16[24,3072]{1,0:T(8,128)(2,1)}), bf16[768,3072]{1,0:T(8,128)(2,1)}) %all-gather.23.cloned.1.call-update) | async-done | bytes 4718608 | tf_op jit(solution)/shard_map/while/body/eval_jaxpr/all_gather | solution.py:234
  455.4 61.1 %all-gather.27.cloned.1.call-done = bf16[768,3072]{1,0:T(8,128)(2,1)} async-done(((bf16[24,3072]{1,0:T(8,128)(2,1)}), bf16[768,3072]{1,0:T(8,128)(2,1)}) %all-gather.27.cloned.1.call-update) | async-done | bytes 4718608 | tf_op jit(solution)/shard_map/while/body/eval_jaxpr/all_gather | solution.py:235
  679.4 91.0 %reduce-scatter.27.cloned.1.call-done = f32[8,768]{1,0:T(8,128)} async-done(((f32[256,768]{1,0:T(8,128)}), f32[8,768]{1,0:T(8,128)}) %reduce-scatter.27.cloned.1.call-update) | async-done | bytes 24592 | tf_op jit(solution)/shard_map/while/body/eval_jaxpr/reduce_scatter | solution.py:261
  771.2 102.5 %reduce-scatter.33.cloned.1.call-done = f32[24,768]{1,0:T(8,128)} async-done(((f32[768,768]{1,0:T(8,128)}), f32[24,768]{1,0:T(8,128)}) %reduce-scatter.33.cloned.1.call-update) | async-done | bytes 73744 | tf_op jit(solution)/shard_map/while/body/eval_jaxpr/reduce_scatter | solution.py:264
  874.6 103.3 %reduce-scatter.35.cloned.1.call-done = f32[24,768]{1,0:T(8,128)} async-done(((f32[768,768]{1,0:T(8,128)}), f32[24,768]{1,0:T(8,128)}) %reduce-scatter.35.cloned.1.call-update) | async-done | bytes 73744 | tf_op jit(solution)/shard_map/while/body/eval_jaxpr/reduce_scatter | solution.py:265
  978.8 110.4 %reduce-scatter.25.cloned.1.call-done = f32[1472,24]{0,1:T(8,128)} async-done(((f32[1472,768]{0,1:T(8,128)}), f32[1472,24]{0,1:T(8,128)}) %reduce-scatter.25.cloned.1.call-update) | async-done | bytes 141328 | tf_op jit(solution)/shard_map/while/body/eval_jaxpr/reduce_scatter | solution.py:260
  1090.2 123.6 %reduce-scatter.31.cloned.1.call-done = f32[24,2304]{1,0:T(8,128)} async-done(((f32[768,2304]{1,0:T(8,128)}), f32[24,2304]{1,0:T(8,128)}) %reduce-scatter.31.cloned.1.call-update) | async-done | bytes 221200 | tf_op jit(solution)/shard_map/while/body/eval_jaxpr/reduce_scatter | solution.py:263
  1215.6 138.9 %reduce-scatter.41.cloned.1.call-done = f32[96,768]{1,0:T(8,128)} async-done(((f32[3072,768]{1,0:T(8,128)}), f32[96,768]{1,0:T(8,128)}) %reduce-scatter.41.cloned.1.call-update) | async-done | bytes 294928 | tf_op jit(solution)/shard_map/while/body/eval_jaxpr/reduce_scatter | solution.py:269
  1355.5 139.3 %reduce-scatter.37.cloned.1.call-done = f32[24,3072]{1,0:T(8,128)} async-done(((f32[768,3072]{1,0:T(8,128)}), f32[24,3072]{1,0:T(8,128)}) %reduce-scatter.37.cloned.1.call-update) | async-done | bytes 294928 | tf_op jit(solution)/shard_map/while/body/eval_jaxpr/reduce_scatter | solution.py:267
  1495.9 140.4 %reduce-scatter.39.cloned.1.call-done = f32[24,3072]{1,0:T(8,128)} async-done(((f32[768,3072]{1,0:T(8,128)}), f32[24,3072]{1,0:T(8,128)}) %reduce-scatter.39.cloned.1.call-update) | async-done | bytes 294928 | tf_op jit(solution)/shard_map/while/body/eval_jaxpr/reduce_scatter | solution.py:268
  1637.3 167.8 %reduce-scatter.29.cloned.1.call-done = f32[24,4608]{1,0:T(8,128)} async-done(((f32[768,4608]{1,0:T(8,128)}), f32[24,4608]{1,0:T(8,128)}) %reduce-scatter.29.cloned.1.call-update) | async-done | bytes 442384 | tf_op jit(solution)/shard_map/while/body/eval_jaxpr/reduce_scatter | solution.py:262
  1817.6 65.8 %all-gather.3 = bf16[32,24,5]{1,2,0:T(8,128)(2,1)S(1)} all-gather(bf16[1,24,5]{1,2,0:T(8,128)(2,1)} %bitcast.354), channel_id=1, replica_groups=mesh['dp'=16,'seq'=2] {'dp','seq'}, dimensions={0}, use_global_device_ids=true | all-gather | bytes 7920 | tf_op jit(solution)/shard_map/while/body/eval_jaxpr/all_gather | solution.py:225
  1886.1 65.6 %all_gather.121 = bf16[256,12]{1,0:T(8,128)(2,1)S(1)} all-gather(bf16[8,12]{1,0:T(8,128)(2,1)} %get-tuple-element.1181), channel_id=1, replica_groups=mesh['dp'=16,'seq'=2] {'dp','seq'}, dimensions={0}, use_global_device_ids=true | all-gather | bytes 6336 | tf_op jit(solution)/shard_map/while/body/eval_jaxpr/all_gather | solution.py:233
  1952.8 66.3 %all_gather.117 = bf16[43,768]{0,1:T(8,128)(2,1)S(1)} all-gather(bf16[43,24]{0,1:T(8,128)(2,1)} %get-tuple-element.1173), channel_id=1, replica_groups=mesh['dp'=16,'seq'=2] {'dp','seq'}, dimensions={1}, use_global_device_ids=true | all-gather | bytes 68112 | tf_op jit(solution)/shard_map/while/body/eval_jaxpr/all_gather | solution.py:226
  2021.0 67.0 %all_gather.115 = bf16[256,768]{1,0:T(8,128)(2,1)S(1)} all-gather(bf16[8,768]{1,0:T(8,128)(2,1)S(1)} %copy-done.71), channel_id=1, replica_groups=mesh['dp'=16,'seq'=2] {'dp','seq'}, dimensions={0}, use_global_device_ids=true | all-gather | bytes 405504 | tf_op jit(solution)/shard_map/while/body/eval_jaxpr/all_gather | solution.py:228
  2133.3 48.5 %all-gather.25.cloned.1.call-done = bf16[3072,768]{1,0:T(8,128)(2,1)} async-done(((bf16[96,768]{1,0:T(8,128)(2,1)}), bf16[3072,768]{1,0:T(8,128)(2,1)}) %all-gather.25.cloned.1.call-update) | async-done | bytes 4718608 | tf_op jit(solution)/shard_map/while/body/eval_jaxpr/all_gather | solution.py:236
  2187.0 60.1 %all-gather.23.cloned.1.call-done = bf16[768,3072]{1,0:T(8,128)(2,1)} async-done(((bf16[24,3072]{1,0:T(8,128)(2,1)}), bf16[768,3072]{1,0:T(8,128)(2,1)}) %all-gather.23.cloned.1.call-update) | async-done | bytes 4718608 | tf_op jit(solution)/shard_map/while/body/eval_jaxpr/all_gather | solution.py:234
  2251.3 61.0 %all-gather.27.cloned.1.call-done = bf16[768,3072]{1,0:T(8,128)(2,1)} async-done(((bf16[24,3072]{1,0:T(8,128)(2,1)}), bf16[768,3072]{1,0:T(8,128)(2,1)}) %all-gather.27.cloned.1.call-update) | async-done | bytes 4718608 | tf_op jit(solution)/shard_map/while/body/eval_jaxpr/all_gather | solution.py:235
  2475.2 90.8 %reduce-scatter.27.cloned.1.call-done = f32[8,768]{1,0:T(8,128)} async-done(((f32[256,768]{1,0:T(8,128)}), f32[8,768]{1,0:T(8,128)}) %reduce-scatter.27.cloned.1.call-update) | async-done | bytes 24592 | tf_op jit(solution)/shard_map/while/body/eval_jaxpr/reduce_scatter | solution.py:261
  2566.8 102.7 %reduce-scatter.33.cloned.1.call-done = f32[24,768]{1,0:T(8,128)} async-done(((f32[768,768]{1,0:T(8,128)}), f32[24,768]{1,0:T(8,128)}) %reduce-scatter.33.cloned.1.call-update) | async-done | bytes 73744 | tf_op jit(solution)/shard_map/while/body/eval_jaxpr/reduce_scatter | solution.py:264
  2670.4 103.3 %reduce-scatter.35.cloned.1.call-done = f32[24,768]{1,0:T(8,128)} async-done(((f32[768,768]{1,0:T(8,128)}), f32[24,768]{1,0:T(8,128)}) %reduce-scatter.35.cloned.1.call-update) | async-done | bytes 73744 | tf_op jit(solution)/shard_map/while/body/eval_jaxpr/reduce_scatter | solution.py:265
  2774.7 110.4 %reduce-scatter.25.cloned.1.call-done = f32[1472,24]{0,1:T(8,128)} async-done(((f32[1472,768]{0,1:T(8,128)}), f32[1472,24]{0,1:T(8,128)}) %reduce-scatter.25.cloned.1.call-update) | async-done | bytes 141328 | tf_op jit(solution)/shard_map/while/body/eval_jaxpr/reduce_scatter | solution.py:260
  2886.1 124.0 %reduce-scatter.31.cloned.1.call-done = f32[24,2304]{1,0:T(8,128)} async-done(((f32[768,2304]{1,0:T(8,128)}), f32[24,2304]{1,0:T(8,128)}) %reduce-scatter.31.cloned.1.call-update) | async-done | bytes 221200 | tf_op jit(solution)/shard_map/while/body/eval_jaxpr/reduce_scatter | solution.py:263
  3011.9 139.0 %reduce-scatter.41.cloned.1.call-done = f32[96,768]{1,0:T(8,128)} async-done(((f32[3072,768]{1,0:T(8,128)}), f32[96,768]{1,0:T(8,128)}) %reduce-scatter.41.cloned.1.call-update) | async-done | bytes 294928 | tf_op jit(solution)/shard_map/while/body/eval_jaxpr/reduce_scatter | solution.py:269
  3151.9 139.3 %reduce-scatter.37.cloned.1.call-done = f32[24,3072]{1,0:T(8,128)} async-done(((f32[768,3072]{1,0:T(8,128)}), f32[24,3072]{1,0:T(8,128)}) %reduce-scatter.37.cloned.1.call-update) | async-done | bytes 294928 | tf_op jit(solution)/shard_map/while/body/eval_jaxpr/reduce_scatter | solution.py:267
  3292.3 140.3 %reduce-scatter.39.cloned.1.call-done = f32[24,3072]{1,0:T(8,128)} async-done(((f32[768,3072]{1,0:T(8,128)}), f32[24,3072]{1,0:T(8,128)}) %reduce-scatter.39.cloned.1.call-update) | async-done | bytes 294928 | tf_op jit(solution)/shard_map/while/body/eval_jaxpr/reduce_scatter | solution.py:268
  3433.7 167.7 %reduce-scatter.29.cloned.1.call-done = f32[24,4608]{1,0:T(8,128)} async-done(((f32[768,4608]{1,0:T(8,128)}), f32[24,4608]{1,0:T(8,128)}) %reduce-scatter.29.cloned.1.call-update) | async-done | bytes 442384 | tf_op jit(solution)/shard_map/while/body/eval_jaxpr/reduce_scatter | solution.py:262
  (666 shorter events, 531.8 us)
Async XLA Ops:
  7.6 296.5 %all-gather.13.cloned.1.call-start = ((), (), s32[]{:S(2)}) async-start(), calls=%async_computation.11 | async-start | bytes 2433024 | tf_op jit(solution)/shard_map/while/body/eval_jaxpr/all_gather | solution.py:227
  8.4 298.7 %all-gather.15.cloned.1.call-start = ((), (), s32[]{:S(2)}) async-start(), calls=%async_computation.12 | async-start | bytes 7299072 | tf_op jit(solution)/shard_map/while/body/eval_jaxpr/all_gather | solution.py:229
  9.1 302.7 %all-gather.17.cloned.1.call-start = ((), (), s32[]{:S(2)}) async-start(), calls=%async_computation.13 | async-start | bytes 3649536 | tf_op jit(solution)/shard_map/while/body/eval_jaxpr/all_gather | solution.py:230
  9.8 322.6 %all-gather.19.cloned.1.call-start = ((), (), s32[]{:S(2)}) async-start(), calls=%async_computation.14 | async-start | bytes 1216512 | tf_op jit(solution)/shard_map/while/body/eval_jaxpr/all_gather | solution.py:231
  10.4 324.6 %all-gather.21.cloned.1.call-start = ((), (), s32[]{:S(2)}) async-start(), calls=%async_computation.15 | async-start | bytes 1216512 | tf_op jit(solution)/shard_map/while/body/eval_jaxpr/all_gather | solution.py:232
  11.0 374.7 %all-gather.25.cloned.1.call-start = ((), (), s32[]{:S(2)}) async-start(), calls=%async_computation.17 | async-start | bytes 4866048 | tf_op jit(solution)/shard_map/while/body/eval_jaxpr/all_gather | solution.py:236
  11.6 439.5 %all-gather.23.cloned.1.call-start = ((), (), s32[]{:S(2)}) async-start(), calls=%async_computation.16 | async-start | bytes 4866048 | tf_op jit(solution)/shard_map/while/body/eval_jaxpr/all_gather | solution.py:234
  12.3 504.2 %all-gather.27.cloned.1.call-start = ((), (), s32[]{:S(2)}) async-start(), calls=%async_computation.18 | async-start | bytes 4866048 | tf_op jit(solution)/shard_map/while/body/eval_jaxpr/all_gather | solution.py:235
  13.1 545.8 %reduce-scatter.21.cloned.1.call-start = ((), (), s32[]{:S(2)}) async-start(), calls=%async_computation.19 | async-start | bytes 1179648 | tf_op jit(solution)/shard_map/while
  576.6 297.1 %reduce-scatter.33.cloned.1.call-start = ((), (), s32[]{:S(2)}) async-start(), calls=%async_computation.25 | async-start | bytes 2433024 | tf_op jit(solution)/shard_map/while/body/eval_jaxpr/reduce_scatter | solution.py:264
  579.6 398.3 %reduce-scatter.35.cloned.1.call-start = ((), (), s32[]{:S(2)}) async-start(), calls=%async_computation.26 | async-start | bytes 2433024 | tf_op jit(solution)/shard_map/while/body/eval_jaxpr/reduce_scatter | solution.py:265
  582.6 506.6 %reduce-scatter.25.cloned.1.call-start = ((), (), s32[]{:S(2)}) async-start(), calls=%async_computation.21 | async-start | bytes 4866048 | tf_op jit(solution)/shard_map/while/body/eval_jaxpr/reduce_scatter | solution.py:260
  586.0 627.9 %reduce-scatter.31.cloned.1.call-start = ((), (), s32[]{:S(2)}) async-start(), calls=%async_computation.24 | async-start | bytes 7299072 | tf_op jit(solution)/shard_map/while/body/eval_jaxpr/reduce_scatter | solution.py:263
  591.0 763.4 %reduce-scatter.41.cloned.1.call-start = ((), (), s32[]{:S(2)}) async-start(), calls=%async_computation.29 | async-start | bytes 9732096 | tf_op jit(solution)/shard_map/while/body/eval_jaxpr/reduce_scatter | solution.py:269
  596.1 898.7 %reduce-scatter.37.cloned.1.call-start = ((), (), s32[]{:S(2)}) async-start(), calls=%async_computation.27 | async-start | bytes 9732096 | tf_op jit(solution)/shard_map/while/body/eval_jaxpr/reduce_scatter | solution.py:267
  602.2 1034.0 %reduce-scatter.39.cloned.1.call-start = ((), (), s32[]{:S(2)}) async-start(), calls=%async_computation.28 | async-start | bytes 9732096 | tf_op jit(solution)/shard_map/while/body/eval_jaxpr/reduce_scatter | solution.py:268
  608.3 1196.8 %reduce-scatter.29.cloned.1.call-start = ((), (), s32[]{:S(2)}) async-start(), calls=%async_computation.23 | async-start | bytes 14598144 | tf_op jit(solution)/shard_map/while/body/eval_jaxpr/reduce_scatter | solution.py:262
  1808.8 298.7 %all-gather.17.cloned.1.call-start = ((), (), s32[]{:S(2)}) async-start(), calls=%async_computation.13 | async-start | bytes 3649536 | tf_op jit(solution)/shard_map/while/body/eval_jaxpr/all_gather | solution.py:230
  1809.6 318.2 %all-gather.19.cloned.1.call-start = ((), (), s32[]{:S(2)}) async-start(), calls=%async_computation.14 | async-start | bytes 1216512 | tf_op jit(solution)/shard_map/while/body/eval_jaxpr/all_gather | solution.py:231
  1810.3 320.1 %all-gather.21.cloned.1.call-start = ((), (), s32[]{:S(2)}) async-start(), calls=%async_computation.15 | async-start | bytes 1216512 | tf_op jit(solution)/shard_map/while/body/eval_jaxpr/all_gather | solution.py:232
  1810.9 370.9 %all-gather.25.cloned.1.call-start = ((), (), s32[]{:S(2)}) async-start(), calls=%async_computation.17 | async-start | bytes 4866048 | tf_op jit(solution)/shard_map/while/body/eval_jaxpr/all_gather | solution.py:236
  1811.6 435.4 %all-gather.23.cloned.1.call-start = ((), (), s32[]{:S(2)}) async-start(), calls=%async_computation.16 | async-start | bytes 4866048 | tf_op jit(solution)/shard_map/while/body/eval_jaxpr/all_gather | solution.py:234
  1812.2 500.1 %all-gather.27.cloned.1.call-start = ((), (), s32[]{:S(2)}) async-start(), calls=%async_computation.18 | async-start | bytes 4866048 | tf_op jit(solution)/shard_map/while/body/eval_jaxpr/all_gather | solution.py:235
  1812.8 541.9 %reduce-scatter.21.cloned.1.call-start = ((), (), s32[]{:S(2)}) async-start(), calls=%async_computation.19 | async-start | bytes 1179648 | tf_op jit(solution)/shard_map/while
  2372.4 297.1 %reduce-scatter.33.cloned.1.call-start = ((), (), s32[]{:S(2)}) async-start(), calls=%async_computation.25 | async-start | bytes 2433024 | tf_op jit(solution)/shard_map/while/body/eval_jaxpr/reduce_scatter | solution.py:264
  2375.4 398.3 %reduce-scatter.35.cloned.1.call-start = ((), (), s32[]{:S(2)}) async-start(), calls=%async_computation.26 | async-start | bytes 2433024 | tf_op jit(solution)/shard_map/while/body/eval_jaxpr/reduce_scatter | solution.py:265
  2378.4 506.6 %reduce-scatter.25.cloned.1.call-start = ((), (), s32[]{:S(2)}) async-start(), calls=%async_computation.21 | async-start | bytes 4866048 | tf_op jit(solution)/shard_map/while/body/eval_jaxpr/reduce_scatter | solution.py:260
  2381.8 628.2 %reduce-scatter.31.cloned.1.call-start = ((), (), s32[]{:S(2)}) async-start(), calls=%async_computation.24 | async-start | bytes 7299072 | tf_op jit(solution)/shard_map/while/body/eval_jaxpr/reduce_scatter | solution.py:263
  2386.9 764.0 %reduce-scatter.41.cloned.1.call-start = ((), (), s32[]{:S(2)}) async-start(), calls=%async_computation.29 | async-start | bytes 9732096 | tf_op jit(solution)/shard_map/while/body/eval_jaxpr/reduce_scatter | solution.py:269
  2392.0 899.3 %reduce-scatter.37.cloned.1.call-start = ((), (), s32[]{:S(2)}) async-start(), calls=%async_computation.27 | async-start | bytes 9732096 | tf_op jit(solution)/shard_map/while/body/eval_jaxpr/reduce_scatter | solution.py:267
  2398.1 1034.6 %reduce-scatter.39.cloned.1.call-start = ((), (), s32[]{:S(2)}) async-start(), calls=%async_computation.28 | async-start | bytes 9732096 | tf_op jit(solution)/shard_map/while/body/eval_jaxpr/reduce_scatter | solution.py:268
  2404.2 1197.2 %reduce-scatter.29.cloned.1.call-start = ((), (), s32[]{:S(2)}) async-start(), calls=%async_computation.23 | async-start | bytes 14598144 | tf_op jit(solution)/shard_map/while/body/eval_jaxpr/reduce_scatter | solution.py:262
  (180 other events, 19432.6 us)
Sparse Core Ops, SparseCore 0:
  11.4 60.1 all-gather.12
  74.5 71.7 all-gather.14
  149.3 58.8 all-gather.16
  323.9 61.7 all-gather.24
  388.6 62.4 all-gather.22
  454.0 62.4 all-gather.26
  575.0 94.8 reduce-scatter.22
  675.8 94.5 reduce-scatter.26
  775.6 98.1 reduce-scatter.32
  879.9 98.0 reduce-scatter.34
  983.3 105.9 reduce-scatter.24
  1095.7 118.0 reduce-scatter.30
  1219.6 134.7 reduce-scatter.40
  1360.2 134.6 reduce-scatter.36
  1501.6 134.6 reduce-scatter.38
  1643.3 161.8 reduce-scatter.28
  1811.0 56.3 all-gather.12
  1870.3 71.7 all-gather.14
  1945.0 58.8 all-gather.16
  2120.0 61.7 all-gather.24
  2184.6 62.4 all-gather.22
  2249.8 62.4 all-gather.26
  2370.8 94.8 reduce-scatter.22
  2471.4 94.5 reduce-scatter.26
  2571.4 98.0 reduce-scatter.32
  2675.6 98.0 reduce-scatter.34
  2779.1 105.9 reduce-scatter.24
  2891.7 118.2 reduce-scatter.30
  3015.9 134.8 reduce-scatter.40
  3156.6 134.6 reduce-scatter.36
  3298.0 134.5 reduce-scatter.38
  3439.7 161.7 reduce-scatter.28
  (6 shorter events, 247.0 us)
where the time goes:
time: 3610 us
  waiting for transfers between devices  2600 us (72%)
  blocking collectives  638 us (18%)
  matrix products  241 us (7%)
  other arithmetic  71.7 us (2%)
    reduce_scatter x2, waiting for transfers between devices, advance(): lax.psum_scatter(grad_e, ('dp', 'seq'), scatter_dimension=0, tiled=True)  336 us
    reduce_scatter x2, waiting for transfers between devices, advance(): lax.psum_scatter(grad_k, ('dp', 'seq'), scatter_dimension=0, tiled=True)  281 us
    reduce_scatter x2, waiting for transfers between devices, advance(): lax.psum_scatter(grad_j, ('dp', 'seq'), scatter_dimension=0, tiled=True)  279 us
    reduce_scatter x2, waiting for transfers between devices, advance(): lax.psum_scatter(grad_l, ('dp', 'seq'), scatter_dimension=0, tiled=True)  278 us
    reduce_scatter x2, waiting for transfers between devices, advance(): lax.psum_scatter(grad_f, ('dp', 'seq'), scatter_dimension=0, tiled=True)  248 us
    reduce_scatter x2, waiting for transfers between devices, advance(): lax.psum_scatter(grad_c, ('dp', 'seq'), scatter_dimension=1, tiled=True)  221 us
    reduce_scatter x2, waiting for transfers between devices, advance(): lax.psum_scatter(grad_h, ('dp', 'seq'), scatter_dimension=0, tiled=True)  207 us
    reduce_scatter x2, waiting for transfers between devices, advance(): lax.psum_scatter(grad_g, ('dp', 'seq'), scatter_dimension=0, tiled=True)  205 us
  transfers between devices with their start and end apart: 38, of which 26 were waited for; matrix products, arithmetic and copies ran while one was open for 7% of the time, Pallas kernels for 0%

commit v1 on v0

v1 whole, which is shorter than its diff:
```python
import math

import jax
import jax.numpy as jnp
from jax import lax
from jax.sharding import Mesh
from jax.sharding import PartitionSpec as P

EPSILON = 1e-06
TIME_SCALE = 100.0
F32 = jnp.float32
BF16 = jnp.bfloat16
DP = ("z", "x", "c")
ALL = ("z", "x", "c", "y")
HIGH = lax.Precision.HIGHEST


def dot(left, right, dims=((1,), (0,))):
    return lax.dot_general(left, right, (dims, ((), ())), preferred_element_type=F32)


def time_features(moment, width):
    half_width = width // 2
    frequency = jnp.exp(-math.log(10000.0) * jnp.arange(half_width, dtype=F32) / half_width)
    angles = TIME_SCALE * moment[:, None] * frequency[None, :]
    return jnp.concatenate([jnp.sin(angles), jnp.cos(angles)], axis=-1)


def normalise(rows):
    centre = rows - jnp.mean(rows, axis=-1, keepdims=True)
    spread = jnp.mean(centre * centre, axis=-1, keepdims=True)
    root = lax.rsqrt(spread + EPSILON)
    return centre * root, root


def normalise_back(grad, scale, normed, root):
    u = grad * (1.0 + scale)
    inner = u - jnp.mean(u, axis=-1, keepdims=True)
    return root * (inner - normed * jnp.mean(u * normed, axis=-1, keepdims=True))


def swap(value, axis):
    return lax.ppermute(value, axis, [(0, 1), (1, 0)])


def shift(value, axis, size, by):
    return lax.ppermute(value, axis, [(i, (i + by) % size) for i in range(size)])


def add_low(left, right):
    return (left.astype(F32) + right.astype(F32)).astype(BF16)


def reduce_scatter(grad, sizes):
    nz, nx, nc, ny = sizes
    rows, columns = grad.shape[1:]
    here = lax.axis_index("c")
    parts = grad.reshape(nz, nx, nc, ny, rows, columns)
    pick = lambda a, i, axis: lax.dynamic_index_in_dim(a, i, axis, keepdims=False)
    parts = add_low(pick(parts, here, 2), swap(pick(parts, 1 - here, 2), "c"))
    half = rows // 2
    done = []
    for which, order in enumerate((("y", "x"), ("x", "y"))):
        block = parts[:, :, :, which * half : (which + 1) * half]
        left = ["z", "x", "y"]
        for axis in order:
            at = left.index(axis)
            here = lax.axis_index(axis)
            block = add_low(pick(block, here, at), swap(pick(block, 1 - here, at), axis))
            left.remove(axis)
        place = lax.axis_index("z")
        total = pick(block, place, 0).astype(F32)
        for by in range(1, nz):
            total = total + shift(pick(block, (place + by) % nz, 0), "z", nz, by).astype(F32)
        done.append(total)
    return jnp.concatenate(done, axis=0)


def on_device(sizes, tokens, pair, cath_class, cath_arch, cath_topo, times, out_grad,
              emb_class, emb_arch, emb_topo, w_time, w_ada, w_qkv, w_gate, w_out, w_pair,
              w_ffgate, w_ffup, w_ffdown):
    nz, nx, nc, ny = sizes
    ndp = nz * nx * nc
    devices = ndp * ny
    chains, local, width = tokens.shape
    length = pair.shape[2]
    heads = w_pair.shape[1]
    head = width // heads
    factor = head ** (-0.5)
    rows = chains * local
    own = emb_class.shape[1]
    hidden_width = w_ffgate.shape[1]
    time_rows = w_time.shape[0]

    attention_w = lax.all_gather(jnp.concatenate([w_qkv, w_gate, w_out], axis=1), ALL, axis=0, tiled=True)
    full_qkv_gate = attention_w[:, : 4 * width]
    full_qkv = attention_w[:, : 3 * width]
    full_gate = attention_w[:, 3 * width : 4 * width]
    full_out = attention_w[:, 4 * width :]
    full_ff = lax.all_gather(jnp.concatenate([w_ffgate, w_ffup], axis=1), ALL, axis=0, tiled=True)
    full_down = lax.all_gather(w_ffdown, ALL, axis=0, tiled=True)

    facts = jnp.stack([cath_class.astype(F32), cath_arch.astype(F32), cath_topo.astype(F32), times]).reshape(1, -1)
    pair_rows_w = w_pair.astype(F32).reshape(1, -1)
    pack = jnp.concatenate(
        [
            w_time.astype(F32).reshape(time_rows, devices, own).transpose(1, 0, 2).reshape(devices, -1),
            jnp.broadcast_to(facts, (devices, facts.shape[1])),
            jnp.broadcast_to(pair_rows_w, (devices, pair_rows_w.shape[1])),
        ],
        axis=1,
    )
    got = lax.all_to_all(pack, ALL, split_axis=0, concat_axis=0, tiled=True)
    size_time = time_rows * own
    time_columns = got[:, :size_time].reshape(devices * time_rows, own).astype(BF16)
    size_facts = 4 * chains
    everyone = got[:, size_time : size_time + size_facts].reshape(ndp, ny, 4, chains)[:, 0]
    everyone = everyone.transpose(1, 0, 2).reshape(4, ndp * chains)
    full_pair_w = got[:, size_time + size_facts :].reshape(-1, heads).astype(BF16)
    labels = everyone[:3].astype(jnp.int32)
    features = time_features(everyone[3], devices * time_rows).astype(BF16)
    hot = [
        (labels[k][:, None] == jnp.arange(table.shape[0], dtype=jnp.int32)[None, :]).astype(BF16)
        for k, table in enumerate((emb_class, emb_arch, emb_topo))
    ]
    before = dot(hot[0], emb_class) + dot(hot[1], emb_arch) + dot(hot[2], emb_topo) + dot(features, time_columns)
    sig_before = jax.nn.sigmoid(before)
    condition_low = (before * sig_before).astype(BF16)
    modes_part = dot(condition_low, w_ada)
    modes = lax.all_to_all(modes_part.reshape(ndp, chains, 6 * width), DP, split_axis=0, concat_axis=0, tiled=True)
    modes = jnp.sum(modes, axis=0)
    modes = modes + swap(modes, "y")
    shift_one, scale_one, gate_one, shift_two, scale_two, gate_two = (
        m[:, None, :] for m in jnp.split(modes, 6, axis=-1)
    )

    entry = tokens.astype(F32)
    norm_one, root_one = normalise(entry)
    normed_one = (norm_one * (1.0 + scale_one) + shift_one).astype(BF16).reshape(rows, width)
    everything = dot(normed_one, full_qkv_gate)
    projected = everything[:, : 3 * width].astype(BF16)
    gate_logits = everything[:, 3 * width :]
    queries = projected[:, :width].reshape(chains, local, heads, head)
    mine = projected[:, width:].reshape(chains, local, 2 * width)
    other = swap(mine, "y")
    place = lax.axis_index("y")
    both = jnp.where(place == 0, jnp.concatenate([mine, other], axis=1), jnp.concatenate([other, mine], axis=1))
    keys = both[:, :, :width].reshape(chains, length, heads, head)
    values = both[:, :, width:].reshape(chains, length, heads, head)
    bias = jnp.einsum("bijc,ch->bhij", pair, full_pair_w, preferred_element_type=F32)
    scores = jnp.einsum("bihd,bjhd->bhij", queries, keys, preferred_element_type=F32) * factor + bias
    probs = jax.nn.softmax(scores, axis=-1)
    probs_low = probs.astype(BF16)
    attended = jnp.einsum("bhij,bjhd->bihd", probs_low, values, preferred_element_type=F32).reshape(rows, width)
    sigmoid_gate = jax.nn.sigmoid(gate_logits)
    gated = (attended * sigmoid_gate).astype(BF16)
    branch_one = dot(gated, full_out).reshape(chains, local, width)
    middle = entry + gate_one * branch_one
    norm_two, root_two = normalise(middle)
    normed_two = (norm_two * (1.0 + scale_two) + shift_two).astype(BF16).reshape(rows, width)
    ff_both = dot(normed_two, full_ff)
    ff_gate, ff_up = ff_both[:, :hidden_width], ff_both[:, hidden_width:]
    sig_ff = jax.nn.sigmoid(ff_gate)
    silu_ff = ff_gate * sig_ff
    hidden = (silu_ff * ff_up).astype(BF16)
    branch_two = dot(hidden, full_down).reshape(chains, local, width)
    result = (middle + gate_two * branch_two).astype(BF16)

    upstream = out_grad.astype(F32)
    branch_two_grad = (gate_two * upstream).astype(BF16).reshape(rows, width)
    gate_two_grad = jnp.sum(upstream * branch_two, axis=1)
    grad_down = dot(hidden, branch_two_grad, ((0,), (0,))).astype(BF16)
    hidden_grad = dot(branch_two_grad, full_down, ((1,), (1,)))
    ff_gate_grad = (hidden_grad * ff_up * (sig_ff + silu_ff * (1.0 - sig_ff))).astype(BF16)
    ff_up_grad = (hidden_grad * silu_ff).astype(BF16)
    ff_grad = jnp.concatenate([ff_gate_grad, ff_up_grad], axis=1)
    grad_ff = dot(normed_two, ff_grad, ((0,), (0,))).astype(BF16)
    normed_two_grad = dot(ff_grad, full_ff, ((1,), (1,))).reshape(chains, local, width)
    shift_two_grad = jnp.sum(normed_two_grad, axis=1)
    scale_two_grad = jnp.sum(normed_two_grad * norm_two, axis=1)
    middle_grad = upstream + normalise_back(normed_two_grad, scale_two, norm_two, root_two)
    gate_one_grad = jnp.sum(middle_grad * branch_one, axis=1)
    branch_one_grad = (gate_one * middle_grad).astype(BF16).reshape(rows, width)
    grad_out = dot(gated, branch_one_grad, ((0,), (0,))).astype(BF16)
    gated_grad = dot(branch_one_grad, full_out, ((1,), (1,)))
    attended_grad = (gated_grad * sigmoid_gate).astype(BF16).reshape(chains, local, heads, head)
    logits_grad = (gated_grad * attended * (sigmoid_gate * (1.0 - sigmoid_gate))).astype(BF16)
    value_grad = jnp.einsum("bhij,bihd->bjhd", probs_low, attended_grad, preferred_element_type=F32)
    probs_grad = jnp.einsum("bihd,bjhd->bhij", attended_grad, values, preferred_element_type=F32)
    scores_grad = (probs * (probs_grad - jnp.sum(probs_grad * probs, axis=-1, keepdims=True))).astype(BF16)
    query_grad = jnp.einsum("bhij,bjhd->bihd", scores_grad, keys, preferred_element_type=F32) * factor
    query_grad = query_grad.reshape(rows, width).astype(BF16)
    key_grad = jnp.einsum("bhij,bihd->bjhd", scores_grad, queries, preferred_element_type=F32) * factor
    joined = jnp.concatenate(
        [key_grad.reshape(chains, length, width), value_grad.reshape(chains, length, width)], axis=2
    ).astype(BF16)
    joined = joined.reshape(chains, ny, local, 2 * width)
    keep = lax.dynamic_index_in_dim(joined, place, 1, keepdims=False)
    give = lax.dynamic_index_in_dim(joined, 1 - place, 1, keepdims=False)
    owned = add_low(keep, swap(give, "y")).reshape(rows, 2 * width)
    everything_grad = jnp.concatenate([query_grad, owned, logits_grad], axis=1)
    pair_grad = jnp.einsum("bhij,ch->bijc", scores_grad, full_pair_w, preferred_element_type=F32).astype(BF16)
    grad_pair_w = jnp.einsum("bijc,bhij->ch", pair, scores_grad, preferred_element_type=F32)
    grad_everything = dot(normed_one, everything_grad, ((0,), (0,))).astype(BF16)
    normed_one_grad = dot(everything_grad, full_qkv_gate, ((1,), (1,))).reshape(chains, local, width)
    shift_one_grad = jnp.sum(normed_one_grad, axis=1)
    scale_one_grad = jnp.sum(normed_one_grad * norm_one, axis=1)
    tokens_grad = (middle_grad + normalise_back(normed_one_grad, scale_one, norm_one, root_one)).astype(BF16)

    sum_down = reduce_scatter(grad_down.reshape(devices, -1, width), sizes)
    sum_ff = reduce_scatter(grad_ff.reshape(devices, -1, 2 * hidden_width), sizes)
    sum_attention = reduce_scatter(
        jnp.concatenate([grad_everything, grad_out], axis=1).reshape(devices, -1, 5 * width), sizes
    )

    modes_grad = jnp.concatenate(
        [shift_one_grad, scale_one_grad, gate_one_grad, shift_two_grad, scale_two_grad, gate_two_grad], axis=-1
    )
    modes_grad = modes_grad + swap(modes_grad, "y")
    modes_all = lax.all_to_all(
        jnp.broadcast_to(modes_grad[None], (ndp, chains, 6 * width)), DP, split_axis=0, concat_axis=0, tiled=True
    ).reshape(ndp * chains, 6 * width)
    grad_ada = lax.dot_general(condition_low.astype(F32), modes_all, (((0,), (0,)), ((), ())), precision=HIGH)
    condition_grad = lax.dot_general(modes_all, w_ada.astype(F32), (((1,), (1,)), ((), ())), precision=HIGH)
    before_grad = condition_grad * (sig_before * (1.0 + before * (1.0 - sig_before)))
    outer = lambda left: lax.dot_general(left.astype(F32), before_grad, (((0,), (0,)), ((), ())), precision=HIGH)
    grad_class, grad_arch, grad_topo = outer(hot[0]), outer(hot[1]), outer(hot[2])
    time_pack = jnp.concatenate(
        [outer(features).reshape(devices, time_rows * own), grad_pair_w.reshape(devices, -1)], axis=1
    )
    time_got = lax.all_to_all(time_pack, ALL, split_axis=0, concat_axis=0, tiled=True)
    grad_time = time_got[:, :size_time].reshape(devices, time_rows, own).transpose(1, 0, 2).reshape(time_rows, width)
    grad_pair_own = jnp.sum(time_got[:, size_time:], axis=0).reshape(w_pair.shape)

    return (
        result,
        tokens_grad,
        pair_grad,
        grad_class,
        grad_arch,
        grad_topo,
        grad_time,
        grad_ada,
        sum_attention[:, : 3 * width],
        sum_attention[:, 3 * width : 4 * width],
        sum_attention[:, 4 * width :],
        grad_pair_own,
        sum_ff[:, :hidden_width],
        sum_ff[:, hidden_width:],
        sum_down,
    )


def solution(mesh):
    ndp, ny = mesh.shape["dp"], mesh.shape["seq"]
    sizes = (ndp // 4, 2, 2, ny)
    fine = Mesh(mesh.devices.reshape(sizes), ALL)
    row, col = P(ALL, None), P(None, ALL)
    in_specs = (P(DP, "y", None), P(DP, "y", None, None), P(DP), P(DP), P(DP), P(DP), P(DP, "y", None)) + (col,) * 3 + (row,) * 9
    out_specs = (P(DP, "y", None), P(DP, "y", None), P(DP, "y", None, None)) + (col,) * 3 + (row,) * 9

    def body(*args):
        return on_device(sizes, *args)

    return jax.shard_map(body, mesh=fine, in_specs=in_specs, out_specs=out_specs, check_vma=False)
```

time: 3610 us -> 538 us (0.15)
  waiting for transfers between devices: 2600 us -> 223 us
  blocking collectives: 638 us -> 0 us
  matrix products: 241 us -> 124 us
  starting transfers between devices: 2.14 us -> 79.9 us
    reduce_scatter x18 -> x0, waiting for transfers between devices: 2230 us -> none  [the longest x2 336 us: advance(): lax.psum_scatter(grad_e, ('dp', 'seq'), scatter_dimension=0, tiled=True)]
    all_gather x10 -> x0, blocking collectives: 553 us -> none  [the longest x2 136 us: weights_now(): lax.all_gather(emb_class, ('dp', 'seq'), axis=1, tiled=True)]
    all_gather x16 -> x3, waiting for transfers between devices: 339 us -> 115 us  [the longest x1 56.8 us: on_device(): full_down = lax.all_gather(w_ffdown, ALL, axis=0, tiled=True)]
    dot_general x66 -> x32, matrix products: 241 us -> 124 us  [the longest x17 47.3 us: dot(): lax.dot_general(left, right, (dims, ((), ())), preferred_element_type=F32)]
    while x2 -> x0, blocking collectives: 85.4 us -> none
    ppermute x0 -> x37, waiting for transfers between devices: none -> 69.5 us  [the longest x19 43.4 us: swap(): return lax.ppermute(value, axis, [(0, 1), (1, 0)])]
    ppermute x0 -> x37, starting transfers between devices: none -> 61.1 us  [the longest x18 38.8 us: shift(): lax.ppermute(value, axis, [(i, (i + by) % size) for i in range(size)])]
    all_to_all x0 -> x4, waiting for transfers between devices: none -> 37.9 us  [the longest x1 22.8 us: on_device(): lax.all_to_all(modes_part.reshape(ndp, chains, 6 * width), DP, split_axis...]
  transfers between devices with their start and end apart: 38 -> 44, of which waited for: 26 -> 26; matrix products, arithmetic and copies ran while one was open for 7% -> 24% of each run, Pallas kernels for 0% -> 0%
where the time goes in v1:
time: 538 us; the launch traced here: 532 us
  waiting for transfers between devices  223 us (41%)
  matrix products  124 us (23%)
  starting transfers between devices  79.9 us (15%)
  local copies, waits for them, and re-layouts  49.6 us (9%)
  other arithmetic  40.4 us (8%)
  between operations  15.3 us (3%)
    all_gather x1, waiting for transfers between devices, on_device(): full_down = lax.all_gather(w_ffdown, ALL, axis=0, tiled=True)  56.8 us
    dot_general x17, matrix products, dot(): lax.dot_general(left, right, (dims, ((), ())), preferred_element_type=F32)  47.3 us
    ppermute x19, waiting for transfers between devices, swap(): return lax.ppermute(value, axis, [(0, 1), (1, 0)])  43.4 us
    ppermute x18, starting transfers between devices, shift(): lax.ppermute(value, axis, [(i, (i + by) % size) for i in range(size)])  38.8 us
    all_gather x1, waiting for transfers between devices, on_device(): lax.all_gather(jnp.concatenate([w_ffgate, w_ffup], axis=1), ALL, axis=0,...  36.8 us
    ppermute x18, waiting for transfers between devices, shift(): lax.ppermute(value, axis, [(i, (i + by) % size) for i in range(size)])  26.2 us
    dynamic_slice x10, local copies, waits for them, and re-layouts, reduce_scatter(): lax.dynamic_index_in_dim(a, i, axis, keepdims=False)  23.4 us
    all_to_all x1, waiting for transfers between devices, on_device(): lax.all_to_all(modes_part.reshape(ndp, chains, 6 * width), DP, split_axis...  22.8 us
  transfers between devices with their start and end apart: 44, of which 26 were waited for; matrix products, arithmetic and copies ran while one was open for 24% of the time, Pallas kernels for 0%

profile of v1, /device:TPU:0, one launch (start us, length us, event | category | flops | bytes accessed | tf_op | source)
XLA Modules:
  0.0 532.5 jit_solution(17990591464851785862)
XLA Ops:
  15.5 7.3 %all-to-all-start = ((f32[32,1,296]{2,1,0:T(1,128)}), f32[32,1,296]{2,1,0:T(1,128)S(1)}, u32[]{:S(2)}, u32[]{:S(2)}) async-start(f32[32,1,296]{2,1,0:T(1,128)} %copy.244), calls=%async_computation | async-start | bytes 98304 | tf_op jit(solution)/shard_map/all_to_all | solution.py:113
  23.5 7.5 %all-to-all-done = f32[32,1,296]{2,1,0:T(1,128)S(1)} async-done(((f32[32,1,296]{2,1,0:T(1,128)}), f32[32,1,296]{2,1,0:T(1,128)S(1)}, u32[]{:S(2)}, u32[]{:S(2)}) %all-to-all-start) | async-done | bytes 37920 | tf_op jit(solution)/shard_map/all_to_all | solution.py:113
  40.1 22.8 %all-to-all-done.1 = f32[16,2,4608]{2,1,0:T(2,128)S(1)} async-done(((f32[16,2,4608]{2,1,0:T(2,128)}), f32[16,2,4608]{2,1,0:T(2,128)S(1)}, u32[]{:S(2)}, u32[]{:S(2)}) %all-to-all-start.1) | async-done | bytes 589856 | tf_op jit(solution)/shard_map/all_to_all | solution.py:130
  67.4 21.5 %all-gather.4.cloned.1.call-done = bf16[768,3840]{1,0:T(8,128)(2,1)} async-done(((bf16[24,3840]{1,0:T(8,128)(2,1)}), bf16[768,3840]{1,0:T(8,128)(2,1)}) %all-gather.4.cloned.1.call-update) | async-done | bytes 5898256 | tf_op jit(solution)/shard_map/all_gather | solution.py:95
  88.9 5.4 %fusion.121 = (bf16[256,3072]{1,0:T(8,128)(2,1)S(1)}, f32[256,3072]{1,0:T(8,128)}) fusion(bf16[256,768]{1,0:T(8,128)(2,1)S(1)} %bitcast.326, bf16[768,3840]{1,0:T(8,128)(2,1)} %all-gather.4.cloned.1.call-done), kind=kOutput, calls=%fused_computation.287 | convolution fusion | flops 1208745984 | bytes 9830400 | tf_op jit(solution)/shard_map/dot_general | solution.py:19
  96.0 16.8 %fusion.91 = f32[12,2,128,256]{3,0,2,1:T(8,128)} fusion(bf16[2,128,256,256]{3,2,1,0:T(8,128)(2,1)} %param.20, bf16[256,12]{1,0:T(8,128)(2,1)S(1)} %convert_element_type.401), kind=kOutput, calls=%fused_computation.214 | convolution fusion | flops 402653184 | bytes 36706304 | tf_op jit(solution)/shard_map/bijc,ch->bhij/dot_general | solution.py:150
  117.6 4.6 bitcast_add_fusion
  125.0 8.4 %convolution_bitcast_fusion = f32[2,128,12,64]{1,3,2,0:T(8,128)S(1)} fusion(bf16[2,256,12,64]{1,3,2,0:T(8,128)(2,1)S(1)} %bitcast.334, f32[2,12,128]{2,1,0:T(8,128)S(1)} %get-tuple-element.81, f32[2,12,128,256]{3,2,1,0:T(8,128)} %copy-done.3), kind=kOutput, calls=%fused_computation.65 | convolution fusion | flops 103025920 | bytes 4730880 | tf_op jit(solution)/shard_map/bhij,bjhd->bihd/dot_general | solution.py:154
  138.3 36.8 %all-gather.6.cloned.1.call-done = bf16[768,6144]{1,0:T(8,128)(2,1)} async-done(((bf16[24,6144]{1,0:T(8,128)(2,1)}), bf16[768,6144]{1,0:T(8,128)(2,1)}) %all-gather.6.cloned.1.call-update) | async-done | bytes 9437200 | tf_op jit(solution)/shard_map/all_gather | solution.py:100
  175.1 8.4 %fusion.123 = f32[256,6144]{1,0:T(8,128)} fusion(bf16[256,768]{1,0:T(8,128)(2,1)S(1)} %bitcast.318, bf16[768,6144]{1,0:T(8,128)(2,1)} %all-gather.6.cloned.1.call-done), kind=kOutput, calls=%fused_computation.289 | convolution fusion | flops 2415919104 | bytes 16121856 | tf_op jit(solution)/shard_map/dot_general | solution.py:19
  183.5 56.8 %all-gather.8.cloned.1.call-done = bf16[3072,768]{1,0:T(8,128)(2,1)} async-done(((bf16[96,768]{1,0:T(8,128)(2,1)}), bf16[3072,768]{1,0:T(8,128)(2,1)}) %all-gather.8.cloned.1.call-update) | async-done | bytes 4718608 | tf_op jit(solution)/shard_map/all_gather | solution.py:101
  240.3 7.2 %multiply_convert_fusion.2 = (bf16[256,3072]{1,0:T(8,128)(2,1)S(1)}, bf16[256,3072]{1,0:T(8,128)(2,1)S(1)}, bf16[256,3072]{1,0:T(8,128)(2,1)S(1)}) fusion(f32[256,6144]{1,0:T(8,128)} %fusion.123, bf16[256,768]{1,0:T(8,128)(2,1)S(1)} %bitcast.328, bf16[3072,768]{1,0:T(8,128)(2,1)} %all-gather.8.cloned.1.call-done), kind=kOutput, calls=%fused_computation.27 | convolution fusion | flops 1218969600 | bytes 16121856 | tf_op jit(solution)/shard_map/dot_general | solution.py:19
  260.2 9.5 %fusion.20 = bf16[2,256,12,64]{1,3,2,0:T(8,128)(2,1)} fusion(bf16[2,128,12,64]{1,0,3,2:T(2,128)(2,1)} %reshape.287, f32[2,12,128]{2,1,0:T(8,128)S(1)} %get-tuple-element.81, f32[2,12,128,256]{3,2,1,0:T(8,128)} %copy-done.3), kind=kOutput, calls=%fused_computation.63 | convolution fusion | flops 103419136 | bytes 4337664 | tf_op jit(solution)/shard_map/bhij,bihd->bjhd/dot_general | solution.py:188
  274.0 13.7 %fusion.25 = f32[256,12]{0,1:T(8,128)S(1)} fusion(bf16[2,128,256,256]{3,2,1,0:T(8,128)(2,1)} %param.20, bf16[2,12,128,256]{3,2,1,0:T(8,128)(2,1)S(1)} %multiply_convert_fusion), kind=kOutput, calls=%fused_computation.79 | convolution fusion | flops 402653184 | bytes 35139584 | tf_op jit(solution)/shard_map/bijc,bhij->ch/dot_general | solution.py:203
  293.0 5.2 convolution_convert_fusion.1
  298.1 14.9 %convolution_convert_fusion = bf16[2,128,256,256]{3,2,1,0:T(8,128)(2,1)} fusion(bf16[2,12,128,256]{3,2,1,0:T(8,128)(2,1)S(1)} %multiply_convert_fusion, bf16[256,12]{1,0:T(8,128)(2,1)S(1)} %convert_element_type.401), kind=kOutput, calls=%fused_computation.1 | convolution fusion | flops 419430400 | bytes 35133440 | tf_op jit(solution)/shard_map/bhij,ch->bijc/dot_general | solution.py:202
  323.4 4.3 constant_dynamic-slice_fusion.1
  329.5 4.8 constant_dynamic-slice_fusion.5
  334.2 5.1 copy.365
  352.3 4.0 all-to-all-start.2
  356.2 4.7 constant_dynamic-slice_fusion.7
  364.2 7.6 %all-to-all-done.2 = f32[16,2,4608]{2,1,0:T(2,128)S(1)} async-done(((f32[16,2,4608]{2,1,0:T(2,128)}), f32[16,2,4608]{2,1,0:T(2,128)S(1)}, u32[]{:S(2)}, u32[]{:S(2)}) %all-to-all-start.2) | async-done | bytes 589856 | tf_op jit(solution)/shard_map/all_to_all | solution.py:220
  373.7 3.8 all-to-all-start.3
  390.4 9.2 %collective-permute-done.32 = bf16[4,2,48,768]{3,2,0,1:T(8,128)(2,1)} collective-permute-done((bf16[4,2,48,768]{3,2,0,1:T(8,128)(2,1)}, bf16[4,2,48,768]{3,2,0,1:T(8,128)(2,1)}, u32[]{:S(2)}, u32[]{:S(2)}) %collective-permute-start.32) | collective-permute-done | bytes 589856 | tf_op jit(solution)/shard_map/ppermute | solution.py:43
  405.4 3.9 collective-permute-done.33
  430.4 10.5 %collective-permute-done.10 = bf16[4,2,12,3840]{3,0,2,1:T(4,128)(2,1)S(1)} collective-permute-done((bf16[4,2,12,3840]{3,0,2,1:T(4,128)(2,1)S(1)}, bf16[4,2,12,3840]{3,0,2,1:T(4,128)(2,1)S(1)}, u32[]{:S(2)}, u32[]{:S(2)}) %collective-permute-start.10) | collective-permute-done | bytes 737312 | tf_op jit(solution)/shard_map/ppermute | solution.py:43
  442.6 4.8 collective-permute-done.5
  474.3 4.1 collective-permute-done.8
  485.1 6.7 %collective-permute-done.22 = bf16[4,12,6144]{2,0,1:T(4,128)(2,1)S(1)} collective-permute-done((bf16[4,12,6144]{2,0,1:T(4,128)(2,1)S(1)}, bf16[4,12,6144]{2,0,1:T(4,128)(2,1)S(1)}, u32[]{:S(2)}, u32[]{:S(2)}) %collective-permute-start.22) | collective-permute-done | bytes 589856 | tf_op jit(solution)/shard_map/ppermute | solution.py:43
  502.1 9.2 %collective-permute-start.19 = (bf16[12,6144]{1,0:T(8,128)(2,1)S(1)}, bf16[12,6144]{1,0:T(8,128)(2,1)S(1)}, u32[]{:S(2)}, u32[]{:S(2)}) collective-permute-start(bf16[12,6144]{1,0:T(8,128)(2,1)S(1)} %get-tuple-element.51), channel_id=1, source_target_pairs={{0,16},{8,24},{16,0},{24,8},{1,17},{9,25},{17,1},{25,9},{2,18},{10... | collective-permute-start | bytes 442376 | tf_op jit(solution)/shard_map/ppermute | solution.py:47
  511.3 7.5 %collective-permute-done.24 = bf16[12,6144]{1,0:T(8,128)(2,1)S(1)} collective-permute-done((bf16[12,6144]{1,0:T(8,128)(2,1)S(1)}, bf16[12,6144]{1,0:T(8,128)(2,1)S(1)}, u32[]{:S(2)}, u32[]{:S(2)}) %collective-permute-start.24) | collective-permute-done | bytes 147488 | tf_op jit(solution)/shard_map/ppermute | solution.py:47
  518.9 5.9 %collective-permute-done.19 = bf16[12,6144]{1,0:T(8,128)(2,1)S(1)} collective-permute-done((bf16[12,6144]{1,0:T(8,128)(2,1)S(1)}, bf16[12,6144]{1,0:T(8,128)(2,1)S(1)}, u32[]{:S(2)}, u32[]{:S(2)}) %collective-permute-start.19) | collective-permute-done | bytes 147488 | tf_op jit(solution)/shard_map/ppermute | solution.py:47
  (376 shorter events, 174.4 us)
Async XLA Ops:
  7.2 81.7 %all-gather.4.cloned.1.call-start = ((), (), s32[]{:S(2)}) async-start(), calls=%async_computation.4 | async-start | bytes 6082560 | tf_op jit(solution)/shard_map/all_gather | solution.py:95
  8.9 166.1 %all-gather.6.cloned.1.call-start = ((), (), s32[]{:S(2)}) async-start(), calls=%async_computation.5 | async-start | bytes 9732096 | tf_op jit(solution)/shard_map/all_gather | solution.py:100
  15.5 15.5 %all-to-all-start = ((f32[32,1,296]{2,1,0:T(1,128)}), f32[32,1,296]{2,1,0:T(1,128)S(1)}, u32[]{:S(2)}, u32[]{:S(2)}) async-start(f32[32,1,296]{2,1,0:T(1,128)} %copy.244), calls=%async_computation | async-start | bytes 98304 | tf_op jit(solution)/shard_map/all_to_all | solution.py:113
  22.8 217.5 %all-gather.8.cloned.1.call-start = ((), (), s32[]{:S(2)}) async-start(), calls=%async_computation.6 | async-start | bytes 4866048 | tf_op jit(solution)/shard_map/all_gather | solution.py:101
  36.1 26.8 %all-to-all-start.1 = ((f32[16,2,4608]{2,1,0:T(2,128)}), f32[16,2,4608]{2,1,0:T(2,128)S(1)}, u32[]{:S(2)}, u32[]{:S(2)}) async-start(f32[16,2,4608]{2,1,0:T(2,128)} %reshape.274), calls=%async_computation.1 | async-start | bytes 1179648 | tf_op jit(solution)/shard_map/all_to_all | solution.py:130
  94.4 21.9 %collective-permute-start.1 = (bf16[2,128,1536]{2,1,0:T(8,128)(2,1)S(1)}, bf16[2,128,1536]{2,1,0:T(8,128)(2,1)S(1)}, u32[]{:S(2)}, u32[]{:S(2)}) collective-permute-start(bf16[2,128,1536]{2,1,0:T(8,128)(2,1)S(1)} %bitcast.322), channel_id=1, source_target_pairs={{0,1},{1,0},{2,3},{3,2},{4,5},{5,4},{6,7},{7,6},{8,9},{9,8},{10,11... | collective-permute-start | bytes 2359304 | tf_op jit(solution)/shard_map/ppermute | solution.py:43
  321.9 20.0 %collective-permute-start.2 = (bf16[2,128,1536]{2,1,0:T(8,128)(2,1)}, bf16[2,128,1536]{2,1,0:T(8,128)(2,1)}, u32[]{:S(2)}, u32[]{:S(2)}) collective-permute-start(bf16[2,128,1536]{2,1,0:T(8,128)(2,1)} %fusion.54), channel_id=1, source_target_pairs={{0,1},{1,0},{2,3},{3,2},{4,5},{5,4},{6,7},{7,6},{8,9},{9,8},{10,11... | collective-permute-start | bytes 2359304 | tf_op jit(solution)/shard_map/ppermute | solution.py:43
  329.4 50.2 %collective-permute-start.26 = (bf16[4,2,2,96,768]{4,3,0,2,1:T(8,128)(2,1)}, bf16[4,2,2,96,768]{4,3,0,2,1:T(8,128)(2,1)}, u32[]{:S(2)}, u32[]{:S(2)}) collective-permute-start(bf16[4,2,2,96,768]{4,3,0,2,1:T(8,128)(2,1)} %bitcast.292), channel_id=1, source_target_pairs={{0,2},{2,0},{1,3},{3,1},{4,6},{6,4},{5,7},{7,5},{8,10},{10,8},{9,1... | collective-permute-start | bytes 7077896 | tf_op jit(solution)/shard_map/ppermute | solution.py:43
  339.4 108.9 %collective-permute-start.15 = (bf16[4,2,2,24,6144]{4,3,0,2,1:T(8,128)(2,1)}, bf16[4,2,2,24,6144]{4,3,0,2,1:T(8,128)(2,1)}, u32[]{:S(2)}, u32[]{:S(2)}) collective-permute-start(bf16[4,2,2,24,6144]{4,3,0,2,1:T(8,128)(2,1)} %bitcast.290), channel_id=1, source_target_pairs={{0,2},{2,0},{1,3},{3,1},{4,6},{6,4},{5,7},{7,5},{8,10},{10,8},{9,1... | collective-permute-start | bytes 14155784 | tf_op jit(solution)/shard_map/ppermute | solution.py:43
  352.3 19.5 %all-to-all-start.2 = ((f32[16,2,4608]{2,1,0:T(2,128)}), f32[16,2,4608]{2,1,0:T(2,128)S(1)}, u32[]{:S(2)}, u32[]{:S(2)}) async-start(f32[16,2,4608]{2,1,0:T(2,128)} %broadcast_in_dim.18), calls=%async_computation.2 | async-start | bytes 1179648 | tf_op jit(solution)/shard_map/all_to_all | solution.py:220
  362.7 59.7 %collective-permute-start.4 = (bf16[4,2,2,24,3840]{4,3,0,2,1:T(8,128)(2,1)}, bf16[4,2,2,24,3840]{4,3,0,2,1:T(8,128)(2,1)}, u32[]{:S(2)}, u32[]{:S(2)}) collective-permute-start(bf16[4,2,2,24,3840]{4,3,0,2,1:T(8,128)(2,1)} %bitcast.291), channel_id=1, source_target_pairs={{0,2},{2,0},{1,3},{3,1},{4,6},{6,4},{5,7},{7,5},{8,10},{10,8},{9,1... | collective-permute-start | bytes 8847368 | tf_op jit(solution)/shard_map/ppermute | solution.py:43
  373.7 15.1 %all-to-all-start.3 = ((f32[32,1,288]{2,1,0:T(1,128)}), f32[32,1,288]{2,1,0:T(1,128)S(1)}, u32[]{:S(2)}, u32[]{:S(2)}) async-start(f32[32,1,288]{2,1,0:T(1,128)} %copy.274), calls=%async_computation.3 | async-start | bytes 98304 | tf_op jit(solution)/shard_map/all_to_all | solution.py:231
  383.8 15.8 %collective-permute-start.32 = (bf16[4,2,48,768]{3,2,0,1:T(8,128)(2,1)}, bf16[4,2,48,768]{3,2,0,1:T(8,128)(2,1)}, u32[]{:S(2)}, u32[]{:S(2)}) collective-permute-start(bf16[4,2,48,768]{3,2,0,1:T(8,128)(2,1)} %dynamic-slice_bitcast_fusion.4), channel_id=1, source_target_pairs={{0,4},{4,0},{1,5},{5,1},{2,6},{6,2},{3,7},{7,3},{8,12},{12,8},{9,1... | collective-permute-start | bytes 1769480 | tf_op jit(solution)/shard_map/ppermute | solution.py:43
  386.4 16.2 %collective-permute-start.27 = (bf16[4,2,48,768]{3,2,0,1:T(8,128)(2,1)S(1)}, bf16[4,2,48,768]{3,2,0,1:T(8,128)(2,1)}, u32[]{:S(2)}, u32[]{:S(2)}) collective-permute-start(bf16[4,2,48,768]{3,2,0,1:T(8,128)(2,1)S(1)} %dynamic-slice_bitcast_fusion.5), channel_id=1, source_target_pairs={{0,1},{1,0},{2,3},{3,2},{4,5},{5,4},{6,7},{7,6},{8,9},{9,8},{10,11... | collective-permute-start | bytes 1769480 | tf_op jit(solution)/shard_map/ppermute | solution.py:43
  403.9 9.4 %collective-permute-start.28 = (bf16[4,48,768]{2,1,0:T(8,128)(2,1)S(1)}, bf16[4,48,768]{2,1,0:T(8,128)(2,1)S(1)}, u32[]{:S(2)}, u32[]{:S(2)}) collective-permute-start(bf16[4,48,768]{2,1,0:T(8,128)(2,1)S(1)} %dynamic-slice_bitcast_fusion.9), channel_id=1, source_target_pairs={{0,4},{4,0},{1,5},{5,1},{2,6},{6,2},{3,7},{7,3},{8,12},{12,8},{9,1... | collective-permute-start | bytes 884744 | tf_op jit(solution)/shard_map/ppermute | solution.py:43
  416.1 11.3 %collective-permute-start.29 = (bf16[48,768]{1,0:T(8,128)(2,1)S(1)}, bf16[48,768]{1,0:T(8,128)(2,1)S(1)}, u32[]{:S(2)}, u32[]{:S(2)}) collective-permute-start(bf16[48,768]{1,0:T(8,128)(2,1)S(1)} %get-tuple-element.62), channel_id=1, source_target_pairs={{0,8},{8,16},{16,24},{24,0},{1,9},{9,17},{17,25},{25,1},{2,10},{10... | collective-permute-start | bytes 221192 | tf_op jit(solution)/shard_map/ppermute | solution.py:47
  416.4 11.1 %collective-permute-start.31 = (bf16[48,768]{1,0:T(8,128)(2,1)S(1)}, bf16[48,768]{1,0:T(8,128)(2,1)S(1)}, u32[]{:S(2)}, u32[]{:S(2)}) collective-permute-start(bf16[48,768]{1,0:T(8,128)(2,1)S(1)} %get-tuple-element.63), channel_id=1, source_target_pairs={{0,24},{8,0},{16,8},{24,16},{1,25},{9,1},{17,9},{25,17},{2,26},{10... | collective-permute-start | bytes 221192 | tf_op jit(solution)/shard_map/ppermute | solution.py:47
  425.9 15.0 %collective-permute-start.10 = (bf16[4,2,12,3840]{3,0,2,1:T(4,128)(2,1)S(1)}, bf16[4,2,12,3840]{3,0,2,1:T(4,128)(2,1)S(1)}, u32[]{:S(2)}, u32[]{:S(2)}) collective-permute-start(bf16[4,2,12,3840]{3,0,2,1:T(4,128)(2,1)S(1)} %copy.283), channel_id=1, source_target_pairs={{0,4},{4,0},{1,5},{5,1},{2,6},{6,2},{3,7},{7,3},{8,12},{12,8},{9,1... | collective-permute-start | bytes 2211848 | tf_op jit(solution)/shard_map/ppermute | solution.py:43
  428.9 18.5 %collective-permute-start.5 = (bf16[4,2,12,3840]{3,0,2,1:T(4,128)(2,1)S(1)}, bf16[4,2,12,3840]{3,0,2,1:T(4,128)(2,1)S(1)}, u32[]{:S(2)}, u32[]{:S(2)}) collective-permute-start(bf16[4,2,12,3840]{3,0,2,1:T(4,128)(2,1)S(1)} %copy.280), channel_id=1, source_target_pairs={{0,1},{1,0},{2,3},{3,2},{4,5},{5,4},{6,7},{7,6},{8,9},{9,8},{10,11... | collective-permute-start | bytes 2211848 | tf_op jit(solution)/shard_map/ppermute | solution.py:43
  441.1 16.9 %collective-permute-start.11 = (bf16[4,12,3840]{2,1,0:T(8,128)(2,1)S(1)}, bf16[4,12,3840]{2,1,0:T(8,128)(2,1)S(1)}, u32[]{:S(2)}, u32[]{:S(2)}) collective-permute-start(bf16[4,12,3840]{2,1,0:T(8,128)(2,1)S(1)} %dynamic-slice_bitcast_fusion.6), channel_id=1, source_target_pairs={{0,1},{1,0},{2,3},{3,2},{4,5},{5,4},{6,7},{7,6},{8,9},{9,8},{10,11... | collective-permute-start | bytes 1105928 | tf_op jit(solution)/shard_map/ppermute | solution.py:43
  447.6 14.4 %collective-permute-start.6 = (bf16[4,12,3840]{2,1,0:T(8,128)(2,1)S(1)}, bf16[4,12,3840]{2,1,0:T(8,128)(2,1)S(1)}, u32[]{:S(2)}, u32[]{:S(2)}) collective-permute-start(bf16[4,12,3840]{2,1,0:T(8,128)(2,1)S(1)} %dynamic-slice_bitcast_fusion.7), channel_id=1, source_target_pairs={{0,4},{4,0},{1,5},{5,1},{2,6},{6,2},{3,7},{7,3},{8,12},{12,8},{9,1... | collective-permute-start | bytes 1105928 | tf_op jit(solution)/shard_map/ppermute | solution.py:43
  453.9 25.9 %collective-permute-start.21 = (bf16[4,2,12,6144]{3,0,2,1:T(4,128)(2,1)S(1)}, bf16[4,2,12,6144]{3,0,2,1:T(4,128)(2,1)S(1)}, u32[]{:S(2)}, u32[]{:S(2)}) collective-permute-start(bf16[4,2,12,6144]{3,0,2,1:T(4,128)(2,1)S(1)} %copy.293), channel_id=1, source_target_pairs={{0,4},{4,0},{1,5},{5,1},{2,6},{6,2},{3,7},{7,3},{8,12},{12,8},{9,1... | collective-permute-start | bytes 3538952 | tf_op jit(solution)/shard_map/ppermute | solution.py:43
  456.4 27.2 %collective-permute-start.16 = (bf16[4,2,12,6144]{3,0,2,1:T(4,128)(2,1)S(1)}, bf16[4,2,12,6144]{3,0,2,1:T(4,128)(2,1)S(1)}, u32[]{:S(2)}, u32[]{:S(2)}) collective-permute-start(bf16[4,2,12,6144]{3,0,2,1:T(4,128)(2,1)S(1)} %copy.288), channel_id=1, source_target_pairs={{0,1},{1,0},{2,3},{3,2},{4,5},{5,4},{6,7},{7,6},{8,9},{9,8},{10,11... | collective-permute-start | bytes 3538952 | tf_op jit(solution)/shard_map/ppermute | solution.py:43
  459.3 9.7 %collective-permute-start.14 = (bf16[12,3840]{1,0:T(8,128)(2,1)S(1)}, bf16[12,3840]{1,0:T(8,128)(2,1)S(1)}, u32[]{:S(2)}, u32[]{:S(2)}) collective-permute-start(bf16[12,3840]{1,0:T(8,128)(2,1)S(1)} %get-tuple-element.56), channel_id=1, source_target_pairs={{0,24},{8,0},{16,8},{24,16},{1,25},{9,1},{17,9},{25,17},{2,26},{10... | collective-permute-start | bytes 276488 | tf_op jit(solution)/shard_map/ppermute | solution.py:47
  481.2 10.6 %collective-permute-start.22 = (bf16[4,12,6144]{2,0,1:T(4,128)(2,1)S(1)}, bf16[4,12,6144]{2,0,1:T(4,128)(2,1)S(1)}, u32[]{:S(2)}, u32[]{:S(2)}) collective-permute-start(bf16[4,12,6144]{2,0,1:T(4,128)(2,1)S(1)} %bitcast.337), channel_id=1, source_target_pairs={{0,1},{1,0},{2,3},{3,2},{4,5},{5,4},{6,7},{7,6},{8,9},{9,8},{10,11... | collective-permute-start | bytes 1769480 | tf_op jit(solution)/shard_map/ppermute | solution.py:43
  484.9 12.2 %collective-permute-start.17 = (bf16[4,12,6144]{2,0,1:T(4,128)(2,1)S(1)}, bf16[4,12,6144]{2,0,1:T(4,128)(2,1)S(1)}, u32[]{:S(2)}, u32[]{:S(2)}) collective-permute-start(bf16[4,12,6144]{2,0,1:T(4,128)(2,1)S(1)} %bitcast.336), channel_id=1, source_target_pairs={{0,4},{4,0},{1,5},{5,1},{2,6},{6,2},{3,7},{7,3},{8,12},{12,8},{9,1... | collective-permute-start | bytes 1769480 | tf_op jit(solution)/shard_map/ppermute | solution.py:43
  492.3 9.8 %collective-permute-start.23 = (bf16[12,6144]{1,0:T(8,128)(2,1)S(1)}, bf16[12,6144]{1,0:T(8,128)(2,1)S(1)}, u32[]{:S(2)}, u32[]{:S(2)}) collective-permute-start(bf16[12,6144]{1,0:T(8,128)(2,1)S(1)} %get-tuple-element.46), channel_id=1, source_target_pairs={{0,8},{8,16},{16,24},{24,0},{1,9},{9,17},{17,25},{25,1},{2,10},{10... | collective-permute-start | bytes 442376 | tf_op jit(solution)/shard_map/ppermute | solution.py:47
  493.1 18.1 %collective-permute-start.25 = (bf16[12,6144]{1,0:T(8,128)(2,1)S(1)}, bf16[12,6144]{1,0:T(8,128)(2,1)S(1)}, u32[]{:S(2)}, u32[]{:S(2)}) collective-permute-start(bf16[12,6144]{1,0:T(8,128)(2,1)S(1)} %get-tuple-element.47), channel_id=1, source_target_pairs={{0,24},{8,0},{16,8},{24,16},{1,25},{9,1},{17,9},{25,17},{2,26},{10... | collective-permute-start | bytes 442376 | tf_op jit(solution)/shard_map/ppermute | solution.py:47
  496.2 22.6 %collective-permute-start.24 = (bf16[12,6144]{1,0:T(8,128)(2,1)S(1)}, bf16[12,6144]{1,0:T(8,128)(2,1)S(1)}, u32[]{:S(2)}, u32[]{:S(2)}) collective-permute-start(bf16[12,6144]{1,0:T(8,128)(2,1)S(1)} %get-tuple-element.48), channel_id=1, source_target_pairs={{0,16},{8,24},{16,0},{24,8},{1,17},{9,25},{17,1},{25,9},{2,18},{10... | collective-permute-start | bytes 442376 | tf_op jit(solution)/shard_map/ppermute | solution.py:47
  497.5 21.4 %collective-permute-start.18 = (bf16[12,6144]{1,0:T(8,128)(2,1)S(1)}, bf16[12,6144]{1,0:T(8,128)(2,1)S(1)}, u32[]{:S(2)}, u32[]{:S(2)}) collective-permute-start(bf16[12,6144]{1,0:T(8,128)(2,1)S(1)} %get-tuple-element.49), channel_id=1, source_target_pairs={{0,8},{8,16},{16,24},{24,0},{1,9},{9,17},{17,25},{25,1},{2,10},{10... | collective-permute-start | bytes 442376 | tf_op jit(solution)/shard_map/ppermute | solution.py:47
  497.9 21.0 %collective-permute-start.20 = (bf16[12,6144]{1,0:T(8,128)(2,1)S(1)}, bf16[12,6144]{1,0:T(8,128)(2,1)S(1)}, u32[]{:S(2)}, u32[]{:S(2)}) collective-permute-start(bf16[12,6144]{1,0:T(8,128)(2,1)S(1)} %get-tuple-element.50), channel_id=1, source_target_pairs={{0,24},{8,0},{16,8},{24,16},{1,25},{9,1},{17,9},{25,17},{2,26},{10... | collective-permute-start | bytes 442376 | tf_op jit(solution)/shard_map/ppermute | solution.py:47
  502.1 22.7 %collective-permute-start.19 = (bf16[12,6144]{1,0:T(8,128)(2,1)S(1)}, bf16[12,6144]{1,0:T(8,128)(2,1)S(1)}, u32[]{:S(2)}, u32[]{:S(2)}) collective-permute-start(bf16[12,6144]{1,0:T(8,128)(2,1)S(1)} %get-tuple-element.51), channel_id=1, source_target_pairs={{0,16},{8,24},{16,0},{24,8},{1,17},{9,25},{17,1},{25,9},{2,18},{10... | collective-permute-start | bytes 442376 | tf_op jit(solution)/shard_map/ppermute | solution.py:47
  (69 other events, 846.6 us)
Sparse Core Ops, SparseCore 0:
  11.5 77.3 all-gather.3
  92.4 82.6 all-gather.5
  178.0 62.2 all-gather.7

commit v2 on v1

v2 whole, which is shorter than its diff:
```python
import functools
import math

import jax
import jax.numpy as jnp
from jax import lax
from jax.experimental import pallas as pl
from jax.experimental.pallas import tpu as pltpu
from jax.sharding import Mesh
from jax.sharding import PartitionSpec as P

EPSILON = 1e-06
TIME_SCALE = 100.0
F32 = jnp.float32
BF16 = jnp.bfloat16
DP = ("z", "x", "c")
ALL = ("z", "x", "c", "y")
HIGH = lax.Precision.HIGHEST
NT, TN = ((1,), (1,)), ((0,), (0,))
TILE = 16
VMEM = 60 * 1024 * 1024


def dot(left, right, dims=((1,), (0,))):
    return lax.dot_general(left, right, (dims, ((), ())), preferred_element_type=F32)


def params():
    return pltpu.CompilerParams(vmem_limit_bytes=VMEM)


def time_features(moment, width):
    half_width = width // 2
    frequency = jnp.exp(-math.log(10000.0) * jnp.arange(half_width, dtype=F32) / half_width)
    angles = TIME_SCALE * moment[:, None] * frequency[None, :]
    return jnp.concatenate([jnp.sin(angles), jnp.cos(angles)], axis=-1)


def normalise(rows):
    centre = rows - jnp.mean(rows, axis=-1, keepdims=True)
    spread = jnp.mean(centre * centre, axis=-1, keepdims=True)
    root = lax.rsqrt(spread + EPSILON)
    return centre * root, root


def normalise_back(grad, scale, normed, root):
    u = grad * (1.0 + scale)
    inner = u - jnp.mean(u, axis=-1, keepdims=True)
    return root * (inner - normed * jnp.mean(u * normed, axis=-1, keepdims=True))


def swap(value, axis):
    return lax.ppermute(value, axis, [(0, 1), (1, 0)])


def shift(value, axis, size, by):
    return lax.ppermute(value, axis, [(i, (i + by) % size) for i in range(size)])


def add_low(left, right):
    return (left.astype(F32) + right.astype(F32)).astype(BF16)


def after(value, *others):
    return lax.optimization_barrier((value, *others))[0]


def ordered(own, other, axis, at):
    low = jnp.stack([own, other], axis=at)
    high = jnp.stack([other, own], axis=at)
    return jnp.where(lax.axis_index(axis) == 0, low, high)


class Gathering:
    def __init__(self, block, nz, routes):
        self.nz, self.routes, self.block = nz, routes, block
        self.got = [shift(block, "z", nz, by) for by in range(1, nz)]

    def first(self):
        nz = self.nz
        parts = [self.block] + self.got
        line = jnp.stack([parts[(nz - 1 - i) % nz] for i in range(2 * nz - 1)])
        full = lax.dynamic_slice_in_dim(line, nz - 1 - lax.axis_index("z"), nz, 0)
        half = full.shape[-1] // 2
        self.full = [full[..., :half], full[..., half:]]
        self.got = [swap(f, r[0]) for f, r in zip(self.full, self.routes)]

    def second(self):
        self.full = [ordered(f, g, r[0], 1) for f, g, r in zip(self.full, self.got, self.routes)]
        self.got = [swap(f, r[1]) for f, r in zip(self.full, self.routes)]

    def third(self):
        self.full = [ordered(f, g, r[1], 2 if r[1] == "y" else 1) for f, g, r in zip(self.full, self.got, self.routes)]
        self.got = [swap(f, "c") for f in self.full]

    def total(self):
        return [ordered(f, g, "c", 2).reshape(-1, f.shape[-1]) for f, g in zip(self.full, self.got)]


def spread(rows, order, nz):
    n = 8 * nz * rows
    new = jnp.arange(n, dtype=jnp.int32)
    part = new // (nz * rows)
    at = {"c": part // 4, order[0]: part // 2 % 2, order[1]: part % 2}
    at = {k: v ^ lax.axis_index(k) for k, v in at.items()}
    old = (((new // rows % nz * 2 + at["x"]) * 2 + at["c"]) * 2 + at["y"]) * rows + new % rows
    return (jnp.arange(n, dtype=jnp.int32)[:, None] == old[None, :]).astype(BF16)


def relative(value, hot):
    return dot(hot, value, ((0,), (1,))).astype(BF16)


class Reduction:
    def __init__(self, keep, send, nz, order):
        self.keep, self.nz, self.order = keep, nz, order
        self.got = swap(send, "c")

    def first(self):
        self.give = add_low(self.keep[2:], self.got[2:])
        self.keep = add_low(self.keep[:2], self.got[:2])
        self.got = swap(self.give, self.order[0])
        return self

    def second(self):
        self.give = add_low(self.keep[1], self.got[1])
        self.keep = add_low(self.keep[0], self.got[0])
        self.got = swap(self.give, self.order[1])
        return self

    def third(self):
        self.give = block = add_low(self.keep, self.got)
        place = lax.axis_index("z")
        pick = lambda i: lax.dynamic_index_in_dim(block, i, 0, keepdims=False)
        self.keep = pick(place)
        self.got = [shift(pick((place + by) % self.nz), "z", self.nz, by) for by in range(1, self.nz)]
        return self

    def total(self):
        total = self.keep.astype(F32)
        for got in self.got:
            total = total + got.astype(F32)
        return total


def bias_kernel(pair_ref, wide_ref, out_ref, table):
    lanes = lax.broadcasted_iota(jnp.int32, wide_ref.shape, 1) % TILE
    channels = wide_ref.shape[0]

    @pl.when((pl.program_id(0) == 0) & (pl.program_id(1) == 0))
    def _():
        wide = wide_ref[...].astype(F32)
        for i in range(TILE):
            table[i * channels : (i + 1) * channels, :] = jnp.where(lanes == i, wide, 0.0).astype(BF16)

    rows = jnp.concatenate([pair_ref[0, i] for i in range(TILE)], axis=1)
    out_ref[0, 0] = dot(rows, table[...]).T


def pair_bias(pair, wide):
    chains, local, length, channels = pair.shape
    blocks, tall = local // TILE, wide.shape[1]
    return pl.pallas_call(
        bias_kernel,
        grid=(chains, blocks),
        in_specs=[
            pl.BlockSpec((1, TILE, length, channels), lambda b, i: (b, i, 0, 0)),
            pl.BlockSpec(wide.shape, lambda b, i: (0, 0)),
        ],
        out_specs=pl.BlockSpec((1, 1, tall, length), lambda b, i: (b, i, 0, 0)),
        out_shape=jax.ShapeDtypeStruct((chains, blocks, tall, length), F32),
        scratch_shapes=[pltpu.VMEM((TILE * channels, tall), BF16)],
        compiler_params=params(),
        cost_estimate=pl.CostEstimate(flops=2 * pair.size * tall, bytes_accessed=2 * pair.size, transcendentals=0),
        name="pair_bias",
    )(pair, wide)


def attend_kernel(factor, bias_ref, q_ref, k_ref, v_ref, mask_ref, probs_ref, out_ref):
    heads = mask_ref.shape[0] // TILE
    keys, values, mask = k_ref[0], v_ref[0], mask_ref[...]
    for n in range(bias_ref.shape[1]):
        at = pl.ds(n * TILE, TILE)
        wide = jnp.concatenate([q_ref[at, :]] * heads, axis=0) * mask
        scores = dot(wide, keys, NT) * factor + bias_ref[0, n]
        powers = jnp.exp(scores - jnp.max(scores, axis=-1, keepdims=True))
        probs = powers * (1.0 / jnp.sum(powers, axis=-1, keepdims=True))
        probs_ref[0, n] = probs
        mixed = dot(probs.astype(BF16), values) * mask.astype(F32)
        total = mixed[:TILE]
        for h in range(1, heads):
            total = total + mixed[h * TILE : (h + 1) * TILE]
        out_ref[at, :] = total


def attend(bias, queries, keys, values, mask, factor, group=4):
    chains, blocks, tall, length = bias.shape
    width = mask.shape[1]
    rows = chains * blocks * TILE
    steps = blocks // group
    row_spec = pl.BlockSpec((group * TILE, width), lambda b, i: (b * steps + i, 0))
    square = pl.BlockSpec((1, group, tall, length), lambda b, i: (b, i, 0, 0))
    return pl.pallas_call(
        functools.partial(attend_kernel, factor),
        grid=(chains, steps),
        in_specs=[
            square,
            row_spec,
            pl.BlockSpec((1, length, width), lambda b, i: (b, 0, 0)),
            pl.BlockSpec((1, length, width), lambda b, i: (b, 0, 0)),
            pl.BlockSpec(mask.shape, lambda b, i: (0, 0)),
        ],
        out_specs=[square, row_spec],
        out_shape=[jax.ShapeDtypeStruct(bias.shape, F32), jax.ShapeDtypeStruct((rows, width), F32)],
        compiler_params=params(),
        cost_estimate=pl.CostEstimate(flops=4 * bias.size * width, bytes_accessed=10 * bias.size, transcendentals=bias.size),
        name="attend",
    )(bias, queries, keys, values, mask)


def attend_back_kernel(factor, probs_ref, q_ref, g_ref, k_ref, v_ref, mask_ref, ds_ref, dq_ref, dk_ref, dv_ref, dk_sum, dv_sum):
    heads = mask_ref.shape[0] // TILE
    keys, values, mask = k_ref[0], v_ref[0], mask_ref[...]

    @pl.when(pl.program_id(1) == 0)
    def _():
        dk_sum[...] = jnp.zeros_like(dk_sum)
        dv_sum[...] = jnp.zeros_like(dv_sum)

    for n in range(probs_ref.shape[1]):
        at = pl.ds(n * TILE, TILE)
        probs = probs_ref[0, n]
        queries = jnp.concatenate([q_ref[at, :]] * heads, axis=0) * mask
        grads = jnp.concatenate([g_ref[at, :]] * heads, axis=0) * mask
        probs_grad = dot(grads, values, NT)
        inner = jnp.sum(probs_grad * probs, axis=-1, keepdims=True)
        scores_grad = (probs * (probs_grad - inner)).astype(BF16)
        ds_ref[0, n] = scores_grad
        mixed = dot(scores_grad, keys) * mask.astype(F32)
        total = mixed[:TILE]
        for h in range(1, heads):
            total = total + mixed[h * TILE : (h + 1) * TILE]
        dq_ref[at, :] = (total * factor).astype(BF16)
        dk_sum[...] += dot(scores_grad, queries, TN)
        dv_sum[...] += dot(probs.astype(BF16), grads, TN)

    @pl.when(pl.program_id(1) == pl.num_programs(1) - 1)
    def _():
        dk_ref[0] = (dk_sum[...] * factor).astype(BF16)
        dv_ref[0] = dv_sum[...].astype(BF16)


def attend_back(probs, queries, grads, keys, values, mask, factor, group=4):
    chains, blocks, tall, length = probs.shape
    width = mask.shape[1]
    rows = chains * blocks * TILE
    steps = blocks // group
    row_spec = pl.BlockSpec((group * TILE, width), lambda b, i: (b * steps + i, 0))
    square = pl.BlockSpec((1, group, tall, length), lambda b, i: (b, i, 0, 0))
    return pl.pallas_call(
        functools.partial(attend_back_kernel, factor),
        grid=(chains, steps),
        in_specs=[
            square,
            row_spec,
            row_spec,
            pl.BlockSpec((1, length, width), lambda b, i: (b, 0, 0)),
            pl.BlockSpec((1, length, width), lambda b, i: (b, 0, 0)),
            pl.BlockSpec(mask.shape, lambda b, i: (0, 0)),
        ],
        out_specs=[square, row_spec] + [pl.BlockSpec((1, length, width), lambda b, i: (b, 0, 0))] * 2,
        out_shape=[
            jax.ShapeDtypeStruct(probs.shape, BF16),
            jax.ShapeDtypeStruct((rows, width), BF16),
            jax.ShapeDtypeStruct((chains, length, width), BF16),
            jax.ShapeDtypeStruct((chains, length, width), BF16),
        ],
        scratch_shapes=[pltpu.VMEM((length, width), F32), pltpu.VMEM((length, width), F32)],
        compiler_params=params(),
        cost_estimate=pl.CostEstimate(flops=10 * probs.size * width, bytes_accessed=6 * probs.size, transcendentals=0),
        name="attend_back",
    )(probs, queries, grads, keys, values, mask)


def pair_back_kernel(ds_ref, pair_ref, tall_ref, turn_ref, old_dw_ref, *rest):
    grad_ref, dw_ref, table = rest[-3:]
    channels = tall_ref.shape[1]

    @pl.when(pl.program_id(0) == 0)
    def _():
        rows = lax.broadcasted_iota(jnp.int32, tall_ref.shape, 0) % TILE
        tall = tall_ref[...].astype(F32)
        for i in range(TILE):
            table[:, i * channels : (i + 1) * channels] = jnp.where(rows == i, tall, 0.0).astype(BF16)
        dw_ref[...] = old_dw_ref[...]

    scores_grad = ds_ref[0, 0]
    turned = scores_grad.T
    by_row = dot(turn_ref[...], scores_grad).astype(BF16)
    span = 4
    total = dw_ref[...]
    for k in range(TILE // span):
        spread = dot(turned, table[:, k * span * channels : (k + 1) * span * channels]).astype(BF16)
        for n in range(span):
            i = k * span + n
            grad_ref[0, i] = spread[:, n * channels : (n + 1) * channels]
            total = total + dot(by_row[i * TILE : (i + 1) * TILE], pair_ref[0, i])
    dw_ref[...] = total


def pair_back(scores_grad, pair, tall, turn, part, parts, old_dw, *old):
    chains, local, length, channels = pair.shape
    blocks, high = scores_grad.shape[1:3]
    count = chains * blocks // parts
    place = lambda i: ((part * count + i) // blocks, (part * count + i) % blocks, 0, 0)
    fixed = lambda i: (0, 0)
    return pl.pallas_call(
        pair_back_kernel,
        grid=(count,),
        in_specs=[
            pl.BlockSpec((1, 1, high, length), place),
            pl.BlockSpec((1, TILE, length, channels), place),
            pl.BlockSpec(tall.shape, fixed),
            pl.BlockSpec(turn.shape, fixed),
            pl.BlockSpec((TILE, channels), fixed),
        ]
        + [pl.BlockSpec(memory_space=pl.ANY)] * len(old),
        out_specs=[
            pl.BlockSpec((1, TILE, length, channels), place),
            pl.BlockSpec((TILE, channels), fixed),
        ],
        out_shape=[jax.ShapeDtypeStruct(pair.shape, BF16), jax.ShapeDtypeStruct((TILE, channels), F32)],
        input_output_aliases={5: 0} if old else {},
        scratch_shapes=[pltpu.VMEM((high, TILE * channels), BF16)],
        compiler_params=params(),
        cost_estimate=pl.CostEstimate(flops=4 * pair.size * high // parts, bytes_accessed=4 * pair.size // parts, transcendentals=0),
        name="pair_back",
    )(scores_grad, pair, tall, turn, old_dw, *old)


def feed_kernel(rows_ref, turned_ref, g_ref, order_ref, line_ref, gate_ref, up_ref, down_ref,
                out_ref, back_ref, keep_down, send_down, keep_gate, send_gate, keep_up, send_up):
    @pl.when(pl.program_id(0) == 0)
    def _():
        out_ref[...] = jnp.zeros_like(out_ref)
        back_ref[...] = jnp.zeros_like(back_ref)

    rows, grads = rows_ref[...], g_ref[...]
    w_gate, w_up = gate_ref[...], up_ref[...]
    width = rows.shape[1]
    stack = [down_ref[:, k * width : (k + 1) * width] for k in range(down_ref.shape[1] // width)]
    w_down = dot(line_ref[...], jnp.concatenate(stack, axis=0)).astype(BF16)
    gate = dot(rows, w_gate)
    up = dot(rows, w_up)
    sig = jax.nn.sigmoid(gate)
    silu = gate * sig
    hidden = (silu * up).astype(BF16)
    out_ref[...] += dot(hidden, w_down)
    hidden_grad = dot(grads, w_down, NT)
    gate_grad = (hidden_grad * up * (sig + silu * (1.0 - sig))).astype(BF16)
    up_grad = (hidden_grad * silu).astype(BF16)
    back_ref[...] += dot(gate_grad, w_gate, NT) + dot(up_grad, w_up, NT)
    half = turned_ref.shape[1] // 2
    for k, (right, keep, send) in enumerate(((gate_grad, keep_gate, send_gate), (up_grad, keep_up, send_up))):
        full = dot(turned_ref[k], right).astype(BF16)
        keep[...] = full[:half]
        send[...] = full[half:]
    hidden_turned = dot(order_ref[...], hidden, NT).astype(BF16)
    full = dot(hidden_turned, grads).reshape((2,) + keep_down.shape)
    keep_down[...] = full[0].astype(BF16)
    send_down[...] = full[1].astype(BF16)


def feed(rows, turned, grads, order, line, weights, nz):
    count, width = rows.shape
    hidden = weights.shape[1] // 3
    block = order.shape[0]
    steps = hidden // block
    per = nz // steps
    own = block // (8 * per)
    fixed = lambda m: (0, 0)
    return pl.pallas_call(
        feed_kernel,
        grid=(steps,),
        in_specs=[
            pl.BlockSpec((count, width), fixed),
            pl.BlockSpec((2, width, count), lambda m: (0, 0, 0)),
            pl.BlockSpec((count, width), fixed),
            pl.BlockSpec((block, block), fixed),
            pl.BlockSpec((block, block), fixed),
            pl.BlockSpec((width, block), lambda m: (0, m)),
            pl.BlockSpec((width, block), lambda m: (0, steps + m)),
            pl.BlockSpec((width // steps, hidden), lambda m: (m, 2)),
        ],
        out_specs=[
            pl.BlockSpec((count, width), fixed),
            pl.BlockSpec((count, width), fixed),
            pl.BlockSpec((4, per, own, width), lambda m: (0, m, 0, 0)),
            pl.BlockSpec((4, per, own, width), lambda m: (0, m, 0, 0)),
            *[pl.BlockSpec((width // 2, block), lambda m: (0, m))] * 4,
        ],
        out_shape=[
            jax.ShapeDtypeStruct((count, width), F32),
            jax.ShapeDtypeStruct((count, width), F32),
            jax.ShapeDtypeStruct((4, nz, own, width), BF16),
            jax.ShapeDtypeStruct((4, nz, own, width), BF16),
            *[jax.ShapeDtypeStruct((width // 2, hidden), BF16)] * 4,
        ],
        compiler_params=params(),
        cost_estimate=pl.CostEstimate(flops=24 * count * width * hidden, bytes_accessed=12 * width * hidden, transcendentals=count * hidden),
        name="feed",
    )(rows, turned, grads, order, line, weights, weights, weights)


def join_kernel(*refs):
    at = 0
    for ref in refs[:-1]:
        pieces = [ref[k] for k in range(ref.shape[0])] if len(ref.shape) == 3 else [ref[...]]
        for piece in pieces:
            refs[-1][:, at : at + piece.shape[1]] = piece
            at += piece.shape[1]


def join(*pieces):
    columns = sum(p.shape[-1] * (p.shape[0] if p.ndim == 3 else 1) for p in pieces)
    return pl.pallas_call(
        join_kernel,
        out_shape=jax.ShapeDtypeStruct((pieces[0].shape[-2], columns), BF16),
        compiler_params=params(),
        name="join",
    )(*pieces)


def project_kernel(own_ref, all_ref, first_ref, second_ref, q_ref, k_ref, v_ref, gate_ref):
    width = own_ref.shape[1]
    own, every = own_ref[...], all_ref[...]
    q_ref[...] = dot(own, first_ref[:, :width]).astype(BF16)
    k_ref[...] = dot(every, first_ref[:, width : 2 * width]).astype(BF16)
    v_ref[...] = dot(every, second_ref[:, :width]).astype(BF16)
    gate_ref[...] = dot(own, second_ref[:, width : 2 * width])


def project(own, every, first, second):
    count, width = own.shape
    many = every.shape[0]
    return pl.pallas_call(
        project_kernel,
        out_shape=[
            jax.ShapeDtypeStruct((count, width), BF16),
            jax.ShapeDtypeStruct((many, width), BF16),
            jax.ShapeDtypeStruct((many, width), BF16),
            jax.ShapeDtypeStruct((count, width), F32),
        ],
        compiler_params=params(),
        cost_estimate=pl.CostEstimate(flops=4 * (count + many) * width * width, bytes_accessed=12 * width * width, transcendentals=0),
        name="project",
    )(own, every, first, second)


def project_back_kernel(own_ref, all_ref, gated_ref, dq_ref, dk_ref, dv_ref, dg_ref, out_ref, *sums):
    width = own_ref.shape[1]
    half = width // 2
    for k, (inner, outer) in enumerate((((own_ref, dq_ref), (all_ref, dk_ref)), ((all_ref, dv_ref), (own_ref, dg_ref)))):
        for n in range(2):
            rows = slice(n * half, (n + 1) * half)
            result = sums[2 * k + n]
            result[:, :width] = dot(inner[0][k, rows], inner[1][...]).astype(BF16)
            result[:, width : 2 * width] = dot(outer[0][k, rows], outer[1][...]).astype(BF16)
            result[:, 2 * width :] = dot(gated_ref[k, rows], out_ref[:, k * half : (k + 1) * half]).astype(BF16)


def project_back(own, every, gated, dq, dk, dv, dg, out):
    width = own.shape[1]
    return pl.pallas_call(
        project_back_kernel,
        out_shape=[jax.ShapeDtypeStruct((width // 2, 5 * width // 2), BF16)] * 4,
        compiler_params=params(),
        cost_estimate=pl.CostEstimate(flops=16 * own.size * width, bytes_accessed=16 * width * width, transcendentals=0),
        name="project_back",
    )(own, every, gated, dq, dk, dv, dg, out)


def on_device(sizes, tokens, pair, cath_class, cath_arch, cath_topo, times, out_grad,
              emb_class, emb_arch, emb_topo, w_time, w_ada, w_qkv, w_gate, w_out, w_pair,
              w_ffgate, w_ffup, w_ffdown):
    nz, nx, nc, ny = sizes
    ndp = nz * nx * nc
    devices = ndp * ny
    chains, local, width = tokens.shape
    length = pair.shape[2]
    heads = w_pair.shape[1]
    head = width // heads
    factor = head ** (-0.5)
    rows = chains * local
    own = emb_class.shape[1]
    hidden_width = w_ffgate.shape[1]
    time_rows = w_time.shape[0]

    half = width // 2
    groups = w_ffdown.shape[0] // own
    routes = (("y", "x"), ("x", "y"))
    stacked = join(w_ffgate, w_ffup, w_ffdown.reshape(groups, own, width))
    weights = lax.all_gather(stacked, ALL, axis=0, tiled=True)
    attention = Gathering(
        join(w_qkv[:, : 2 * width], w_out[:, :half], w_qkv[:, 2 * width :], w_gate, w_out[:, half:]), nz, routes
    )
    tokens_other = swap(tokens, "y")

    facts = jnp.stack([cath_class.astype(F32), cath_arch.astype(F32), cath_topo.astype(F32), times]).reshape(1, -1)
    pair_rows_w = w_pair.astype(F32).reshape(1, -1)
    pack = jnp.concatenate(
        [
            w_time.astype(F32).reshape(time_rows, devices, own).transpose(1, 0, 2).reshape(devices, -1),
            jnp.broadcast_to(facts, (devices, facts.shape[1])),
            jnp.broadcast_to(pair_rows_w, (devices, pair_rows_w.shape[1])),
        ],
        axis=1,
    )
    got = lax.all_to_all(pack, ALL, split_axis=0, concat_axis=0, tiled=True)
    size_time = time_rows * own
    time_columns = got[:, :size_time].reshape(devices * time_rows, own).astype(BF16)
    size_facts = 4 * chains
    everyone = got[:, size_time : size_time + size_facts].reshape(ndp, ny, 4, chains)[:, 0]
    everyone = everyone.transpose(1, 0, 2).reshape(4, ndp * chains)
    full_pair_w = got[:, size_time + size_facts :].reshape(-1, heads).astype(BF16)
    labels = everyone[:3].astype(jnp.int32)
    features = time_features(everyone[3], devices * time_rows).astype(BF16)
    hot = [
        (labels[k][:, None] == jnp.arange(table.shape[0], dtype=jnp.int32)[None, :]).astype(BF16)
        for k, table in enumerate((emb_class, emb_arch, emb_topo))
    ]
    before = dot(hot[0], emb_class) + dot(hot[1], emb_arch) + dot(hot[2], emb_topo) + dot(features, time_columns)
    sig_before = jax.nn.sigmoid(before)
    condition_low = (before * sig_before).astype(BF16)
    modes_part = dot(condition_low, w_ada)
    modes = lax.all_to_all(modes_part.reshape(ndp, chains, 6 * width), DP, split_axis=0, concat_axis=0, tiled=True)
    modes = jnp.sum(modes, axis=0)
    modes = modes + swap(modes, "y")
    shift_one, scale_one, gate_one, shift_two, scale_two, gate_two = (
        m[:, None, :] for m in jnp.split(modes, 6, axis=-1)
    )

    entry = tokens.astype(F32)
    norm_one, root_one = normalise(entry)
    normed_one = (norm_one * (1.0 + scale_one) + shift_one).astype(BF16)
    norm_other, _ = normalise(tokens_other.astype(F32))
    normed_other = (norm_other * (1.0 + scale_one) + shift_one).astype(BF16)
    normed_all = ordered(normed_one, normed_other, "y", 1).reshape(chains * length, width)
    normed_one = normed_one.reshape(rows, width)
    mask = (jnp.arange(heads * TILE)[:, None] // TILE == jnp.arange(width)[None, :] // head).astype(BF16)
    wide_pair = jnp.repeat(full_pair_w, TILE, axis=1)
    attention.first()
    bias = pair_bias(after(pair, *attention.full), wide_pair)
    attention.got[0] = after(attention.got[0], bias)
    attention.second()
    hots = [spread(own, route, nz) for route in routes]
    order = spread(groups * own, routes[1], nz * width // hidden_width).T
    in_turned = jnp.stack([relative(normed_one, hot) for hot in hots])
    all_turned = jnp.stack([relative(normed_all, hot) for hot in hots])
    attention.third()
    first_w, second_w = attention.total()
    full_out = jnp.concatenate([first_w[:, 2 * width :], second_w[:, 2 * width :]], axis=1)
    queries, keys, values, gate_logits = project(normed_one, normed_all, first_w, second_w)
    keys, values = keys.reshape(chains, length, width), values.reshape(chains, length, width)
    sigmoid_gate = jax.nn.sigmoid(gate_logits)
    probs, attended = attend(bias, queries, keys, values, mask, factor)
    gated = (attended * sigmoid_gate).astype(BF16)
    branch_one = dot(gated, full_out).reshape(chains, local, width)
    middle = entry + gate_one * branch_one
    norm_two, root_two = normalise(middle)
    normed_two = (norm_two * (1.0 + scale_two) + shift_two).astype(BF16).reshape(rows, width)
    upstream = out_grad.astype(F32)
    branch_two_grad = (gate_two * upstream).astype(BF16).reshape(rows, width)
    out_turned = jnp.stack([relative(gated, hot) for hot in hots])
    turned = jnp.stack([relative(normed_two, hots[k]) for k in (1, 0)])
    steps = hidden_width // width
    new = jnp.arange(width, dtype=jnp.int32)
    per_step = width // (steps * own)
    old = (new // own % groups) * (per_step * own) + new // (groups * own) * own + new % own
    line = (jnp.arange(width, dtype=jnp.int32)[None, :] == old[:, None]).astype(BF16)
    weights = after(weights, out_turned, turned)
    branch_two, normed_two_grad, *grads = feed(normed_two, turned, branch_two_grad, order, line, weights, nz)
    split = lambda v: v.reshape(4, nz, -1, v.shape[-1])
    down_sum = Reduction(grads[0], grads[1], nz, routes[1])
    gate_sum = Reduction(split(grads[2]), split(grads[3]), nz, routes[1])
    up_sum = Reduction(split(grads[4]), split(grads[5]), nz, routes[0])

    normed_two_grad = normed_two_grad.reshape(chains, local, width)
    middle_grad = upstream + normalise_back(normed_two_grad, scale_two, norm_two, root_two)
    branch_one_grad = (gate_one * middle_grad).astype(BF16).reshape(rows, width)
    gated_grad = dot(branch_one_grad, full_out, NT)
    attended_grad = (gated_grad * sigmoid_gate).astype(BF16)
    logits_grad = (gated_grad * attended * (sigmoid_gate * (1.0 - sigmoid_gate))).astype(BF16)
    up_sum.first(), down_sum.first(), gate_sum.first()
    attended_grad = after(attended_grad, down_sum.give, gate_sum.give, up_sum.give)
    scores_grad, query_grad, key_grad, value_grad = attend_back(
        probs, queries, attended_grad, keys, values, mask, factor
    )
    kept_sent = project_back(
        in_turned, all_turned, out_turned, query_grad, key_grad.reshape(-1, width), value_grad.reshape(-1, width),
        logits_grad, branch_one_grad,
    )
    in_sums = [Reduction(split(kept_sent[2 * k]), split(kept_sent[2 * k + 1]), nz, routes[k]) for k in range(2)]
    place = lax.axis_index("y")
    joined = jnp.stack([key_grad, value_grad]).reshape(2, chains, ny, local, width)
    keep = lax.dynamic_index_in_dim(joined, place, 2, keepdims=False)
    give = lax.dynamic_index_in_dim(joined, 1 - place, 2, keepdims=False)
    got = swap(give, "y")
    turn_rows = jnp.arange(TILE * TILE)[:, None]
    turn_columns = jnp.arange(heads * TILE)[None, :]
    turn = ((turn_rows // TILE == turn_columns % TILE) & (turn_rows % TILE == turn_columns // TILE)).astype(BF16)
    tall_pair = wide_pair.T
    pair_sums = (jnp.zeros((TILE, pair.shape[3]), F32),)
    pieces = 4

    def more_pair(k, *needed):
        new_grad, new_sum = pair_back(after(scores_grad, *needed), pair, tall_pair, turn, k, pieces, *pair_sums)
        return (new_sum, new_grad)

    pair_sums = more_pair(0, kept_sent[0])
    up_sum.got = after(up_sum.got, pair_sums[0])
    down_sum.got = after(down_sum.got, pair_sums[0])
    up_sum.second(), down_sum.second()
    for s in in_sums:
        s.got = after(s.got, pair_sums[0])
        s.first()
    pair_sums = more_pair(1, up_sum.give, down_sum.give, *[s.give for s in in_sums])
    owned = add_low(keep, after(got, pair_sums[0])).reshape(2, rows, width)
    gate_sum.got = after(gate_sum.got, pair_sums[0])
    gate_sum.second()
    normed_one_grad = (
        dot(query_grad, first_w[:, :width], NT)
        + dot(owned[0], first_w[:, width : 2 * width], NT)
        + dot(owned[1], second_w[:, :width], NT)
        + dot(logits_grad, second_w[:, width : 2 * width], NT)
    ).reshape(chains, local, width)
    pair_sums = more_pair(2, normed_one_grad, gate_sum.give)
    up_sum.got = after(up_sum.got, pair_sums[0])
    down_sum.got = after(down_sum.got, pair_sums[0])
    up_sum.third(), down_sum.third()
    pair_sums = more_pair(3, up_sum.give, down_sum.give)
    for s in in_sums:
        s.got = after(s.got, pair_sums[0])
        s.second()
    gate_sum.got = after(gate_sum.got, pair_sums[0])
    gate_sum.third()
    for s in in_sums:
        s.third()
    pair_w_sum, pair_grad = pair_sums
    sum_down, sum_gate, sum_up = down_sum.total(), gate_sum.total(), up_sum.total()
    sums = [s.total() for s in in_sums]
    sum_out = jnp.concatenate([s[:, 2 * width :] for s in sums], axis=1)
    grad_pair_w = pair_w_sum[:heads].T

    branch_two = branch_two.reshape(chains, local, width)
    result = (middle + gate_two * branch_two).astype(BF16)
    gate_two_grad = jnp.sum(upstream * branch_two, axis=1)
    shift_two_grad = jnp.sum(normed_two_grad, axis=1)
    scale_two_grad = jnp.sum(normed_two_grad * norm_two, axis=1)
    gate_one_grad = jnp.sum(middle_grad * branch_one, axis=1)
    shift_one_grad = jnp.sum(normed_one_grad, axis=1)
    scale_one_grad = jnp.sum(normed_one_grad * norm_one, axis=1)
    tokens_grad = (middle_grad + normalise_back(normed_one_grad, scale_one, norm_one, root_one)).astype(BF16)

    modes_grad = jnp.concatenate(
        [shift_one_grad, scale_one_grad, gate_one_grad, shift_two_grad, scale_two_grad, gate_two_grad], axis=-1
    )
    modes_grad = modes_grad + swap(modes_grad, "y")
    modes_all = lax.all_to_all(
        jnp.broadcast_to(modes_grad[None], (ndp, chains, 6 * width)), DP, split_axis=0, concat_axis=0, tiled=True
    ).reshape(ndp * chains, 6 * width)
    grad_ada = lax.dot_general(condition_low.astype(F32), modes_all, (((0,), (0,)), ((), ())), precision=HIGH)
    condition_grad = lax.dot_general(modes_all, w_ada.astype(F32), (((1,), (1,)), ((), ())), precision=HIGH)
    before_grad = condition_grad * (sig_before * (1.0 + before * (1.0 - sig_before)))
    outer = lambda left: lax.dot_general(left.astype(F32), before_grad, (((0,), (0,)), ((), ())), precision=HIGH)
    grad_class, grad_arch, grad_topo = outer(hot[0]), outer(hot[1]), outer(hot[2])
    time_pack = jnp.concatenate(
        [outer(features).reshape(devices, time_rows * own), grad_pair_w.reshape(devices, -1)], axis=1
    )
    time_got = lax.all_to_all(time_pack, ALL, split_axis=0, concat_axis=0, tiled=True)
    grad_time = time_got[:, :size_time].reshape(devices, time_rows, own).transpose(1, 0, 2).reshape(time_rows, width)
    grad_pair_own = jnp.sum(time_got[:, size_time:], axis=0).reshape(w_pair.shape)

    return (
        result,
        tokens_grad,
        pair_grad,
        grad_class,
        grad_arch,
        grad_topo,
        grad_time,
        grad_ada,
        jnp.concatenate([sums[0][:, : 2 * width], sums[1][:, :width]], axis=1),
        sums[1][:, width : 2 * width],
        sum_out,
        grad_pair_own,
        sum_gate,
        sum_up,
        sum_down,
    )


def solution(mesh):
    ndp, ny = mesh.shape["dp"], mesh.shape["seq"]
    sizes = (ndp // 4, 2, 2, ny)
    fine = Mesh(mesh.devices.reshape(sizes), ALL)
    row, col = P(ALL, None), P(None, ALL)
    in_specs = (P(DP, "y", None), P(DP, "y", None, None), P(DP), P(DP), P(DP), P(DP), P(DP, "y", None)) + (col,) * 3 + (row,) * 9
    out_specs = (P(DP, "y", None), P(DP, "y", None), P(DP, "y", None, None)) + (col,) * 3 + (row,) * 9

    def body(*args):
        return on_device(sizes, *args)

    return jax.shard_map(body, mesh=fine, in_specs=in_specs, out_specs=out_specs, check_vma=False)
```

time: 538 us -> 413 us (0.77)
  waiting for transfers between devices: 223 us -> 80 us
  Pallas kernels: 0 us -> 128 us
  matrix products: 124 us -> 16.4 us
  local copies, waits for them, and re-layouts: 49.6 us -> 29.4 us
  other arithmetic: 40.4 us -> 59.9 us
    pallas_call x0 -> x12, Pallas kernels: none -> 128 us  [the longest x4 37.7 us: pair_back(): pl.pallas_call(pair_back_kernel, grid=(count,), in_specs=[pl.BlockSpec((1...]
    all_gather x3 -> x1, waiting for transfers between devices: 115 us -> 0.01 us  [on_device(): weights = lax.all_gather(stacked, ALL, axis=0, tiled=True)]
    dot_general x9 -> x0, matrix products: 72.4 us -> none  [the longest x1 16.8 us: on_device(): jnp.einsum('bijc,ch->bhij', pair, full_pair_w, preferred_element_type=F32)]
    dot_general x17 -> x19, matrix products: 47.3 us -> 12 us  [dot(): lax.dot_general(left, right, (dims, ((), ())), preferred_element_type=F32)]
    dynamic_slice x10 -> x0, local copies, waits for them, and re-layouts: 23.4 us -> none  [reduce_scatter(): lax.dynamic_index_in_dim(a, i, axis, keepdims=False)]
    all_to_all x1, waiting for transfers between devices: 22.8 us -> 0.01 us  [on_device(): lax.all_to_all(modes_part.reshape(ndp, chains, 6 * width), DP, split_axis...]
    convert_element_type x16, other arithmetic: 16.2 us -> 27.7 us  [add_low(): return (left.astype(F32) + right.astype(F32)).astype(BF16)]
    unnamed x124 -> x152, local copies, waits for them, and re-layouts: 0.98 us -> 12.4 us
  transfers between devices with their start and end apart: 44 -> 48, of which waited for: 26 -> 12; matrix products, arithmetic and copies ran while one was open for 24% -> 23% of each run, Pallas kernels for 0% -> 25%
where the time goes in v2:
time: 413 us; the launch traced here: 407 us
  Pallas kernels  128 us (31%)
  waiting for transfers between devices  80 us (19%)
  starting transfers between devices  77.2 us (19%)
  other arithmetic  59.9 us (15%)
  local copies, waits for them, and re-layouts  29.4 us (7%)
  matrix products  16.4 us (4%)
  between operations  15.6 us (4%)
    ppermute x25, waiting for transfers between devices, swap(): return lax.ppermute(value, axis, [(0, 1), (1, 0)])  45.8 us
    pallas_call x4, Pallas kernels, pair_back(): pl.pallas_call(pair_back_kernel, grid=(count,), in_specs=[pl.BlockSpec((1...  37.7 us
    ppermute x18, starting transfers between devices, shift(): lax.ppermute(value, axis, [(i, (i + by) % size) for i in range(size)])  35 us
    convert_element_type x16, other arithmetic, add_low(): return (left.astype(F32) + right.astype(F32)).astype(BF16)  27.7 us
    pallas_call x1, Pallas kernels, feed(): pl.pallas_call(feed_kernel, grid=(steps,), in_specs=[pl.BlockSpec((count,...  25.4 us
    pallas_call x1, Pallas kernels, pair_bias(): pl.pallas_call(bias_kernel, grid=(chains, blocks), in_specs=[pl.BlockSpec...  22.3 us
    ppermute x18, waiting for transfers between devices, shift(): lax.ppermute(value, axis, [(i, (i + by) % size) for i in range(size)])  20.7 us
    ppermute x25, starting transfers between devices, swap(): return lax.ppermute(value, axis, [(0, 1), (1, 0)])  20.5 us
  transfers between devices with their start and end apart: 48, of which 12 were waited for; matrix products, arithmetic and copies ran while one was open for 23% of the time, Pallas kernels for 25%

profile of v2, /device:TPU:0, one launch (start us, length us, event | category | flops | bytes accessed | tf_op | source)
XLA Modules:
  0.0 406.7 jit_solution(1105611284559719845)
XLA Ops:
  14.4 5.0 %collective-permute-start.1 = (bf16[24,3840]{1,0:T(8,128)(2,1)}, bf16[24,3840]{1,0:T(8,128)(2,1)S(1)}, u32[]{:S(2)}, u32[]{:S(2)}) collective-permute-start(bf16[24,3840]{1,0:T(8,128)(2,1)} %join.2), channel_id=1, source_target_pairs={{0,24},{8,0},{16,8},{24,16},{1,25},{9,1},{17,9},{25,17},{2,26},{10... | collective-permute-start | bytes 552968 | tf_op jit(solution)/shard_map/ppermute | solution.py:57
  21.9 5.1 %all-to-all-start = ((f32[32,1,296]{2,1,0:T(1,128)}), f32[32,1,296]{2,1,0:T(1,128)S(1)}, u32[]{:S(2)}, u32[]{:S(2)}) async-start(f32[32,1,296]{2,1,0:T(1,128)} %copy.90), calls=%async_computation | async-start | bytes 98304 | tf_op jit(solution)/shard_map/all_to_all | solution.py:519
  32.8 13.5 %all-to-all-done = f32[32,1,296]{2,1,0:T(1,128)S(1)} async-done(((f32[32,1,296]{2,1,0:T(1,128)}), f32[32,1,296]{2,1,0:T(1,128)S(1)}, u32[]{:S(2)}, u32[]{:S(2)}) %all-to-all-start) | async-done | bytes 37920 | tf_op jit(solution)/shard_map/all_to_all | solution.py:519
  51.2 6.5 %all-to-all-start.1 = ((f32[16,2,4608]{2,1,0:T(2,128)}), f32[16,2,4608]{2,1,0:T(2,128)S(1)}, u32[]{:S(2)}, u32[]{:S(2)}) async-start(f32[16,2,4608]{2,1,0:T(2,128)} %reshape.1040), calls=%async_computation.1 | async-start | bytes 1179648 | tf_op jit(solution)/shard_map/all_to_all | solution.py:536
  60.8 22.3 %pair_bias.1.bias_ref = f32[2,8,192,256]{3,2,1,0:T(8,128)} custom-call(bf16[2,128,256,256]{3,2,1,0:T(8,128)(2,1)} %pair_ref.8, bf16[256,192]{1,0:T(8,128)(2,1)} %copy.99.wide_ref), custom_call_target="tpu_custom_call" | custom-call | flops 6442450944 | bytes 33554432 | tf_op jit(solution)/shard_map/pair_bias/pallas_call | solution.py:163
  91.1 22.7 %collective-permute-done = f32[2,4608]{1,0:T(2,128)S(1)} collective-permute-done((f32[2,4608]{1,0:T(2,128)S(1)}, f32[2,4608]{1,0:T(2,128)S(1)}, u32[]{:S(2)}, u32[]{:S(2)}) %collective-permute-start) | collective-permute-done | bytes 36896 | tf_op jit(solution)/shard_map/ppermute | solution.py:53
  120.5 3.7 collective-permute-done.6
  130.8 6.3 %project.1 = (bf16[256,768]{1,0:T(8,128)(2,1)}, bf16[512,768]{1,0:T(8,128)(2,1)}, bf16[512,768]{1,0:T(8,128)(2,1)}, f32[256,768]{1,0:T(8,128)}) custom-call(bf16[256,768]{1,0:T(8,128)(2,1)} %bitcast.299, bf16[512,768]{1,0:T(8,128)(2,1)} %bitcast.308, bf16[768,1920]{1,0:T(8,128)(2,1)} %bitcast.276, bf16[768,1920]{1,0:T(8,128)(2,1)} %bitcast.272), custom_call_target="tpu_custom_call" | custom-call | flops 1811939328 | bytes 7077888 | tf_op jit(solution)/shard_map/project/pallas_call | solution.py:446
  137.0 11.5 %attend.1 = (f32[2,8,192,256]{3,2,1,0:T(8,128)}, f32[256,768]{1,0:T(8,128)}) custom-call(f32[2,8,192,256]{3,2,1,0:T(8,128)} %pair_bias.1.bias_ref, bf16[256,768]{1,0:T(8,128)(2,1)} %get-tuple-element.66.q_ref, bf16[2,256,768]{2,1,0:T(8,128)(2,1)} %bitcast.351, bf16[2,256,768]{2,1,0:T(8,128)(2,1)} %bitcast.353, bf16[192,768]{1,0:T(8,128)(2,1)} %compare_convert_fusion.mask_ref), custom_call_target="tpu_custom_call" | custom-call | flops 2415919104 | bytes 7864320 | tf_op jit(solution)/shard_map/attend/pallas_call | solution.py:203
  155.7 25.4 %feed.1 = (f32[256,768]{1,0:T(8,128)}, f32[256,768]{1,0:T(8,128)}, bf16[4,4,96,768]{3,2,1,0:T(8,128)(2,1)}, bf16[4,4,96,768]{3,2,1,0:T(8,128)(2,1)}, bf16[384,30...) custom-call(bf16[256,768]{1,0:T(8,128)(2,1)} %bitcast.335, ...), custom_call_target="tpu_custom_call" | custom-call | flops 14495514624 | bytes 28311552 | tf_op jit(solution)/shard_map/feed/pallas_call | solution.py:382
  198.8 2.4 fusion
  203.0 15.3 %attend_back.1 = (bf16[2,8,192,256]{3,2,1,0:T(8,128)(2,1)}, bf16[256,768]{1,0:T(8,128)(2,1)}, bf16[2,256,768]{2,1,0:T(8,128)(2,1)}, bf16[2,256,768]{2,1,0:T(8,128)(2,1)}) custom-call(f32[2,8,192,256]{3,2,1,0:T(8,128)} %get-tuple-element.74.probs_ref, bf16[256,768]{1,0:T(8,128)(2,1)} %get-tuple-element.66.q_ref, bf16[256,768]{1,0:T(8,128)(2,1)} %get-tuple-element.81.g_ref, ...), custom_call_target="tpu_custom_call" | custom-call | flops 6039797760 | bytes 4718592 | tf_op jit(solution)/shard_map/attend_back/pallas_call | solution.py:260
  218.3 6.2 %project_back.1 = (bf16[384,1920]{1,0:T(8,128)(2,1)}, bf16[384,1920]{1,0:T(8,128)(2,1)}, bf16[384,1920]{1,0:T(8,128)(2,1)}, bf16[384,1920]{1,0:T(8,128)(2,1)}) custom-call(bf16[2,768,256]{2,1,0:T(8,128)(2,1)} %pad_maximum_fusion.6.own_ref, bf16[2,768,512]{2,1,0:T(8,128)(2,1)} %pad_maximum_fusion.all_ref, bf16[2,768,256]{2,1,0:T(8,128)(2,1)} %pad_maximum_fusion.5.gated_ref, ...), custom_call_target="tpu_custom_call" | custom-call | flops 4831838208 | bytes 9437184 | tf_op jit(solution)/shard_map/project_back/pallas_call | solution.py:474
  225.6 9.6 %pair_back.4 = (bf16[2,128,256,256]{3,2,1,0:T(8,128)(2,1)}, f32[16,256]{1,0:T(8,128)}) custom-call(bf16[2,8,192,256]{3,2,1,0:T(8,128)(2,1)} %get-tuple-element.106.ds_ref, bf16[2,128,256,256]{3,2,1,0:T(8,128)(2,1)} %pair_ref.8, bf16[192,256]{1,0:T(8,128)(2,1)} %bitcast.292, bf16[256,192]{1,0:T(8,128)(2,1)} %and_convert_fusion.turn_ref, ...), custom_call_target="tpu_custom_call" | custom-call | flops 3221225472 | bytes 16777216 | tf_op jit(solution)/shard_map/pair_back/pallas_call | solution.py:317
  235.3 2.5 fusion.80
  247.5 2.8 fusion.26
  251.4 2.8 fusion.25
  254.2 9.3 %pair_back.5 = (bf16[2,128,256,256]{3,2,1,0:T(8,128)(2,1)}, f32[16,256]{1,0:T(8,128)}) custom-call(bf16[2,8,192,256]{3,2,1,0:T(8,128)(2,1)} %get-tuple-element.106.ds_ref, bf16[2,128,256,256]{3,2,1,0:T(8,128)(2,1)} %pair_ref.8, bf16[192,256]{1,0:T(8,128)(2,1)} %bitcast.293, ...), custom_call_target="tpu_custom_call", output_to_operand_aliasing={{0}: (5, {})} | custom-call | flops 3221225472 | bytes 16777216 | tf_op jit(solution)/shard_map/pair_back/pallas_call | solution.py:317
  274.9 9.4 %pair_back.6 = (bf16[2,128,256,256]{3,2,1,0:T(8,128)(2,1)}, f32[16,256]{1,0:T(8,128)}) custom-call(bf16[2,8,192,256]{3,2,1,0:T(8,128)(2,1)} %get-tuple-element.106.ds_ref, bf16[2,128,256,256]{3,2,1,0:T(8,128)(2,1)} %pair_ref.8, bf16[192,256]{1,0:T(8,128)(2,1)} %bitcast.294, ...), custom_call_target="tpu_custom_call", output_to_operand_aliasing={{0}: (5, {})} | custom-call | flops 3221225472 | bytes 16777216 | tf_op jit(solution)/shard_map/pair_back/pallas_call | solution.py:317
  285.4 17.2 %collective-permute-done.22 = f32[2,4608]{1,0:T(2,128)S(1)} collective-permute-done((f32[2,4608]{1,0:T(2,128)S(1)}, f32[2,4608]{1,0:T(2,128)S(1)}, u32[]{:S(2)}, u32[]{:S(2)}) %collective-permute-start.22) | collective-permute-done | bytes 36896 | tf_op jit(solution)/shard_map/ppermute | solution.py:53
  303.6 4.7 %all-to-all-start.2 = ((f32[16,2,4608]{2,1,0:T(2,128)}), f32[16,2,4608]{2,1,0:T(2,128)S(1)}, u32[]{:S(2)}, u32[]{:S(2)}) async-start(f32[16,2,4608]{2,1,0:T(2,128)} %broadcast_in_dim.24), calls=%async_computation.2 | async-start | bytes 1179648 | tf_op jit(solution)/shard_map/all_to_all | solution.py:669
  315.2 2.4 collective-permute-start.41
  319.0 9.4 %pair_back.7 = (bf16[2,128,256,256]{3,2,1,0:T(8,128)(2,1)}, f32[16,256]{1,0:T(8,128)}) custom-call(bf16[2,8,192,256]{3,2,1,0:T(8,128)(2,1)} %get-tuple-element.106.ds_ref, bf16[2,128,256,256]{3,2,1,0:T(8,128)(2,1)} %pair_ref.8, bf16[192,256]{1,0:T(8,128)(2,1)} %bitcast.295, ...), custom_call_target="tpu_custom_call", output_to_operand_aliasing={{0}: (5, {})} | custom-call | flops 3221225472 | bytes 16777216 | tf_op jit(solution)/shard_map/pair_back/pallas_call | solution.py:317
  329.4 4.4 %collective-permute-start.37 = (bf16[24,3072]{1,0:T(8,128)(2,1)}, bf16[24,3072]{1,0:T(8,128)(2,1)S(1)}, u32[]{:S(2)}, u32[]{:S(2)}) collective-permute-start(bf16[24,3072]{1,0:T(8,128)(2,1)} %get-tuple-element.153), channel_id=1, source_target_pairs={{0,8},{8,16},{16,24},{24,0},{1,9},{9,17},{17,25},{25,1},{2,10},{10... | collective-permute-start | bytes 442376 | tf_op jit(solution)/shard_map/ppermute | solution.py:57
  333.8 4.5 %collective-permute-done.41 = bf16[96,768]{1,0:T(8,128)(2,1)} collective-permute-done((bf16[96,768]{1,0:T(8,128)(2,1)}, bf16[96,768]{1,0:T(8,128)(2,1)}, u32[]{:S(2)}, u32[]{:S(2)}) %collective-permute-start.41) | collective-permute-done | bytes 147488 | tf_op jit(solution)/shard_map/ppermute | solution.py:57
  343.0 4.7 %collective-permute-done.38 = bf16[24,3072]{1,0:T(8,128)(2,1)S(1)} collective-permute-done((bf16[24,3072]{1,0:T(8,128)(2,1)}, bf16[24,3072]{1,0:T(8,128)(2,1)S(1)}, u32[]{:S(2)}, u32[]{:S(2)}) %collective-permute-start.38) | collective-permute-done | bytes 147488 | tf_op jit(solution)/shard_map/ppermute | solution.py:57
  347.7 2.7 collective-permute-done.39
  361.5 5.4 %collective-permute-done.35 = bf16[24,3072]{1,0:T(8,128)(2,1)S(1)} collective-permute-done((bf16[24,3072]{1,0:T(8,128)(2,1)S(1)}, bf16[24,3072]{1,0:T(8,128)(2,1)S(1)}, u32[]{:S(2)}, u32[]{:S(2)}) %collective-permute-start.35) | collective-permute-done | bytes 147488 | tf_op jit(solution)/shard_map/ppermute | solution.py:57
  369.0 4.5 %collective-permute-start.25 = (bf16[24,1920]{1,0:T(8,128)(2,1)S(1)}, bf16[24,1920]{1,0:T(8,128)(2,1)S(1)}, u32[]{:S(2)}, u32[]{:S(2)}) collective-permute-start(bf16[24,1920]{1,0:T(8,128)(2,1)S(1)} %get-tuple-element.160), channel_id=1, source_target_pairs={{0,8},{8,16},{16,24},{24,0},{1,9},{9,17},{17,25},{25,1},{2,10},{10... | collective-permute-start | bytes 276488 | tf_op jit(solution)/shard_map/ppermute | solution.py:57
  374.8 2.8 collective-permute-start.27
  384.7 5.3 %all-to-all-start.3 = ((f32[32,1,288]{2,1,0:T(1,128)}), f32[32,1,288]{2,1,0:T(1,128)S(1)}, u32[]{:S(2)}, u32[]{:S(2)}) async-start(f32[32,1,288]{2,1,0:T(1,128)} %copy.109), calls=%async_computation.3 | async-start | bytes 98304 | tf_op jit(solution)/shard_map/all_to_all | solution.py:680
  390.1 3.7 collective-permute-start.32
  (413 shorter events, 137.0 us)
Async XLA Ops:
  7.3 148.4 %all-gather.2.cloned.1.call-start = ((), (), s32[]{:S(2)}) async-start(), calls=%async_computation.4 | async-start | bytes 14598144 | tf_op jit(solution)/shard_map/all_gather | solution.py:503
  14.4 43.3 %collective-permute-start.1 = (bf16[24,3840]{1,0:T(8,128)(2,1)}, bf16[24,3840]{1,0:T(8,128)(2,1)S(1)}, u32[]{:S(2)}, u32[]{:S(2)}) collective-permute-start(bf16[24,3840]{1,0:T(8,128)(2,1)} %join.2), channel_id=1, source_target_pairs={{0,24},{8,0},{16,8},{24,16},{1,25},{9,1},{17,9},{25,17},{2,26},{10... | collective-permute-start | bytes 552968 | tf_op jit(solution)/shard_map/ppermute | solution.py:57
  19.5 38.3 %collective-permute-start.2 = (bf16[24,3840]{1,0:T(8,128)(2,1)}, bf16[24,3840]{1,0:T(8,128)(2,1)S(1)}, u32[]{:S(2)}, u32[]{:S(2)}) collective-permute-start(bf16[24,3840]{1,0:T(8,128)(2,1)} %join.2), channel_id=1, source_target_pairs={{0,16},{8,24},{16,0},{24,8},{1,17},{9,25},{17,1},{25,9},{2,18},{10... | collective-permute-start | bytes 552968 | tf_op jit(solution)/shard_map/ppermute | solution.py:57
  19.5 38.3 %collective-permute-start.3 = (bf16[24,3840]{1,0:T(8,128)(2,1)}, bf16[24,3840]{1,0:T(8,128)(2,1)S(1)}, u32[]{:S(2)}, u32[]{:S(2)}) collective-permute-start(bf16[24,3840]{1,0:T(8,128)(2,1)} %join.2), channel_id=1, source_target_pairs={{0,8},{8,16},{16,24},{24,0},{1,9},{9,17},{17,25},{25,1},{2,10},{10... | collective-permute-start | bytes 552968 | tf_op jit(solution)/shard_map/ppermute | solution.py:57
  21.9 24.3 %all-to-all-start = ((f32[32,1,296]{2,1,0:T(1,128)}), f32[32,1,296]{2,1,0:T(1,128)S(1)}, u32[]{:S(2)}, u32[]{:S(2)}) async-start(f32[32,1,296]{2,1,0:T(1,128)} %copy.90), calls=%async_computation | async-start | bytes 98304 | tf_op jit(solution)/shard_map/all_to_all | solution.py:519
  27.0 56.1 %collective-permute-start.4 = (bf16[2,128,768]{2,1,0:T(8,128)(2,1)S(1)}, bf16[2,128,768]{2,1,0:T(8,128)(2,1)S(1)}, u32[]{:S(2)}, u32[]{:S(2)}) collective-permute-start(bf16[2,128,768]{2,1,0:T(8,128)(2,1)S(1)} %copy-done.5), channel_id=1, source_target_pairs={{0,1},{1,0},{2,3},{3,2},{4,5},{5,4},{6,7},{7,6},{8,9},{9,8},{10,11... | collective-permute-start | bytes 1179656 | tf_op jit(solution)/shard_map/ppermute | solution.py:53
  51.2 38.7 %all-to-all-start.1 = ((f32[16,2,4608]{2,1,0:T(2,128)}), f32[16,2,4608]{2,1,0:T(2,128)S(1)}, u32[]{:S(2)}, u32[]{:S(2)}) async-start(f32[16,2,4608]{2,1,0:T(2,128)} %reshape.1040), calls=%async_computation.1 | async-start | bytes 1179648 | tf_op jit(solution)/shard_map/all_to_all | solution.py:536
  58.0 25.5 %collective-permute-start.8 = (bf16[4,24,1920]{2,1,0:T(8,128)(2,1)S(1)}, bf16[4,24,1920]{2,1,0:T(8,128)(2,1)S(1)}, u32[]{:S(2)}, u32[]{:S(2)}) collective-permute-start(bf16[4,24,1920]{2,1,0:T(8,128)(2,1)S(1)} %get-tuple-element.145), channel_id=1, source_target_pairs={{0,4},{4,0},{1,5},{5,1},{2,6},{6,2},{3,7},{7,3},{8,12},{12,8},{9,1... | collective-permute-start | bytes 1105928 | tf_op jit(solution)/shard_map/ppermute | solution.py:53
  60.1 25.7 %collective-permute-start.5 = (bf16[4,24,1920]{2,1,0:T(8,128)(2,1)S(1)}, bf16[4,24,1920]{2,1,0:T(8,128)(2,1)S(1)}, u32[]{:S(2)}, u32[]{:S(2)}) collective-permute-start(bf16[4,24,1920]{2,1,0:T(8,128)(2,1)S(1)} %get-tuple-element.146), channel_id=1, source_target_pairs={{0,1},{1,0},{2,3},{3,2},{4,5},{5,4},{6,7},{7,6},{8,9},{9,8},{10,11... | collective-permute-start | bytes 1105928 | tf_op jit(solution)/shard_map/ppermute | solution.py:53
  84.5 35.6 %collective-permute-start.9 = (bf16[4,2,24,1920]{3,2,0,1:T(8,128)(2,1)}, bf16[4,2,24,1920]{3,2,0,1:T(8,128)(2,1)S(1)}, u32[]{:S(2)}, u32[]{:S(2)}) collective-permute-start(bf16[4,2,24,1920]{3,2,0,1:T(8,128)(2,1)} %maximum_select_fusion.8), channel_id=1, source_target_pairs={{0,1},{1,0},{2,3},{3,2},{4,5},{5,4},{6,7},{7,6},{8,9},{9,8},{10,11... | collective-permute-start | bytes 2211848 | tf_op jit(solution)/shard_map/ppermute | solution.py:53
  90.1 23.8 %collective-permute-start = (f32[2,4608]{1,0:T(2,128)S(1)}, f32[2,4608]{1,0:T(2,128)S(1)}, u32[]{:S(2)}, u32[]{:S(2)}) collective-permute-start(f32[2,4608]{1,0:T(2,128)S(1)} %reduce_sum.162), channel_id=1, source_target_pairs={{0,1},{1,0},{2,3},{3,2},{4,5},{5,4},{6,7},{7,6},{8,9},{9,8},{10,11... | collective-permute-start | bytes 110600 | tf_op jit(solution)/shard_map/ppermute | solution.py:53
  91.0 33.3 %collective-permute-start.6 = (bf16[4,2,24,1920]{3,2,0,1:T(8,128)(2,1)S(1)}, bf16[4,2,24,1920]{3,2,0,1:T(8,128)(2,1)S(1)}, u32[]{:S(2)}, u32[]{:S(2)}) collective-permute-start(bf16[4,2,24,1920]{3,2,0,1:T(8,128)(2,1)S(1)} %maximum_select_fusion.6), channel_id=1, source_target_pairs={{0,4},{4,0},{1,5},{5,1},{2,6},{6,2},{3,7},{7,3},{8,12},{12,8},{9,1... | collective-permute-start | bytes 2211848 | tf_op jit(solution)/shard_map/ppermute | solution.py:53
  181.5 17.3 %collective-permute-start.12 = (bf16[4,4,24,3072]{3,2,1,0:T(8,128)(2,1)}, bf16[4,4,24,3072]{3,2,1,0:T(8,128)(2,1)S(1)}, u32[]{:S(2)}, u32[]{:S(2)}) collective-permute-start(bf16[4,4,24,3072]{3,2,1,0:T(8,128)(2,1)} %bitcast.347), channel_id=1, source_target_pairs={{0,2},{2,0},{1,3},{3,1},{4,6},{6,4},{5,7},{7,5},{8,10},{10,8},{9,1... | collective-permute-start | bytes 7077896 | tf_op jit(solution)/shard_map/ppermute | solution.py:53
  194.9 46.1 %collective-permute-start.16 = (bf16[2,4,96,768]{3,2,1,0:T(8,128)(2,1)}, bf16[2,4,96,768]{3,2,1,0:T(8,128)(2,1)}, u32[]{:S(2)}, u32[]{:S(2)}) collective-permute-start(bf16[2,4,96,768]{3,2,1,0:T(8,128)(2,1)} %get-tuple-element.124), channel_id=1, source_target_pairs={{0,4},{4,0},{1,5},{5,1},{2,6},{6,2},{3,7},{7,3},{8,12},{12,8},{9,1... | collective-permute-start | bytes 3538952 | tf_op jit(solution)/shard_map/ppermute | solution.py:53
  197.5 44.1 %collective-permute-start.15 = (bf16[2,4,24,3072]{3,2,1,0:T(8,128)(2,1)}, bf16[2,4,24,3072]{3,2,1,0:T(8,128)(2,1)}, u32[]{:S(2)}, u32[]{:S(2)}) collective-permute-start(bf16[2,4,24,3072]{3,2,1,0:T(8,128)(2,1)} %get-tuple-element.130), channel_id=1, source_target_pairs={{0,1},{1,0},{2,3},{3,2},{4,5},{5,4},{6,7},{7,6},{8,9},{9,8},{10,11... | collective-permute-start | bytes 3538952 | tf_op jit(solution)/shard_map/ppermute | solution.py:53
  201.2 62.3 %collective-permute-start.20 = (bf16[2,4,24,3072]{3,2,1,0:T(8,128)(2,1)}, bf16[2,4,24,3072]{3,2,1,0:T(8,128)(2,1)}, u32[]{:S(2)}, u32[]{:S(2)}) collective-permute-start(bf16[2,4,24,3072]{3,2,1,0:T(8,128)(2,1)} %get-tuple-element.126), channel_id=1, source_target_pairs={{0,4},{4,0},{1,5},{5,1},{2,6},{6,2},{3,7},{7,3},{8,12},{12,8},{9,1... | collective-permute-start | bytes 3538952 | tf_op jit(solution)/shard_map/ppermute | solution.py:53
  224.5 22.8 %collective-permute-start.18 = (bf16[4,4,24,1920]{3,2,1,0:T(8,128)(2,1)}, bf16[4,4,24,1920]{3,2,1,0:T(8,128)(2,1)}, u32[]{:S(2)}, u32[]{:S(2)}) collective-permute-start(bf16[4,4,24,1920]{3,2,1,0:T(8,128)(2,1)} %bitcast.350), channel_id=1, source_target_pairs={{0,2},{2,0},{1,3},{3,1},{4,6},{6,4},{5,7},{7,5},{8,10},{10,8},{9,1... | collective-permute-start | bytes 4423688 | tf_op jit(solution)/shard_map/ppermute | solution.py:53
  224.5 23.0 %collective-permute-start.17 = (bf16[4,4,24,1920]{3,2,1,0:T(8,128)(2,1)}, bf16[4,4,24,1920]{3,2,1,0:T(8,128)(2,1)}, u32[]{:S(2)}, u32[]{:S(2)}) collective-permute-start(bf16[4,4,24,1920]{3,2,1,0:T(8,128)(2,1)} %bitcast.349), channel_id=1, source_target_pairs={{0,2},{2,0},{1,3},{3,1},{4,6},{6,4},{5,7},{7,5},{8,10},{10,8},{9,1... | collective-permute-start | bytes 4423688 | tf_op jit(solution)/shard_map/ppermute | solution.py:53
  241.0 22.5 %collective-permute-start.14 = (bf16[2,2,128,768]{3,2,1,0:T(8,128)(2,1)}, bf16[2,2,128,768]{3,2,1,0:T(8,128)(2,1)}, u32[]{:S(2)}, u32[]{:S(2)}) collective-permute-start(bf16[2,2,128,768]{3,2,1,0:T(8,128)(2,1)} %fusion.119), channel_id=1, source_target_pairs={{0,1},{1,0},{2,3},{3,2},{4,5},{5,4},{6,7},{7,6},{8,9},{9,8},{10,11... | collective-permute-start | bytes 2359304 | tf_op jit(solution)/shard_map/ppermute | solution.py:53
  244.2 64.2 %collective-permute-start.21 = (bf16[4,96,768]{2,1,0:T(8,128)(2,1)}, bf16[4,96,768]{2,1,0:T(8,128)(2,1)}, u32[]{:S(2)}, u32[]{:S(2)}) collective-permute-start(bf16[4,96,768]{2,1,0:T(8,128)(2,1)} %fusion.131), channel_id=1, source_target_pairs={{0,1},{1,0},{2,3},{3,2},{4,5},{5,4},{6,7},{7,6},{8,9},{9,8},{10,11... | collective-permute-start | bytes 1769480 | tf_op jit(solution)/shard_map/ppermute | solution.py:53
  247.3 62.7 %collective-permute-start.19 = (bf16[4,24,3072]{2,1,0:T(8,128)(2,1)}, bf16[4,24,3072]{2,1,0:T(8,128)(2,1)}, u32[]{:S(2)}, u32[]{:S(2)}) collective-permute-start(bf16[4,24,3072]{2,1,0:T(8,128)(2,1)} %fusion.130), channel_id=1, source_target_pairs={{0,4},{4,0},{1,5},{5,1},{2,6},{6,2},{3,7},{7,3},{8,12},{12,8},{9,1... | collective-permute-start | bytes 1769480 | tf_op jit(solution)/shard_map/ppermute | solution.py:53
  250.3 106.4 %collective-permute-start.23 = (bf16[2,4,24,1920]{3,2,1,0:T(8,128)(2,1)}, bf16[2,4,24,1920]{3,2,1,0:T(8,128)(2,1)}, u32[]{:S(2)}, u32[]{:S(2)}) collective-permute-start(bf16[2,4,24,1920]{3,2,1,0:T(8,128)(2,1)} %get-tuple-element.136), channel_id=1, source_target_pairs={{0,1},{1,0},{2,3},{3,2},{4,5},{5,4},{6,7},{7,6},{8,9},{9,8},{10,11... | collective-permute-start | bytes 2211848 | tf_op jit(solution)/shard_map/ppermute | solution.py:53
  272.3 78.8 %collective-permute-start.33 = (bf16[4,24,3072]{2,1,0:T(8,128)(2,1)}, bf16[4,24,3072]{2,1,0:T(8,128)(2,1)}, u32[]{:S(2)}, u32[]{:S(2)}) collective-permute-start(bf16[4,24,3072]{2,1,0:T(8,128)(2,1)} %fusion.133), channel_id=1, source_target_pairs={{0,1},{1,0},{2,3},{3,2},{4,5},{5,4},{6,7},{7,6},{8,9},{9,8},{10,11... | collective-permute-start | bytes 1769480 | tf_op jit(solution)/shard_map/ppermute | solution.py:53
  273.7 28.8 %collective-permute-start.22 = (f32[2,4608]{1,0:T(2,128)S(1)}, f32[2,4608]{1,0:T(2,128)S(1)}, u32[]{:S(2)}, u32[]{:S(2)}) collective-permute-start(f32[2,4608]{1,0:T(2,128)S(1)} %constant_dynamic-update-slice_fusion), channel_id=1, source_target_pairs={{0,1},{1,0},{2,3},{3,2},{4,5},{5,4},{6,7},{7,6},{8,9},{9,8},{10,11... | collective-permute-start | bytes 110600 | tf_op jit(solution)/shard_map/ppermute | solution.py:53
  303.6 75.5 %all-to-all-start.2 = ((f32[16,2,4608]{2,1,0:T(2,128)}), f32[16,2,4608]{2,1,0:T(2,128)S(1)}, u32[]{:S(2)}, u32[]{:S(2)}) async-start(f32[16,2,4608]{2,1,0:T(2,128)} %broadcast_in_dim.24), calls=%async_computation.2 | async-start | bytes 1179648 | tf_op jit(solution)/shard_map/all_to_all | solution.py:669
  315.2 23.1 %collective-permute-start.41 = (bf16[96,768]{1,0:T(8,128)(2,1)}, bf16[96,768]{1,0:T(8,128)(2,1)}, u32[]{:S(2)}, u32[]{:S(2)}) collective-permute-start(bf16[96,768]{1,0:T(8,128)(2,1)} %get-tuple-element.152), channel_id=1, source_target_pairs={{0,16},{8,24},{16,0},{24,8},{1,17},{9,25},{17,1},{25,9},{2,18},{10... | collective-permute-start | bytes 442376 | tf_op jit(solution)/shard_map/ppermute | solution.py:57
  317.6 20.7 %collective-permute-start.42 = (bf16[96,768]{1,0:T(8,128)(2,1)}, bf16[96,768]{1,0:T(8,128)(2,1)}, u32[]{:S(2)}, u32[]{:S(2)}) collective-permute-start(bf16[96,768]{1,0:T(8,128)(2,1)} %get-tuple-element.151), channel_id=1, source_target_pairs={{0,24},{8,0},{16,8},{24,16},{1,25},{9,1},{17,9},{25,17},{2,26},{10... | collective-permute-start | bytes 442376 | tf_op jit(solution)/shard_map/ppermute | solution.py:57
  341.7 17.7 %collective-permute-start.28 = (bf16[2,4,24,1920]{3,2,1,0:T(8,128)(2,1)S(1)}, bf16[2,4,24,1920]{3,2,1,0:T(8,128)(2,1)S(1)}, u32[]{:S(2)}, u32[]{:S(2)}) collective-permute-start(bf16[2,4,24,1920]{3,2,1,0:T(8,128)(2,1)S(1)} %copy-done.38), channel_id=1, source_target_pairs={{0,4},{4,0},{1,5},{5,1},{2,6},{6,2},{3,7},{7,3},{8,12},{12,8},{9,1... | collective-permute-start | bytes 2211848 | tf_op jit(solution)/shard_map/ppermute | solution.py:53
  359.4 18.2 %collective-permute-start.29 = (bf16[4,24,1920]{2,1,0:T(8,128)(2,1)S(1)}, bf16[4,24,1920]{2,1,0:T(8,128)(2,1)S(1)}, u32[]{:S(2)}, u32[]{:S(2)}) collective-permute-start(bf16[4,24,1920]{2,1,0:T(8,128)(2,1)S(1)} %fusion.140), channel_id=1, source_target_pairs={{0,1},{1,0},{2,3},{3,2},{4,5},{5,4},{6,7},{7,6},{8,9},{9,8},{10,11... | collective-permute-start | bytes 1105928 | tf_op jit(solution)/shard_map/ppermute | solution.py:53
  369.0 21.1 %collective-permute-start.25 = (bf16[24,1920]{1,0:T(8,128)(2,1)S(1)}, bf16[24,1920]{1,0:T(8,128)(2,1)S(1)}, u32[]{:S(2)}, u32[]{:S(2)}) collective-permute-start(bf16[24,1920]{1,0:T(8,128)(2,1)S(1)} %get-tuple-element.160), channel_id=1, source_target_pairs={{0,8},{8,16},{16,24},{24,0},{1,9},{9,17},{17,25},{25,1},{2,10},{10... | collective-permute-start | bytes 276488 | tf_op jit(solution)/shard_map/ppermute | solution.py:57
  373.5 20.2 %collective-permute-start.26 = (bf16[24,1920]{1,0:T(8,128)(2,1)S(1)}, bf16[24,1920]{1,0:T(8,128)(2,1)S(1)}, u32[]{:S(2)}, u32[]{:S(2)}) collective-permute-start(bf16[24,1920]{1,0:T(8,128)(2,1)S(1)} %get-tuple-element.162), channel_id=1, source_target_pairs={{0,16},{8,24},{16,0},{24,8},{1,17},{9,25},{17,1},{25,9},{2,18},{10... | collective-permute-start | bytes 276488 | tf_op jit(solution)/shard_map/ppermute | solution.py:57
  374.8 19.0 %collective-permute-start.27 = (bf16[24,1920]{1,0:T(8,128)(2,1)S(1)}, bf16[24,1920]{1,0:T(8,128)(2,1)S(1)}, u32[]{:S(2)}, u32[]{:S(2)}) collective-permute-start(bf16[24,1920]{1,0:T(8,128)(2,1)S(1)} %get-tuple-element.161), channel_id=1, source_target_pairs={{0,24},{8,0},{16,8},{24,16},{1,25},{9,1},{17,9},{25,17},{2,26},{10... | collective-permute-start | bytes 276488 | tf_op jit(solution)/shard_map/ppermute | solution.py:57
  (85 other events, 622.4 us)
Sparse Core Ops, SparseCore 0:
  11.6 141.1 all-gather.1

commit v3 on v2

--- a/solution.py
+++ b/solution.py
@@ -107,18 +107,36 @@
     return (jnp.arange(n, dtype=jnp.int32)[:, None] == old[None, :]).astype(BF16)
 
 
+def down_order(rows, groups, routes, nz):
+    n = 8 * nz * rows * groups
+    new = jnp.arange(n, dtype=jnp.int32)
+    group = new // (8 * nz * rows)
+    part = new // (nz * rows) % 8
+    late = group >= groups // 2
+    firsts, seconds = part // 2 % 2, part % 2
+    at = {"c": part // 4}
+    for axis in ("x", "y"):
+        early_bit = firsts if routes[1][0] == axis else seconds
+        late_bit = firsts if routes[0][0] == axis else seconds
+        at[axis] = jnp.where(late, late_bit, early_bit)
+    at = {k: v ^ lax.axis_index(k) for k, v in at.items()}
+    old = (((new // rows % nz * 2 + at["x"]) * 2 + at["c"]) * 2 + at["y"]) * groups * rows + group * rows + new % rows
+    return (jnp.arange(n, dtype=jnp.int32)[None, :] == old[:, None]).astype(BF16)
+
+
 def relative(value, hot):
     return dot(hot, value, ((0,), (1,))).astype(BF16)
 
 
 class Reduction:
     def __init__(self, keep, send, nz, order):
-        self.keep, self.nz, self.order = keep, nz, order
+        self.keep = keep if isinstance(keep, tuple) else (keep[:2], keep[2:])
+        self.nz, self.order = nz, order
         self.got = swap(send, "c")
 
     def first(self):
-        self.give = add_low(self.keep[2:], self.got[2:])
-        self.keep = add_low(self.keep[:2], self.got[:2])
+        self.give = add_low(self.keep[1], self.got[2:])
+        self.keep = add_low(self.keep[0], self.got[:2])
         self.got = swap(self.give, self.order[0])
         return self
 
@@ -129,47 +147,47 @@
         return self
 
     def third(self):
-        self.give = block = add_low(self.keep, self.got)
+        return add_low(self.keep, self.got)
+
+
+class Line:
+    def __init__(self, blocks, nz):
+        block = jnp.concatenate(blocks, axis=-1)
         place = lax.axis_index("z")
         pick = lambda i: lax.dynamic_index_in_dim(block, i, 0, keepdims=False)
         self.keep = pick(place)
-        self.got = [shift(pick((place + by) % self.nz), "z", self.nz, by) for by in range(1, self.nz)]
-        return self
-
-    def total(self):
+        self.sent = [pick((place + by) % nz) for by in range(1, nz)]
+        self.got = [shift(sent, "z", nz, by) for by, sent in enumerate(self.sent, 1)]
+
+    def total(self, *needed):
         total = self.keep.astype(F32)
-        for got in self.got:
+        for got in after(self.got, *needed):
             total = total + got.astype(F32)
         return total
 
 
-def bias_kernel(pair_ref, wide_ref, out_ref, table):
-    lanes = lax.broadcasted_iota(jnp.int32, wide_ref.shape, 1) % TILE
-    channels = wide_ref.shape[0]
-
-    @pl.when((pl.program_id(0) == 0) & (pl.program_id(1) == 0))
-    def _():
-        wide = wide_ref[...].astype(F32)
-        for i in range(TILE):
-            table[i * channels : (i + 1) * channels, :] = jnp.where(lanes == i, wide, 0.0).astype(BF16)
-
-    rows = jnp.concatenate([pair_ref[0, i] for i in range(TILE)], axis=1)
-    out_ref[0, 0] = dot(rows, table[...]).T
-
-
-def pair_bias(pair, wide):
+def bias_kernel(pair_ref, wide_ref, out_ref):
+    wide = wide_ref[...]
+    lanes = lax.broadcasted_iota(jnp.int32, (pair_ref.shape[2], wide.shape[1]), 1) % TILE
+    for n in range(out_ref.shape[1]):
+        total = dot(pair_ref[0, n * TILE], wide)
+        for i in range(1, TILE):
+            total = jnp.where(lanes == i, dot(pair_ref[0, n * TILE + i], wide), total)
+        out_ref[0, n] = total.T
+
+
+def pair_bias(pair, wide, group=4):
     chains, local, length, channels = pair.shape
     blocks, tall = local // TILE, wide.shape[1]
     return pl.pallas_call(
         bias_kernel,
-        grid=(chains, blocks),
+        grid=(chains, blocks // group),
         in_specs=[
-            pl.BlockSpec((1, TILE, length, channels), lambda b, i: (b, i, 0, 0)),
+            pl.BlockSpec((1, group * TILE, length, channels), lambda b, i: (b, i, 0, 0)),
             pl.BlockSpec(wide.shape, lambda b, i: (0, 0)),
         ],
-        out_specs=pl.BlockSpec((1, 1, tall, length), lambda b, i: (b, i, 0, 0)),
+        out_specs=pl.BlockSpec((1, group, tall, length), lambda b, i: (b, i, 0, 0)),
         out_shape=jax.ShapeDtypeStruct((chains, blocks, tall, length), F32),
-        scratch_shapes=[pltpu.VMEM((TILE * channels, tall), BF16)],
         compiler_params=params(),
         cost_estimate=pl.CostEstimate(flops=2 * pair.size * tall, bytes_accessed=2 * pair.size, transcendentals=0),
         name="pair_bias",
@@ -218,7 +236,8 @@
     )(bias, queries, keys, values, mask)
 
 
-def attend_back_kernel(factor, probs_ref, q_ref, g_ref, k_ref, v_ref, mask_ref, ds_ref, dq_ref, dk_ref, dv_ref, dk_sum, dv_sum):
+def attend_back_kernel(factor, place_ref, probs_ref, q_ref, g_ref, k_ref, v_ref, mask_ref, ds_ref, dq_ref, dk_ref, dv_ref,
+                       keep_ref, give_ref, dk_sum, dv_sum):
     heads = mask_ref.shape[0] // TILE
     keys, values, mask = k_ref[0], v_ref[0], mask_ref[...]
 
@@ -248,9 +267,14 @@
     def _():
         dk_ref[0] = (dk_sum[...] * factor).astype(BF16)
         dv_ref[0] = dv_sum[...].astype(BF16)
-
-
-def attend_back(probs, queries, grads, keys, values, mask, factor, group=4):
+        local = keep_ref.shape[1]
+        for ref, place in ((keep_ref, place_ref[0]), (give_ref, 1 - place_ref[0])):
+            at = pl.ds(pl.multiple_of(place * local, local), local)
+            ref[0, :, : dk_sum.shape[1]] = (dk_sum[at, :] * factor).astype(BF16)
+            ref[0, :, dk_sum.shape[1] :] = dv_sum[at, :].astype(BF16)
+
+
+def attend_back(place, probs, queries, grads, keys, values, mask, factor, group=4):
     chains, blocks, tall, length = probs.shape
     width = mask.shape[1]
     rows = chains * blocks * TILE
@@ -261,6 +285,7 @@
         functools.partial(attend_back_kernel, factor),
         grid=(chains, steps),
         in_specs=[
+            pl.BlockSpec(memory_space=pltpu.SMEM),
             square,
             row_spec,
             row_spec,
@@ -268,107 +293,118 @@
             pl.BlockSpec((1, length, width), lambda b, i: (b, 0, 0)),
             pl.BlockSpec(mask.shape, lambda b, i: (0, 0)),
         ],
-        out_specs=[square, row_spec] + [pl.BlockSpec((1, length, width), lambda b, i: (b, 0, 0))] * 2,
+        out_specs=[square, row_spec] + [pl.BlockSpec((1, length, width), lambda b, i: (b, 0, 0))] * 2
+        + [pl.BlockSpec((1, blocks * TILE, 2 * width), lambda b, i: (b, 0, 0))] * 2,
         out_shape=[
             jax.ShapeDtypeStruct(probs.shape, BF16),
             jax.ShapeDtypeStruct((rows, width), BF16),
             jax.ShapeDtypeStruct((chains, length, width), BF16),
             jax.ShapeDtypeStruct((chains, length, width), BF16),
+            jax.ShapeDtypeStruct((chains, blocks * TILE, 2 * width), BF16),
+            jax.ShapeDtypeStruct((chains, blocks * TILE, 2 * width), BF16),
         ],
         scratch_shapes=[pltpu.VMEM((length, width), F32), pltpu.VMEM((length, width), F32)],
         compiler_params=params(),
         cost_estimate=pl.CostEstimate(flops=10 * probs.size * width, bytes_accessed=6 * probs.size, transcendentals=0),
         name="attend_back",
-    )(probs, queries, grads, keys, values, mask)
+    )(place, probs, queries, grads, keys, values, mask)
 
 
 def pair_back_kernel(ds_ref, pair_ref, tall_ref, turn_ref, old_dw_ref, *rest):
-    grad_ref, dw_ref, table = rest[-3:]
-    channels = tall_ref.shape[1]
+    grad_ref, dw_ref = rest[-2:]
 
     @pl.when(pl.program_id(0) == 0)
     def _():
-        rows = lax.broadcasted_iota(jnp.int32, tall_ref.shape, 0) % TILE
-        tall = tall_ref[...].astype(F32)
+        dw_ref[...] = old_dw_ref[...]
+
+    tall = tall_ref[...]
+    total = dw_ref[...]
+    for n in range(ds_ref.shape[1]):
+        scores_grad = ds_ref[0, n]
+        by_row = dot(turn_ref[...], scores_grad).astype(BF16)
+        turned = scores_grad.T
+        lanes = lax.broadcasted_iota(jnp.int32, turned.shape, 1) % TILE
         for i in range(TILE):
-            table[:, i * channels : (i + 1) * channels] = jnp.where(rows == i, tall, 0.0).astype(BF16)
-        dw_ref[...] = old_dw_ref[...]
-
-    scores_grad = ds_ref[0, 0]
-    turned = scores_grad.T
-    by_row = dot(turn_ref[...], scores_grad).astype(BF16)
-    span = 4
-    total = dw_ref[...]
-    for k in range(TILE // span):
-        spread = dot(turned, table[:, k * span * channels : (k + 1) * span * channels]).astype(BF16)
-        for n in range(span):
-            i = k * span + n
-            grad_ref[0, i] = spread[:, n * channels : (n + 1) * channels]
-            total = total + dot(by_row[i * TILE : (i + 1) * TILE], pair_ref[0, i])
+            at = n * TILE + i
+            grad_ref[0, at] = dot(jnp.where(lanes == i, turned, jnp.zeros_like(turned)), tall).astype(BF16)
+            total = total + dot(by_row[i * TILE : (i + 1) * TILE], pair_ref[0, at])
     dw_ref[...] = total
 
 
-def pair_back(scores_grad, pair, tall, turn, part, parts, old_dw, *old):
+def pair_back(scores_grad, pair, tall, turn, start, count, old_dw, *old, group=2):
     chains, local, length, channels = pair.shape
     blocks, high = scores_grad.shape[1:3]
-    count = chains * blocks // parts
-    place = lambda i: ((part * count + i) // blocks, (part * count + i) % blocks, 0, 0)
+    blocks = blocks // group
+    place = lambda i: ((start + i) // blocks, (start + i) % blocks, 0, 0)
+    size = pair.size * count // (chains * blocks)
     fixed = lambda i: (0, 0)
     return pl.pallas_call(
         pair_back_kernel,
         grid=(count,),
         in_specs=[
-            pl.BlockSpec((1, 1, high, length), place),
-            pl.BlockSpec((1, TILE, length, channels), place),
+            pl.BlockSpec((1, group, high, length), place),
+            pl.BlockSpec((1, group * TILE, length, channels), place),
             pl.BlockSpec(tall.shape, fixed),
             pl.BlockSpec(turn.shape, fixed),
             pl.BlockSpec((TILE, channels), fixed),
         ]
         + [pl.BlockSpec(memory_space=pl.ANY)] * len(old),
         out_specs=[
-            pl.BlockSpec((1, TILE, length, channels), place),
+            pl.BlockSpec((1, group * TILE, length, channels), place),
             pl.BlockSpec((TILE, channels), fixed),
         ],
         out_shape=[jax.ShapeDtypeStruct(pair.shape, BF16), jax.ShapeDtypeStruct((TILE, channels), F32)],
         input_output_aliases={5: 0} if old else {},
-        scratch_shapes=[pltpu.VMEM((high, TILE * channels), BF16)],
         compiler_params=params(),
-        cost_estimate=pl.CostEstimate(flops=4 * pair.size * high // parts, bytes_accessed=4 * pair.size // parts, transcendentals=0),
+        cost_estimate=pl.CostEstimate(flops=4 * size * high, bytes_accessed=4 * size, transcendentals=0),
         name="pair_back",
     )(scores_grad, pair, tall, turn, old_dw, *old)
 
 
-def feed_kernel(rows_ref, turned_ref, g_ref, order_ref, line_ref, gate_ref, up_ref, down_ref,
-                out_ref, back_ref, keep_down, send_down, keep_gate, send_gate, keep_up, send_up):
-    @pl.when(pl.program_id(0) == 0)
+def feed_kernel(steps, rows_ref, turned_ref, g_ref, order_ref, line_ref, gate_ref, up_ref, down_ref,
+                out_ref, back_ref, *rest):
+    grads_refs, held = rest[:-1], rest[-1]
+    step = pl.program_id(0)
+    per = held.shape[4] // steps
+    shape = grads_refs[0].shape
+
+    @pl.when(step == 0)
     def _():
         out_ref[...] = jnp.zeros_like(out_ref)
         back_ref[...] = jnp.zeros_like(back_ref)
 
-    rows, grads = rows_ref[...], g_ref[...]
-    w_gate, w_up = gate_ref[...], up_ref[...]
-    width = rows.shape[1]
-    stack = [down_ref[:, k * width : (k + 1) * width] for k in range(down_ref.shape[1] // width)]
-    w_down = dot(line_ref[...], jnp.concatenate(stack, axis=0)).astype(BF16)
-    gate = dot(rows, w_gate)
-    up = dot(rows, w_up)
-    sig = jax.nn.sigmoid(gate)
-    silu = gate * sig
-    hidden = (silu * up).astype(BF16)
-    out_ref[...] += dot(hidden, w_down)
-    hidden_grad = dot(grads, w_down, NT)
-    gate_grad = (hidden_grad * up * (sig + silu * (1.0 - sig))).astype(BF16)
-    up_grad = (hidden_grad * silu).astype(BF16)
-    back_ref[...] += dot(gate_grad, w_gate, NT) + dot(up_grad, w_up, NT)
-    half = turned_ref.shape[1] // 2
-    for k, (right, keep, send) in enumerate(((gate_grad, keep_gate, send_gate), (up_grad, keep_up, send_up))):
-        full = dot(turned_ref[k], right).astype(BF16)
-        keep[...] = full[:half]
-        send[...] = full[half:]
-    hidden_turned = dot(order_ref[...], hidden, NT).astype(BF16)
-    full = dot(hidden_turned, grads).reshape((2,) + keep_down.shape)
-    keep_down[...] = full[0].astype(BF16)
-    send_down[...] = full[1].astype(BF16)
+    @pl.when(step < steps)
+    def _():
+        rows, grads = rows_ref[...], g_ref[...]
+        w_gate, w_up = gate_ref[...], up_ref[...]
+        width = rows.shape[1]
+        stack = [down_ref[:, k * width : (k + 1) * width] for k in range(down_ref.shape[1] // width)]
+        w_down = dot(line_ref[...], jnp.concatenate(stack, axis=0)).astype(BF16)
+        gate = dot(rows, w_gate)
+        up = dot(rows, w_up)
+        sig = jax.nn.sigmoid(gate)
+        silu = gate * sig
+        hidden = (silu * up).astype(BF16)
+        out_ref[...] += dot(hidden, w_down)
+        hidden_grad = dot(grads, w_down, NT)
+        gate_grad = (hidden_grad * up * (sig + silu * (1.0 - sig))).astype(BF16)
+        up_grad = (hidden_grad * silu).astype(BF16)
+        back_ref[...] += dot(gate_grad, w_gate, NT) + dot(up_grad, w_up, NT)
+        for k, right in enumerate((gate_grad, up_grad)):
+            full = dot(turned_ref[k], right).reshape((2,) + shape).astype(BF16)
+            grads_refs[2 * k][...] = full[0]
+            grads_refs[2 * k + 1][...] = full[1]
+        hidden_turned = dot(order_ref[...], hidden, NT).astype(BF16)
+        full = dot(hidden_turned, grads)
+        full = full.reshape(held.shape[:4] + (per,) + shape[2:3] + (width,)).astype(BF16)
+        held[:, :, :, :, pl.ds(step * per, per)] = full
+
+    for route in range(2):
+        for n in range(held.shape[1]):
+            @pl.when(step == steps + n)
+            def _(route=route, n=n):
+                grads_refs[2 * route][...] = held[route, n, 0]
+                grads_refs[2 * route + 1][...] = held[route, n, 1]
 
 
 def feed(rows, turned, grads, order, line, weights, nz):
@@ -376,59 +412,57 @@
     hidden = weights.shape[1] // 3
     block = order.shape[0]
     steps = hidden // block
-    per = nz // steps
-    own = block // (8 * per)
+    groups = hidden // width
+    own = width // (8 * nz)
     fixed = lambda m: (0, 0)
+    last = steps - 1
+    columns = hidden + groups // 2 * width
+    halves = jax.ShapeDtypeStruct((4, nz, own, columns), BF16)
     return pl.pallas_call(
-        feed_kernel,
-        grid=(steps,),
+        functools.partial(feed_kernel, steps),
+        grid=(steps + groups // 2,),
         in_specs=[
             pl.BlockSpec((count, width), fixed),
             pl.BlockSpec((2, width, count), lambda m: (0, 0, 0)),
             pl.BlockSpec((count, width), fixed),
             pl.BlockSpec((block, block), fixed),
             pl.BlockSpec((block, block), fixed),
-            pl.BlockSpec((width, block), lambda m: (0, m)),
-            pl.BlockSpec((width, block), lambda m: (0, steps + m)),
-            pl.BlockSpec((width // steps, hidden), lambda m: (m, 2)),
+            pl.BlockSpec((width, block), lambda m: (0, jnp.minimum(m, last))),
+            pl.BlockSpec((width, block), lambda m: (0, steps + jnp.minimum(m, last))),
+            pl.BlockSpec((width // steps, hidden), lambda m: (jnp.minimum(m, last), 2)),
         ],
         out_specs=[
             pl.BlockSpec((count, width), fixed),
             pl.BlockSpec((count, width), fixed),
-            pl.BlockSpec((4, per, own, width), lambda m: (0, m, 0, 0)),
-            pl.BlockSpec((4, per, own, width), lambda m: (0, m, 0, 0)),
-            *[pl.BlockSpec((width // 2, block), lambda m: (0, m))] * 4,
+            *[pl.BlockSpec((4, nz, own, block), lambda m: (0, 0, 0, m))] * 4,
         ],
         out_shape=[
             jax.ShapeDtypeStruct((count, width), F32),
             jax.ShapeDtypeStruct((count, width), F32),
-            jax.ShapeDtypeStruct((4, nz, own, width), BF16),
-            jax.ShapeDtypeStruct((4, nz, own, width), BF16),
-            *[jax.ShapeDtypeStruct((width // 2, hidden), BF16)] * 4,
-        ],
+            *[halves] * 4,
+        ],
+        scratch_shapes=[pltpu.VMEM((2, groups // 2, 2, 4, nz, own, width), BF16)],
         compiler_params=params(),
         cost_estimate=pl.CostEstimate(flops=24 * count * width * hidden, bytes_accessed=12 * width * hidden, transcendentals=count * hidden),
         name="feed",
     )(rows, turned, grads, order, line, weights, weights, weights)
 
 
-def join_kernel(*refs):
+def join_kernel(cuts, *refs):
     at = 0
-    for ref in refs[:-1]:
-        pieces = [ref[k] for k in range(ref.shape[0])] if len(ref.shape) == 3 else [ref[...]]
-        for piece in pieces:
-            refs[-1][:, at : at + piece.shape[1]] = piece
-            at += piece.shape[1]
-
-
-def join(*pieces):
-    columns = sum(p.shape[-1] * (p.shape[0] if p.ndim == 3 else 1) for p in pieces)
+    for which, start, size in cuts:
+        piece = refs[which][:, start : start + size] if len(refs[which].shape) == 2 else refs[which][start]
+        refs[-1][:, at : at + piece.shape[1]] = piece
+        at += piece.shape[1]
+
+
+def join(arrays, cuts):
     return pl.pallas_call(
-        join_kernel,
-        out_shape=jax.ShapeDtypeStruct((pieces[0].shape[-2], columns), BF16),
+        functools.partial(join_kernel, cuts),
+        out_shape=jax.ShapeDtypeStruct((arrays[0].shape[0], sum(c[2] for c in cuts)), BF16),
         compiler_params=params(),
         name="join",
-    )(*pieces)
+    )(*arrays)
 
 
 def project_kernel(own_ref, all_ref, first_ref, second_ref, q_ref, k_ref, v_ref, gate_ref):
@@ -461,9 +495,8 @@
     width = own_ref.shape[1]
     half = width // 2
     for k, (inner, outer) in enumerate((((own_ref, dq_ref), (all_ref, dk_ref)), ((all_ref, dv_ref), (own_ref, dg_ref)))):
-        for n in range(2):
-            rows = slice(n * half, (n + 1) * half)
-            result = sums[2 * k + n]
+        for n, rows in enumerate((slice(0, half // 2), slice(half // 2, half), slice(half, width))):
+            result = sums[3 * k + n]
             result[:, :width] = dot(inner[0][k, rows], inner[1][...]).astype(BF16)
             result[:, width : 2 * width] = dot(outer[0][k, rows], outer[1][...]).astype(BF16)
             result[:, 2 * width :] = dot(gated_ref[k, rows], out_ref[:, k * half : (k + 1) * half]).astype(BF16)
@@ -473,7 +506,7 @@
     width = own.shape[1]
     return pl.pallas_call(
         project_back_kernel,
-        out_shape=[jax.ShapeDtypeStruct((width // 2, 5 * width // 2), BF16)] * 4,
+        out_shape=[jax.ShapeDtypeStruct((width // n, 5 * width // 2), BF16) for n in (4, 4, 2)] * 2,
         compiler_params=params(),
         cost_estimate=pl.CostEstimate(flops=16 * own.size * width, bytes_accessed=16 * width * width, transcendentals=0),
         name="project_back",
@@ -499,11 +532,16 @@
     half = width // 2
     groups = w_ffdown.shape[0] // own
     routes = (("y", "x"), ("x", "y"))
-    stacked = join(w_ffgate, w_ffup, w_ffdown.reshape(groups, own, width))
+    stacked = join(
+        (w_ffgate, w_ffup, w_ffdown.reshape(groups, own, width)),
+        [(0, 0, hidden_width), (1, 0, hidden_width)] + [(2, k, width) for k in range(groups)],
+    )
     weights = lax.all_gather(stacked, ALL, axis=0, tiled=True)
-    attention = Gathering(
-        join(w_qkv[:, : 2 * width], w_out[:, :half], w_qkv[:, 2 * width :], w_gate, w_out[:, half:]), nz, routes
-    )
+    packed = join(
+        (w_qkv, w_gate, w_out),
+        [(0, 0, 2 * width), (2, 0, half), (0, 2 * width, width), (1, 0, width), (2, half, half)],
+    )
+    attention = Gathering(packed, nz, routes)
     tokens_other = swap(tokens, "y")
 
     facts = jnp.stack([cath_class.astype(F32), cath_arch.astype(F32), cath_topo.astype(F32), times]).reshape(1, -1)
@@ -554,7 +592,8 @@
     attention.got[0] = after(attention.got[0], bias)
     attention.second()
     hots = [spread(own, route, nz) for route in routes]
-    order = spread(groups * own, routes[1], nz * width // hidden_width).T
+    steps = hidden_width // width
+    order = down_order(own, groups, routes, nz // steps)
     in_turned = jnp.stack([relative(normed_one, hot) for hot in hots])
     all_turned = jnp.stack([relative(normed_all, hot) for hot in hots])
     attention.third()
@@ -573,17 +612,27 @@
     branch_two_grad = (gate_two * upstream).astype(BF16).reshape(rows, width)
     out_turned = jnp.stack([relative(gated, hot) for hot in hots])
     turned = jnp.stack([relative(normed_two, hots[k]) for k in (1, 0)])
-    steps = hidden_width // width
     new = jnp.arange(width, dtype=jnp.int32)
     per_step = width // (steps * own)
     old = (new // own % groups) * (per_step * own) + new // (groups * own) * own + new % own
     line = (jnp.arange(width, dtype=jnp.int32)[None, :] == old[:, None]).astype(BF16)
-    weights = after(weights, out_turned, turned)
+    turn_rows = jnp.arange(TILE * TILE)[:, None]
+    turn_columns = jnp.arange(heads * TILE)[None, :]
+    turn = ((turn_rows // TILE == turn_columns % TILE) & (turn_rows % TILE == turn_columns // TILE)).astype(BF16)
+    tall_pair = wide_pair.T
+    weights = after(weights, out_turned, turned, in_turned, all_turned, turn, tall_pair)
     branch_two, normed_two_grad, *grads = feed(normed_two, turned, branch_two_grad, order, line, weights, nz)
-    split = lambda v: v.reshape(4, nz, -1, v.shape[-1])
-    down_sum = Reduction(grads[0], grads[1], nz, routes[1])
-    gate_sum = Reduction(split(grads[2]), split(grads[3]), nz, routes[1])
-    up_sum = Reduction(split(grads[4]), split(grads[5]), nz, routes[0])
+    feed_sums = [Reduction(grads[2 * k], grads[2 * k + 1], nz, routes[1 - k]) for k in range(2)]
+    split = lambda v: v.reshape(-1, nz, own, v.shape[-1])
+
+    def sum_modes(parts):
+        mine = jnp.concatenate(parts, axis=-1)
+        return mine, swap(mine, "y")
+
+    def share_modes(mine, other, *needed):
+        mine = mine + after(other, *needed)
+        mine = jnp.broadcast_to(mine[None], (ndp,) + mine.shape)
+        return lax.all_to_all(mine, DP, split_axis=0, concat_axis=0, tiled=True)
 
     normed_two_grad = normed_two_grad.reshape(chains, local, width)
     middle_grad = upstream + normalise_back(normed_two_grad, scale_two, norm_two, root_two)
@@ -591,86 +640,73 @@
     gated_grad = dot(branch_one_grad, full_out, NT)
     attended_grad = (gated_grad * sigmoid_gate).astype(BF16)
     logits_grad = (gated_grad * attended * (sigmoid_gate * (1.0 - sigmoid_gate))).astype(BF16)
-    up_sum.first(), down_sum.first(), gate_sum.first()
-    attended_grad = after(attended_grad, down_sum.give, gate_sum.give, up_sum.give)
-    scores_grad, query_grad, key_grad, value_grad = attend_back(
-        probs, queries, attended_grad, keys, values, mask, factor
+    branch_two = branch_two.reshape(chains, local, width)
+    gate_one_grad = jnp.sum(middle_grad * branch_one, axis=1)
+    shift_two_grad = jnp.sum(normed_two_grad, axis=1)
+    scale_two_grad = jnp.sum(normed_two_grad * norm_two, axis=1)
+    gate_two_grad = jnp.sum(upstream * branch_two, axis=1)
+    result = (middle + gate_two * branch_two).astype(BF16)
+    for s in feed_sums:
+        s.first()
+    attended_grad = after(attended_grad, *[s.give for s in feed_sums])
+    late_halves = sum_modes([gate_one_grad, shift_two_grad, scale_two_grad, gate_two_grad])
+    place = lax.axis_index("y").astype(jnp.int32)
+    scores_grad, query_grad, key_grad, value_grad, keep, give = attend_back(
+        place.reshape(1), probs, queries, attended_grad, keys, values, mask, factor
     )
     kept_sent = project_back(
         in_turned, all_turned, out_turned, query_grad, key_grad.reshape(-1, width), value_grad.reshape(-1, width),
         logits_grad, branch_one_grad,
     )
-    in_sums = [Reduction(split(kept_sent[2 * k]), split(kept_sent[2 * k + 1]), nz, routes[k]) for k in range(2)]
-    place = lax.axis_index("y")
-    joined = jnp.stack([key_grad, value_grad]).reshape(2, chains, ny, local, width)
-    keep = lax.dynamic_index_in_dim(joined, place, 2, keepdims=False)
-    give = lax.dynamic_index_in_dim(joined, 1 - place, 2, keepdims=False)
+    kept_sent = [split(v) for v in kept_sent]
+    in_sums = [Reduction(tuple(kept_sent[3 * k : 3 * k + 2]), kept_sent[3 * k + 2], nz, routes[k]) for k in range(2)]
     got = swap(give, "y")
-    turn_rows = jnp.arange(TILE * TILE)[:, None]
-    turn_columns = jnp.arange(heads * TILE)[None, :]
-    turn = ((turn_rows // TILE == turn_columns % TILE) & (turn_rows % TILE == turn_columns // TILE)).astype(BF16)
-    tall_pair = wide_pair.T
     pair_sums = (jnp.zeros((TILE, pair.shape[3]), F32),)
-    pieces = 4
-
-    def more_pair(k, *needed):
-        new_grad, new_sum = pair_back(after(scores_grad, *needed), pair, tall_pair, turn, k, pieces, *pair_sums)
+    steps_all = chains * (local // TILE) // 2
+    quarter = steps_all // 4
+
+    def more_pair(start, count, *needed):
+        new_grad, new_sum = pair_back(after(scores_grad, *needed), pair, tall_pair, turn, start, count, *pair_sums)
         return (new_sum, new_grad)
 
-    pair_sums = more_pair(0, kept_sent[0])
-    up_sum.got = after(up_sum.got, pair_sums[0])
-    down_sum.got = after(down_sum.got, pair_sums[0])
-    up_sum.second(), down_sum.second()
+    late_modes = share_modes(*late_halves, kept_sent[0])
+    pair_sums = more_pair(0, quarter, kept_sent[0])
+    for s in feed_sums:
+        s.got = after(s.got, pair_sums[0])
+        s.second()
+    pair_sums = more_pair(quarter, quarter, late_modes, *[s.give for s in feed_sums])
     for s in in_sums:
         s.got = after(s.got, pair_sums[0])
         s.first()
-    pair_sums = more_pair(1, up_sum.give, down_sum.give, *[s.give for s in in_sums])
-    owned = add_low(keep, after(got, pair_sums[0])).reshape(2, rows, width)
-    gate_sum.got = after(gate_sum.got, pair_sums[0])
-    gate_sum.second()
+    owned = add_low(keep, after(got, *[s.give for s in in_sums])).reshape(rows, 2 * width)
     normed_one_grad = (
         dot(query_grad, first_w[:, :width], NT)
-        + dot(owned[0], first_w[:, width : 2 * width], NT)
-        + dot(owned[1], second_w[:, :width], NT)
+        + dot(owned[:, :width], first_w[:, width : 2 * width], NT)
+        + dot(owned[:, width:], second_w[:, :width], NT)
         + dot(logits_grad, second_w[:, width : 2 * width], NT)
     ).reshape(chains, local, width)
-    pair_sums = more_pair(2, normed_one_grad, gate_sum.give)
-    up_sum.got = after(up_sum.got, pair_sums[0])
-    down_sum.got = after(down_sum.got, pair_sums[0])
-    up_sum.third(), down_sum.third()
-    pair_sums = more_pair(3, up_sum.give, down_sum.give)
+    shift_one_grad = jnp.sum(normed_one_grad, axis=1)
+    scale_one_grad = jnp.sum(normed_one_grad * norm_one, axis=1)
+    early_halves = sum_modes([shift_one_grad, scale_one_grad])
+    for s in feed_sums:
+        s.got = after(s.got, normed_one_grad)
+    feed_line = Line([s.third() for s in feed_sums], nz)
+    early_modes = share_modes(*early_halves, *feed_line.sent)
+    pair_sums = more_pair(2 * quarter, steps_all - 2 * quarter, *feed_line.sent, *early_halves)
+    tokens_grad = (middle_grad + normalise_back(normed_one_grad, scale_one, norm_one, root_one)).astype(BF16)
     for s in in_sums:
         s.got = after(s.got, pair_sums[0])
         s.second()
-    gate_sum.got = after(gate_sum.got, pair_sums[0])
-    gate_sum.third()
-    for s in in_sums:
-        s.third()
+    early_modes = after(early_modes, *[s.give for s in in_sums]).reshape(ndp * chains, -1)
+    late_modes = late_modes.reshape(ndp * chains, -1)
     pair_w_sum, pair_grad = pair_sums
-    sum_down, sum_gate, sum_up = down_sum.total(), gate_sum.total(), up_sum.total()
-    sums = [s.total() for s in in_sums]
-    sum_out = jnp.concatenate([s[:, 2 * width :] for s in sums], axis=1)
     grad_pair_w = pair_w_sum[:heads].T
 
-    branch_two = branch_two.reshape(chains, local, width)
-    result = (middle + gate_two * branch_two).astype(BF16)
-    gate_two_grad = jnp.sum(upstream * branch_two, axis=1)
-    shift_two_grad = jnp.sum(normed_two_grad, axis=1)
-    scale_two_grad = jnp.sum(normed_two_grad * norm_two, axis=1)
-    gate_one_grad = jnp.sum(middle_grad * branch_one, axis=1)
-    shift_one_grad = jnp.sum(normed_one_grad, axis=1)
-    scale_one_grad = jnp.sum(normed_one_grad * norm_one, axis=1)
-    tokens_grad = (middle_grad + normalise_back(normed_one_grad, scale_one, norm_one, root_one)).astype(BF16)
-
-    modes_grad = jnp.concatenate(
-        [shift_one_grad, scale_one_grad, gate_one_grad, shift_two_grad, scale_two_grad, gate_two_grad], axis=-1
-    )
-    modes_grad = modes_grad + swap(modes_grad, "y")
-    modes_all = lax.all_to_all(
-        jnp.broadcast_to(modes_grad[None], (ndp, chains, 6 * width)), DP, split_axis=0, concat_axis=0, tiled=True
-    ).reshape(ndp * chains, 6 * width)
-    grad_ada = lax.dot_general(condition_low.astype(F32), modes_all, (((0,), (0,)), ((), ())), precision=HIGH)
-    condition_grad = lax.dot_general(modes_all, w_ada.astype(F32), (((1,), (1,)), ((), ())), precision=HIGH)
+    low_f32, ada_f32 = condition_low.astype(F32), w_ada.astype(F32)
+    exact = lambda left, right, dims: lax.dot_general(left, right, (dims, ((), ())), precision=HIGH)
+    cut = 2 * width
+    grad_ada = jnp.concatenate([exact(low_f32, early_modes, TN), exact(low_f32, late_modes, TN)], axis=1)
+    condition_grad = exact(early_modes, ada_f32[:, :cut], NT) + exact(late_modes, ada_f32[:, cut:], NT)
     before_grad = condition_grad * (sig_before * (1.0 + before * (1.0 - sig_before)))
     outer = lambda left: lax.dot_general(left.astype(F32), before_grad, (((0,), (0,)), ((), ())), precision=HIGH)
     grad_class, grad_arch, grad_topo = outer(hot[0]), outer(hot[1]), outer(hot[2])
@@ -678,6 +714,17 @@
         [outer(features).reshape(devices, time_rows * own), grad_pair_w.reshape(devices, -1)], axis=1
     )
     time_got = lax.all_to_all(time_pack, ALL, split_axis=0, concat_axis=0, tiled=True)
+    for r in in_sums:
+        r.got = after(r.got, time_pack)
+    in_line = Line([r.third() for r in in_sums], nz)
+    feed_total = feed_line.total(time_pack, *in_line.sent)
+    early, late = jnp.split(feed_total, 2, axis=1)
+    sum_gate, sum_up = early[:, :hidden_width], late[:, :hidden_width]
+    sum_down = jnp.concatenate(
+        [t[:, hidden_width + k * width : hidden_width + (k + 1) * width] for t in (early, late) for k in range(groups // 2)], axis=0
+    )
+    sums = jnp.split(in_line.total(), 2, axis=1)
+    sum_out = jnp.concatenate([s[:, 2 * width :] for s in sums], axis=1)
     grad_time = time_got[:, :size_time].reshape(devices, time_rows, own).transpose(1, 0, 2).reshape(time_rows, width)
     grad_pair_own = jnp.sum(time_got[:, size_time:], axis=0).reshape(w_pair.shape)
 

time: 413 us -> 365 us (0.88)
  waiting for transfers between devices: 80 us -> 56.9 us
  starting transfers between devices: 77.2 us -> 66 us
  Pallas kernels: 128 us -> 118 us
  local copies, waits for them, and re-layouts: 29.4 us -> 20.8 us
    ppermute x18 -> x9, starting transfers between devices: 35 us -> 18.1 us  [shift(): lax.ppermute(value, axis, [(i, (i + by) % size) for i in range(size)])]
    ppermute x25 -> x23, waiting for transfers between devices: 45.8 us -> 28.9 us  [swap(): return lax.ppermute(value, axis, [(0, 1), (1, 0)])]
    ppermute x18 -> x9, waiting for transfers between devices: 20.7 us -> 4.62 us  [shift(): lax.ppermute(value, axis, [(i, (i + by) % size) for i in range(size)])]
    unnamed x152 -> x111, local copies, waits for them, and re-layouts: 12.4 us -> 4.76 us
    all_to_all x1 -> x2, waiting for transfers between devices: 0.01 us -> 6.73 us  [share_modes(): return lax.all_to_all(mine, DP, split_axis=0, concat_axis=0, tiled=True)]
    pallas_call x4 -> x3, Pallas kernels: 37.7 us -> 31.4 us  [pair_back(): pl.pallas_call(pair_back_kernel, grid=(count,), in_specs=[pl.BlockSpec((1...]
    all_to_all x1 -> x2, starting transfers between devices: 4.74 us -> 10.9 us  [share_modes(): return lax.all_to_all(mine, DP, split_axis=0, concat_axis=0, tiled=True)]
    pallas_call x4, Pallas kernels: 51.3 us -> 46.4 us  [the longest x1 27.1 us: feed(): pl.pallas_call(functools.partial(feed_kernel, steps), grid=(steps + group...]
  transfers between devices with their start and end apart: 48 -> 38, of which waited for: 12 -> 13; matrix products, arithmetic and copies ran while one was open for 23% -> 27% of each run, Pallas kernels for 25% -> 25%
where the time goes in v3:
time: 365 us; the launch traced here: 360 us
  Pallas kernels  118 us (32%)
  starting transfers between devices  66 us (18%)
  other arithmetic  63.9 us (18%)
  waiting for transfers between devices  56.9 us (16%)
  local copies, waits for them, and re-layouts  20.8 us (6%)
  matrix products  19.5 us (5%)
  between operations  15.5 us (4%)
    pallas_call x3, Pallas kernels, pair_back(): pl.pallas_call(pair_back_kernel, grid=(count,), in_specs=[pl.BlockSpec((1...  31.4 us
    ppermute x23, waiting for transfers between devices, swap(): return lax.ppermute(value, axis, [(0, 1), (1, 0)])  28.9 us
    convert_element_type x13, other arithmetic, add_low(): return (left.astype(F32) + right.astype(F32)).astype(BF16)  27.9 us
    pallas_call x1, Pallas kernels, feed(): pl.pallas_call(functools.partial(feed_kernel, steps), grid=(steps + group...  27.1 us
    ppermute x23, starting transfers between devices, swap(): return lax.ppermute(value, axis, [(0, 1), (1, 0)])  20.6 us
    ppermute x9, starting transfers between devices, shift(): lax.ppermute(value, axis, [(i, (i + by) % size) for i in range(size)])  18.1 us
    pallas_call x1, Pallas kernels, pair_bias(): pl.pallas_call(bias_kernel, grid=(chains, blocks // group), in_specs=[pl....  15.8 us
    pallas_call x1, Pallas kernels, attend_back(): pl.pallas_call(functools.partial(attend_back_kernel, factor), grid=(chain...  15.8 us
  transfers between devices with their start and end apart: 38, of which 13 were waited for; matrix products, arithmetic and copies ran while one was open for 27% of the time, Pallas kernels for 25%

profile of v3, /device:TPU:0, one launch (start us, length us, event | category | flops | bytes accessed | tf_op | source)
XLA Modules:
  0.0 360.0 jit_solution(12202989576780579268)
XLA Ops:
  10.8 5.0 %collective-permute-start.1 = (bf16[24,3840]{1,0:T(8,128)(2,1)}, bf16[24,3840]{1,0:T(8,128)(2,1)S(1)}, u32[]{:S(2)}, u32[]{:S(2)}) collective-permute-start(bf16[24,3840]{1,0:T(8,128)(2,1)} %join.2), channel_id=1, source_target_pairs={{0,24},{8,0},{16,8},{24,16},{1,25},{9,1},{17,9},{25,17},{2,26},{10... | collective-permute-start | bytes 552968 | tf_op jit(solution)/shard_map/ppermute | solution.py:57
  20.9 5.0 %all-to-all-start = ((f32[32,1,296]{2,1,0:T(1,128)}), f32[32,1,296]{2,1,0:T(1,128)S(1)}, u32[]{:S(2)}, u32[]{:S(2)}) async-start(f32[32,1,296]{2,1,0:T(1,128)} %copy.89), calls=%async_computation | async-start | bytes 98304 | tf_op jit(solution)/shard_map/all_to_all | solution.py:557
  31.9 10.7 %all-to-all-done = f32[32,1,296]{2,1,0:T(1,128)S(1)} async-done(((f32[32,1,296]{2,1,0:T(1,128)}), f32[32,1,296]{2,1,0:T(1,128)S(1)}, u32[]{:S(2)}, u32[]{:S(2)}) %all-to-all-start) | async-done | bytes 37920 | tf_op jit(solution)/shard_map/all_to_all | solution.py:557
  47.4 6.7 %all-to-all-start.1 = ((f32[16,2,4608]{2,1,0:T(2,128)}), f32[16,2,4608]{2,1,0:T(2,128)}, u32[]{:S(2)}, u32[]{:S(2)}) async-start(f32[16,2,4608]{2,1,0:T(2,128)} %reshape.1072), calls=%async_computation.1 | async-start | bytes 1179648 | tf_op jit(solution)/shard_map/all_to_all | solution.py:574
  57.2 15.8 %pair_bias.1.bias_ref = f32[2,8,192,256]{3,2,1,0:T(8,128)} custom-call(bf16[2,128,256,256]{3,2,1,0:T(8,128)(2,1)} %pair_ref.6, bf16[256,192]{1,0:T(8,128)(2,1)} %copy.98.wide_ref), custom_call_target="tpu_custom_call" | custom-call | flops 6442450944 | bytes 33554432 | tf_op jit(solution)/shard_map/pair_bias/pallas_call | solution.py:182
  90.6 6.4 %collective-permute-done.6 = bf16[4,2,24,1920]{3,2,0,1:T(8,128)(2,1)S(1)} collective-permute-done((bf16[4,2,24,1920]{3,2,0,1:T(8,128)(2,1)}, bf16[4,2,24,1920]{3,2,0,1:T(8,128)(2,1)S(1)}, u32[]{:S(2)}, u32[]{:S(2)}) %collective-permute-start.6) | collective-permute-done | bytes 737312 | tf_op jit(solution)/shard_map/ppermute | solution.py:53
  97.4 14.8 %collective-permute-done.9 = bf16[4,2,24,1920]{3,2,0,1:T(8,128)(2,1)S(1)} collective-permute-done((bf16[4,2,24,1920]{3,2,0,1:T(8,128)(2,1)S(1)}, bf16[4,2,24,1920]{3,2,0,1:T(8,128)(2,1)S(1)}, u32[]{:S(2)}, u32[]{:S(2)}) %collective-permute-start.9) | collective-permute-done | bytes 737312 | tf_op jit(solution)/shard_map/ppermute | solution.py:53
  119.4 6.2 %project.1 = (bf16[256,768]{1,0:T(8,128)(2,1)}, bf16[512,768]{1,0:T(8,128)(2,1)}, bf16[512,768]{1,0:T(8,128)(2,1)}, f32[256,768]{1,0:T(8,128)}) custom-call(bf16[256,768]{1,0:T(8,128)(2,1)} %bitcast.239, bf16[512,768]{1,0:T(8,128)(2,1)} %bitcast.248, bf16[768,1920]{1,0:T(8,128)(2,1)} %bitcast.221, bf16[768,1920]{1,0:T(8,128)(2,1)} %bitcast.225), custom_call_target="tpu_custom_call" | custom-call | flops 1811939328 | bytes 7077888 | tf_op jit(solution)/shard_map/project/pallas_call | solution.py:480
  125.6 11.4 %attend.1 = (f32[2,8,192,256]{3,2,1,0:T(8,128)}, f32[256,768]{1,0:T(8,128)}) custom-call(f32[2,8,192,256]{3,2,1,0:T(8,128)} %pair_bias.1.bias_ref, bf16[256,768]{1,0:T(8,128)(2,1)} %get-tuple-element.74.q_ref, bf16[2,256,768]{2,1,0:T(8,128)(2,1)} %bitcast.287, bf16[2,256,768]{2,1,0:T(8,128)(2,1)} %bitcast.289, bf16[192,768]{1,0:T(8,128)(2,1)} %compare_convert_fusion.mask_ref), custom_call_target="tpu_custom_call" | custom-call | flops 2415919104 | bytes 7864320 | tf_op jit(solution)/shard_map/attend/pallas_call | solution.py:221
  145.5 27.1 %feed.1 = (f32[256,768]{1,0:T(8,128)}, f32[256,768]{1,0:T(8,128)}, bf16[4,4,24,4608]{3,2,1,0:T(8,128)(2,1)}, bf16[4,4,24,4608]{3,2,1,0:T(8,128)(2,1)}, bf16[4,4,...) custom-call(bf16[256,768]{1,0:T(8,128)(2,1)} %bitcast.273, bf16[2,768,256]{2,1,0:T(8,128)(2,1)} %pad_maximum_fusion.4.turned_ref, ...), custom_call_target="tpu_custom_call" | custom-call | flops 14495514624 | bytes 28311552 | tf_op jit(solution)/shard_map/feed/pallas_call | solution.py:421
  181.1 2.6 add_convert_fusion
  184.9 2.7 add_convert_fusion.1
  187.6 15.8 %attend_back.1 = (bf16[2,8,192,256]{3,2,1,0:T(8,128)(2,1)}, bf16[256,768]{1,0:T(8,128)(2,1)}, bf16[2,256,768]{2,1,0:T(8,128)(2,1)}, bf16[2,256,768]{2,1,0:T(8,12...) custom-call(s32[1]{0:T(128)} %bitcast.56.place_ref, ...), custom_call_target="tpu_custom_call" | custom-call | flops 6039797760 | bytes 4718592 | tf_op jit(solution)/shard_map/attend_back/pallas_call | solution.py:284
  203.4 6.4 %project_back.1 = (bf16[192,1920]{1,0:T(8,128)(2,1)}, bf16[192,1920]{1,0:T(8,128)(2,1)}, bf16[384,1920]{1,0:T(8,128)(2,1)}, bf16[192,1920]{1,0:T(8,128)(2,1)}, b...) custom-call(bf16[2,768,256]{2,1,0:T(8,128)(2,1)} %pad_maximum_fusion.6.own_ref, ...), custom_call_target="tpu_custom_call" | custom-call | flops 4831838208 | bytes 9437184 | tf_op jit(solution)/shard_map/project_back/pallas_call | solution.py:507
  210.6 6.5 %all-to-all-start.2 = ((f32[16,2,3072]{2,1,0:T(2,128)}), f32[16,2,3072]{2,1,0:T(2,128)}, u32[]{:S(2)}, u32[]{:S(2)}) async-start(f32[16,2,3072]{2,1,0:T(2,128)} %broadcast_in_dim.25), calls=%async_computation.2 | async-start | bytes 786432 | tf_op jit(solution)/shard_map/all_to_all | solution.py:635
  219.7 2.4 fusion.76
  222.7 8.1 %pair_back.3 = (bf16[2,128,256,256]{3,2,1,0:T(8,128)(2,1)}, f32[16,256]{1,0:T(8,128)}) custom-call(bf16[2,8,192,256]{3,2,1,0:T(8,128)(2,1)} %get-tuple-element.112.ds_ref, bf16[2,128,256,256]{3,2,1,0:T(8,128)(2,1)} %pair_ref.6, bf16[192,256]{1,0:T(8,128)(2,1)} %bitcast.257, bf16[256,192]{1,0:T(8,128)(2,1)} %and_convert_fusion.turn_ref, ...), custom_call_target="tpu_custom_call" | custom-call | flops 3221225472 | bytes 16777216 | tf_op jit(solution)/shard_map/pair_back/pallas_call | solution.py:341
  237.6 2.6 fusion.96
  240.9 2.3 fusion.95
  243.9 8.1 %pair_back.4 = (bf16[2,128,256,256]{3,2,1,0:T(8,128)(2,1)}, f32[16,256]{1,0:T(8,128)}) custom-call(bf16[2,8,192,256]{3,2,1,0:T(8,128)(2,1)} %get-tuple-element.112.ds_ref, bf16[2,128,256,256]{3,2,1,0:T(8,128)(2,1)} %pair_ref.6, bf16[192,256]{1,0:T(8,128)(2,1)} %bitcast.258, ...), custom_call_target="tpu_custom_call", output_to_operand_aliasing={{0}: (5, {})} | custom-call | flops 3221225472 | bytes 16777216 | tf_op jit(solution)/shard_map/pair_back/pallas_call | solution.py:341
  252.0 3.3 fusion.22
  256.9 3.0 add_convert_fusion.9
  274.8 2.7 collective-permute-start.30
  277.5 3.2 collective-permute-done.21
  280.7 3.2 collective-permute-start.31
  283.9 15.2 %pair_back.5 = (bf16[2,128,256,256]{3,2,1,0:T(8,128)(2,1)}, f32[16,256]{1,0:T(8,128)}) custom-call(bf16[2,8,192,256]{3,2,1,0:T(8,128)(2,1)} %get-tuple-element.112.ds_ref, bf16[2,128,256,256]{3,2,1,0:T(8,128)(2,1)} %pair_ref.6, bf16[192,256]{1,0:T(8,128)(2,1)} %bitcast.259, ...), custom_call_target="tpu_custom_call", output_to_operand_aliasing={{0}: (5, {})} | custom-call | flops 6442450944 | bytes 33554432 | tf_op jit(solution)/shard_map/pair_back/pallas_call | solution.py:341
  300.6 4.4 %all-to-all-start.3 = ((f32[16,2,1536]{2,1,0:T(2,128)}), f32[16,2,1536]{2,1,0:T(2,128)S(1)}, u32[]{:S(2)}, u32[]{:S(2)}) async-start(f32[16,2,1536]{2,1,0:T(2,128)} %broadcast_in_dim.27), calls=%async_computation.3 | async-start | bytes 393216 | tf_op jit(solution)/shard_map/all_to_all | solution.py:635
  312.6 5.5 %all-to-all-done.3 = f32[16,2,1536]{2,1,0:T(2,128)S(1)} async-done(((f32[16,2,1536]{2,1,0:T(2,128)}), f32[16,2,1536]{2,1,0:T(2,128)S(1)}, u32[]{:S(2)}, u32[]{:S(2)}) %all-to-all-start.3) | async-done | bytes 196640 | tf_op jit(solution)/shard_map/all_to_all | solution.py:635
  328.1 4.6 %all-to-all-start.4 = ((f32[32,1,288]{2,1,0:T(1,128)}), f32[32,1,288]{2,1,0:T(1,128)S(1)}, u32[]{:S(2)}, u32[]{:S(2)}) async-start(f32[32,1,288]{2,1,0:T(1,128)} %copy.108), calls=%async_computation.4 | async-start | bytes 98304 | tf_op jit(solution)/shard_map/all_to_all | solution.py:716
  333.6 2.7 collective-permute-start.27
  336.2 3.9 %all-to-all-done.4 = f32[32,1,288]{2,1,0:T(1,128)S(1)} async-done(((f32[32,1,288]{2,1,0:T(1,128)}), f32[32,1,288]{2,1,0:T(1,128)S(1)}, u32[]{:S(2)}, u32[]{:S(2)}) %all-to-all-start.4) | async-done | bytes 36896 | tf_op jit(solution)/shard_map/all_to_all | solution.py:716
  346.3 3.5 collective-permute-done.28
  (342 shorter events, 122.7 us)
Async XLA Ops:
  7.2 138.3 %all-gather.2.cloned.1.call-start = ((), (), s32[]{:S(2)}) async-start(), calls=%async_computation.5 | async-start | bytes 14598144 | tf_op jit(solution)/shard_map/all_gather | solution.py:539
  10.8 43.4 %collective-permute-start.1 = (bf16[24,3840]{1,0:T(8,128)(2,1)}, bf16[24,3840]{1,0:T(8,128)(2,1)S(1)}, u32[]{:S(2)}, u32[]{:S(2)}) collective-permute-start(bf16[24,3840]{1,0:T(8,128)(2,1)} %join.2), channel_id=1, source_target_pairs={{0,24},{8,0},{16,8},{24,16},{1,25},{9,1},{17,9},{25,17},{2,26},{10... | collective-permute-start | bytes 552968 | tf_op jit(solution)/shard_map/ppermute | solution.py:57
  15.9 38.4 %collective-permute-start.2 = (bf16[24,3840]{1,0:T(8,128)(2,1)}, bf16[24,3840]{1,0:T(8,128)(2,1)S(1)}, u32[]{:S(2)}, u32[]{:S(2)}) collective-permute-start(bf16[24,3840]{1,0:T(8,128)(2,1)} %join.2), channel_id=1, source_target_pairs={{0,16},{8,24},{16,0},{24,8},{1,17},{9,25},{17,1},{25,9},{2,18},{10... | collective-permute-start | bytes 552968 | tf_op jit(solution)/shard_map/ppermute | solution.py:57
  15.9 38.4 %collective-permute-start.3 = (bf16[24,3840]{1,0:T(8,128)(2,1)}, bf16[24,3840]{1,0:T(8,128)(2,1)S(1)}, u32[]{:S(2)}, u32[]{:S(2)}) collective-permute-start(bf16[24,3840]{1,0:T(8,128)(2,1)} %join.2), channel_id=1, source_target_pairs={{0,8},{8,16},{16,24},{24,0},{1,9},{9,17},{17,25},{25,1},{2,10},{10... | collective-permute-start | bytes 552968 | tf_op jit(solution)/shard_map/ppermute | solution.py:57
  20.9 21.7 %all-to-all-start = ((f32[32,1,296]{2,1,0:T(1,128)}), f32[32,1,296]{2,1,0:T(1,128)S(1)}, u32[]{:S(2)}, u32[]{:S(2)}) async-start(f32[32,1,296]{2,1,0:T(1,128)} %copy.89), calls=%async_computation | async-start | bytes 98304 | tf_op jit(solution)/shard_map/all_to_all | solution.py:557
  26.0 47.0 %collective-permute-start.4 = (bf16[2,128,768]{2,1,0:T(8,128)(2,1)S(1)}, bf16[2,128,768]{2,1,0:T(8,128)(2,1)S(1)}, u32[]{:S(2)}, u32[]{:S(2)}) collective-permute-start(bf16[2,128,768]{2,1,0:T(8,128)(2,1)S(1)} %copy-done.6), channel_id=1, source_target_pairs={{0,1},{1,0},{2,3},{3,2},{4,5},{5,4},{6,7},{7,6},{8,9},{9,8},{10,11... | collective-permute-start | bytes 1179656 | tf_op jit(solution)/shard_map/ppermute | solution.py:53
  47.4 31.9 %all-to-all-start.1 = ((f32[16,2,4608]{2,1,0:T(2,128)}), f32[16,2,4608]{2,1,0:T(2,128)}, u32[]{:S(2)}, u32[]{:S(2)}) async-start(f32[16,2,4608]{2,1,0:T(2,128)} %reshape.1072), calls=%async_computation.1 | async-start | bytes 1179648 | tf_op jit(solution)/shard_map/all_to_all | solution.py:574
  54.5 18.9 %collective-permute-start.5 = (bf16[4,24,1920]{2,1,0:T(8,128)(2,1)S(1)}, bf16[4,24,1920]{2,1,0:T(8,128)(2,1)S(1)}, u32[]{:S(2)}, u32[]{:S(2)}) collective-permute-start(bf16[4,24,1920]{2,1,0:T(8,128)(2,1)S(1)} %get-tuple-element.155), channel_id=1, source_target_pairs={{0,1},{1,0},{2,3},{3,2},{4,5},{5,4},{6,7},{7,6},{8,9},{9,8},{10,11... | collective-permute-start | bytes 1105928 | tf_op jit(solution)/shard_map/ppermute | solution.py:53
  55.2 22.1 %collective-permute-start.8 = (bf16[4,24,1920]{2,1,0:T(8,128)(2,1)S(1)}, bf16[4,24,1920]{2,1,0:T(8,128)(2,1)S(1)}, u32[]{:S(2)}, u32[]{:S(2)}) collective-permute-start(bf16[4,24,1920]{2,1,0:T(8,128)(2,1)S(1)} %get-tuple-element.154), channel_id=1, source_target_pairs={{0,4},{4,0},{1,5},{5,1},{2,6},{6,2},{3,7},{7,3},{8,12},{12,8},{9,1... | collective-permute-start | bytes 1105928 | tf_op jit(solution)/shard_map/ppermute | solution.py:53
  74.4 22.6 %collective-permute-start.6 = (bf16[4,2,24,1920]{3,2,0,1:T(8,128)(2,1)}, bf16[4,2,24,1920]{3,2,0,1:T(8,128)(2,1)S(1)}, u32[]{:S(2)}, u32[]{:S(2)}) collective-permute-start(bf16[4,2,24,1920]{3,2,0,1:T(8,128)(2,1)} %maximum_select_fusion.6), channel_id=1, source_target_pairs={{0,4},{4,0},{1,5},{5,1},{2,6},{6,2},{3,7},{7,3},{8,12},{12,8},{9,1... | collective-permute-start | bytes 2211848 | tf_op jit(solution)/shard_map/ppermute | solution.py:53
  82.3 30.0 %collective-permute-start.9 = (bf16[4,2,24,1920]{3,2,0,1:T(8,128)(2,1)S(1)}, bf16[4,2,24,1920]{3,2,0,1:T(8,128)(2,1)S(1)}, u32[]{:S(2)}, u32[]{:S(2)}) collective-permute-start(bf16[4,2,24,1920]{3,2,0,1:T(8,128)(2,1)S(1)} %maximum_select_fusion.8), channel_id=1, source_target_pairs={{0,1},{1,0},{2,3},{3,2},{4,5},{5,4},{6,7},{7,6},{8,9},{9,8},{10,11... | collective-permute-start | bytes 2211848 | tf_op jit(solution)/shard_map/ppermute | solution.py:53
  97.4 16.9 %collective-permute-start.7 = (bf16[4,2,2,24,1920]{4,3,0,1,2:T(8,128)(2,1)S(1)}, bf16[4,2,2,24,1920]{4,3,0,1,2:T(8,128)(2,1)S(1)}, u32[]{:S(2)}, u32[]{:S(2)}) collective-permute-start(bf16[4,2,2,24,1920]{4,3,0,1,2:T(8,128)(2,1)S(1)} %maximum_select_fusion.2), channel_id=1, source_target_pairs={{0,2},{2,0},{1,3},{3,1},{4,6},{6,4},{5,7},{7,5},{8,10},{10,8},{9,1... | collective-permute-start | bytes 4423688 | tf_op jit(solution)/shard_map/ppermute | solution.py:53
  177.7 32.0 %collective-permute-start.15 = (f32[2,3072]{1,0:T(2,128)S(1)}, f32[2,3072]{1,0:T(2,128)S(1)}, u32[]{:S(2)}, u32[]{:S(2)}) collective-permute-start(f32[2,3072]{1,0:T(2,128)S(1)} %pad_maximum_fusion.14), channel_id=1, source_target_pairs={{0,1},{1,0},{2,3},{3,2},{4,5},{5,4},{6,7},{7,6},{8,9},{9,8},{10,11... | collective-permute-start | bytes 73736 | tf_op jit(solution)/shard_map/ppermute | solution.py:53
  183.7 53.9 %collective-permute-start.17 = (bf16[2,4,24,4608]{3,2,1,0:T(8,128)(2,1)}, bf16[2,4,24,4608]{3,2,1,0:T(8,128)(2,1)}, u32[]{:S(2)}, u32[]{:S(2)}) collective-permute-start(bf16[2,4,24,4608]{3,2,1,0:T(8,128)(2,1)} %get-tuple-element.140), channel_id=1, source_target_pairs={{0,1},{1,0},{2,3},{3,2},{4,5},{5,4},{6,7},{7,6},{8,9},{9,8},{10,11... | collective-permute-start | bytes 5308424 | tf_op jit(solution)/shard_map/ppermute | solution.py:53
  187.6 50.0 %collective-permute-start.16 = (bf16[2,4,24,4608]{3,2,1,0:T(8,128)(2,1)}, bf16[2,4,24,4608]{3,2,1,0:T(8,128)(2,1)}, u32[]{:S(2)}, u32[]{:S(2)}) collective-permute-start(bf16[2,4,24,4608]{3,2,1,0:T(8,128)(2,1)} %get-tuple-element.142), channel_id=1, source_target_pairs={{0,4},{4,0},{1,5},{5,1},{2,6},{6,2},{3,7},{7,3},{8,12},{12,8},{9,1... | collective-permute-start | bytes 5308424 | tf_op jit(solution)/shard_map/ppermute | solution.py:53
  210.6 21.5 %all-to-all-start.2 = ((f32[16,2,3072]{2,1,0:T(2,128)}), f32[16,2,3072]{2,1,0:T(2,128)}, u32[]{:S(2)}, u32[]{:S(2)}) async-start(f32[16,2,3072]{2,1,0:T(2,128)} %broadcast_in_dim.25), calls=%async_computation.2 | async-start | bytes 786432 | tf_op jit(solution)/shard_map/all_to_all | solution.py:635
  217.2 34.8 %collective-permute-start.18 = (bf16[4,4,24,1920]{3,2,1,0:T(8,128)(2,1)}, bf16[4,4,24,1920]{3,2,1,0:T(8,128)(2,1)}, u32[]{:S(2)}, u32[]{:S(2)}) collective-permute-start(bf16[4,4,24,1920]{3,2,1,0:T(8,128)(2,1)} %bitcast.286), channel_id=1, source_target_pairs={{0,2},{2,0},{1,3},{3,1},{4,6},{6,4},{5,7},{7,5},{8,10},{10,8},{9,1... | collective-permute-start | bytes 4423688 | tf_op jit(solution)/shard_map/ppermute | solution.py:53
  217.7 37.6 %collective-permute-start.14 = (bf16[4,4,24,1920]{3,2,1,0:T(8,128)(2,1)}, bf16[4,4,24,1920]{3,2,1,0:T(8,128)(2,1)}, u32[]{:S(2)}, u32[]{:S(2)}) collective-permute-start(bf16[4,4,24,1920]{3,2,1,0:T(8,128)(2,1)} %bitcast.285), channel_id=1, source_target_pairs={{0,2},{2,0},{1,3},{3,1},{4,6},{6,4},{5,7},{7,5},{8,10},{10,8},{9,1... | collective-permute-start | bytes 4423688 | tf_op jit(solution)/shard_map/ppermute | solution.py:53
  217.8 43.3 %collective-permute-start.13 = (bf16[2,128,1536]{2,1,0:T(8,128)(2,1)}, bf16[2,128,1536]{2,1,0:T(8,128)(2,1)}, u32[]{:S(2)}, u32[]{:S(2)}) collective-permute-start(bf16[2,128,1536]{2,1,0:T(8,128)(2,1)} %get-tuple-element.90), channel_id=1, source_target_pairs={{0,1},{1,0},{2,3},{3,2},{4,5},{5,4},{6,7},{7,6},{8,9},{9,8},{10,11... | collective-permute-start | bytes 2359304 | tf_op jit(solution)/shard_map/ppermute | solution.py:53
  240.2 28.0 %collective-permute-start.20 = (bf16[4,24,4608]{2,1,0:T(8,128)(2,1)}, bf16[4,24,4608]{2,1,0:T(8,128)(2,1)}, u32[]{:S(2)}, u32[]{:S(2)}) collective-permute-start(bf16[4,24,4608]{2,1,0:T(8,128)(2,1)} %fusion.96), channel_id=1, source_target_pairs={{0,4},{4,0},{1,5},{5,1},{2,6},{6,2},{3,7},{7,3},{8,12},{12,8},{9,1... | collective-permute-start | bytes 2654216 | tf_op jit(solution)/shard_map/ppermute | solution.py:53
  243.2 26.9 %collective-permute-start.19 = (bf16[4,24,4608]{2,1,0:T(8,128)(2,1)}, bf16[4,24,4608]{2,1,0:T(8,128)(2,1)}, u32[]{:S(2)}, u32[]{:S(2)}) collective-permute-start(bf16[4,24,4608]{2,1,0:T(8,128)(2,1)} %fusion.95), channel_id=1, source_target_pairs={{0,1},{1,0},{2,3},{3,2},{4,5},{5,4},{6,7},{7,6},{8,9},{9,8},{10,11... | collective-permute-start | bytes 2654216 | tf_op jit(solution)/shard_map/ppermute | solution.py:53
  255.4 43.8 %collective-permute-start.23 = (bf16[2,4,24,1920]{3,2,1,0:T(8,128)(2,1)}, bf16[2,4,24,1920]{3,2,1,0:T(8,128)(2,1)}, u32[]{:S(2)}, u32[]{:S(2)}) collective-permute-start(bf16[2,4,24,1920]{3,2,1,0:T(8,128)(2,1)} %get-tuple-element.149), channel_id=1, source_target_pairs={{0,4},{4,0},{1,5},{5,1},{2,6},{6,2},{3,7},{7,3},{8,12},{12,8},{9,1... | collective-permute-start | bytes 2211848 | tf_op jit(solution)/shard_map/ppermute | solution.py:53
  259.8 40.0 %collective-permute-start.22 = (bf16[2,4,24,1920]{3,2,1,0:T(8,128)(2,1)}, bf16[2,4,24,1920]{3,2,1,0:T(8,128)(2,1)}, u32[]{:S(2)}, u32[]{:S(2)}) collective-permute-start(bf16[2,4,24,1920]{3,2,1,0:T(8,128)(2,1)} %get-tuple-element.151), channel_id=1, source_target_pairs={{0,1},{1,0},{2,3},{3,2},{4,5},{5,4},{6,7},{7,6},{8,9},{9,8},{10,11... | collective-permute-start | bytes 2211848 | tf_op jit(solution)/shard_map/ppermute | solution.py:53
  266.3 14.5 %collective-permute-start.21 = (f32[2,1536]{1,0:T(2,128)S(1)}, f32[2,1536]{1,0:T(2,128)S(1)}, u32[]{:S(2)}, u32[]{:S(2)}) collective-permute-start(f32[2,1536]{1,0:T(2,128)S(1)} %pad_maximum_fusion.16), channel_id=1, source_target_pairs={{0,1},{1,0},{2,3},{3,2},{4,5},{5,4},{6,7},{7,6},{8,9},{9,8},{10,11... | collective-permute-start | bytes 36872 | tf_op jit(solution)/shard_map/ppermute | solution.py:53
  273.1 68.7 %collective-permute-start.29 = (bf16[24,9216]{1,0:T(8,128)(2,1)}, bf16[24,9216]{1,0:T(8,128)(2,1)S(1)}, u32[]{:S(2)}, u32[]{:S(2)}) collective-permute-start(bf16[24,9216]{1,0:T(8,128)(2,1)} %get-tuple-element.144), channel_id=1, source_target_pairs={{0,8},{8,16},{16,24},{24,0},{1,9},{9,17},{17,25},{25,1},{2,10},{10... | collective-permute-start | bytes 1327112 | tf_op jit(solution)/shard_map/ppermute | solution.py:57
  274.8 67.4 %collective-permute-start.30 = (bf16[24,9216]{1,0:T(8,128)(2,1)}, bf16[24,9216]{1,0:T(8,128)(2,1)}, u32[]{:S(2)}, u32[]{:S(2)}) collective-permute-start(bf16[24,9216]{1,0:T(8,128)(2,1)} %get-tuple-element.145), channel_id=1, source_target_pairs={{0,16},{8,24},{16,0},{24,8},{1,17},{9,25},{17,1},{25,9},{2,18},{10... | collective-permute-start | bytes 1327112 | tf_op jit(solution)/shard_map/ppermute | solution.py:57
  280.7 61.5 %collective-permute-start.31 = (bf16[24,9216]{1,0:T(8,128)(2,1)}, bf16[24,9216]{1,0:T(8,128)(2,1)}, u32[]{:S(2)}, u32[]{:S(2)}) collective-permute-start(bf16[24,9216]{1,0:T(8,128)(2,1)} %get-tuple-element.143), channel_id=1, source_target_pairs={{0,24},{8,0},{16,8},{24,16},{1,25},{9,1},{17,9},{25,17},{2,26},{10... | collective-permute-start | bytes 1327112 | tf_op jit(solution)/shard_map/ppermute | solution.py:57
  300.6 17.4 %all-to-all-start.3 = ((f32[16,2,1536]{2,1,0:T(2,128)}), f32[16,2,1536]{2,1,0:T(2,128)S(1)}, u32[]{:S(2)}, u32[]{:S(2)}) async-start(f32[16,2,1536]{2,1,0:T(2,128)} %broadcast_in_dim.27), calls=%async_computation.3 | async-start | bytes 393216 | tf_op jit(solution)/shard_map/all_to_all | solution.py:635
  307.1 14.5 %collective-permute-start.25 = (bf16[4,24,1920]{2,1,0:T(8,128)(2,1)}, bf16[4,24,1920]{2,1,0:T(8,128)(2,1)}, u32[]{:S(2)}, u32[]{:S(2)}) collective-permute-start(bf16[4,24,1920]{2,1,0:T(8,128)(2,1)} %fusion.138), channel_id=1, source_target_pairs={{0,1},{1,0},{2,3},{3,2},{4,5},{5,4},{6,7},{7,6},{8,9},{9,8},{10,11... | collective-permute-start | bytes 1105928 | tf_op jit(solution)/shard_map/ppermute | solution.py:53
  310.7 12.3 %collective-permute-start.24 = (bf16[4,24,1920]{2,1,0:T(8,128)(2,1)}, bf16[4,24,1920]{2,1,0:T(8,128)(2,1)}, u32[]{:S(2)}, u32[]{:S(2)}) collective-permute-start(bf16[4,24,1920]{2,1,0:T(8,128)(2,1)} %fusion.137), channel_id=1, source_target_pairs={{0,4},{4,0},{1,5},{5,1},{2,6},{6,2},{3,7},{7,3},{8,12},{12,8},{9,1... | collective-permute-start | bytes 1105928 | tf_op jit(solution)/shard_map/ppermute | solution.py:53
  325.2 20.1 %collective-permute-start.26 = (bf16[24,3840]{1,0:T(8,128)(2,1)}, bf16[24,3840]{1,0:T(8,128)(2,1)}, u32[]{:S(2)}, u32[]{:S(2)}) collective-permute-start(bf16[24,3840]{1,0:T(8,128)(2,1)} %get-tuple-element.164), channel_id=1, source_target_pairs={{0,8},{8,16},{16,24},{24,0},{1,9},{9,17},{17,25},{25,1},{2,10},{10... | collective-permute-start | bytes 552968 | tf_op jit(solution)/shard_map/ppermute | solution.py:57
  333.6 12.8 %collective-permute-start.27 = (bf16[24,3840]{1,0:T(8,128)(2,1)}, bf16[24,3840]{1,0:T(8,128)(2,1)}, u32[]{:S(2)}, u32[]{:S(2)}) collective-permute-start(bf16[24,3840]{1,0:T(8,128)(2,1)} %get-tuple-element.165), channel_id=1, source_target_pairs={{0,16},{8,24},{16,0},{24,8},{1,17},{9,25},{17,1},{25,9},{2,18},{10... | collective-permute-start | bytes 552968 | tf_op jit(solution)/shard_map/ppermute | solution.py:57
  (57 other events, 465.6 us)
Sparse Core Ops, SparseCore 0:
  11.5 133.9 all-gather.1

commit v4 on v3

--- a/solution.py
+++ b/solution.py
@@ -154,16 +154,25 @@
     def __init__(self, blocks, nz):
         block = jnp.concatenate(blocks, axis=-1)
         place = lax.axis_index("z")
-        pick = lambda i: lax.dynamic_index_in_dim(block, i, 0, keepdims=False)
-        self.keep = pick(place)
-        self.sent = [pick((place + by) % nz) for by in range(1, nz)]
-        self.got = [shift(sent, "z", nz, by) for by, sent in enumerate(self.sent, 1)]
+        self.nz, self.by = nz, 1
+        pick = lambda m: lax.dynamic_index_in_dim(block, place ^ m, 0, keepdims=False)
+        self.keep = jnp.stack([pick(m) for m in range(0, nz, 2)])
+        self.send(jnp.stack([pick(m) for m in range(1, nz, 2)]))
+
+    def send(self, sent):
+        self.sent = sent
+        self.got = lax.ppermute(sent, "z", [(i, i ^ self.by) for i in range(self.nz)])
+
+    def next(self):
+        while self.by * 2 < self.nz:
+            self.by *= 2
+            total = add_low(self.keep, self.got)
+            self.keep = total[::2]
+            self.send(total[1::2])
 
     def total(self, *needed):
-        total = self.keep.astype(F32)
-        for got in after(self.got, *needed):
-            total = total + got.astype(F32)
-        return total
+        got = after(self.got, *needed)
+        return (self.keep.astype(F32) + got.astype(F32))[0]
 
 
 def bias_kernel(pair_ref, wide_ref, out_ref):
@@ -194,21 +203,35 @@
     )(pair, wide)
 
 
+def widen(ref, mask):
+    heads, tiles = mask.shape[0] // TILE, ref.shape[0] // TILE
+    return jnp.concatenate(
+        [jnp.concatenate([ref[n * TILE : (n + 1) * TILE, :]] * heads, axis=0) * mask for n in range(tiles)], axis=0
+    )
+
+
+def narrow(mixed, mask):
+    tall = mask.shape[0]
+    mask = mask.astype(F32)
+    rows = []
+    for n in range(mixed.shape[0] // tall):
+        own = mixed[n * tall : (n + 1) * tall] * mask
+        total = own[:TILE]
+        for h in range(1, tall // TILE):
+            total = total + own[h * TILE : (h + 1) * TILE]
+        rows.append(total)
+    return jnp.concatenate(rows, axis=0)
+
+
 def attend_kernel(factor, bias_ref, q_ref, k_ref, v_ref, mask_ref, probs_ref, out_ref):
-    heads = mask_ref.shape[0] // TILE
-    keys, values, mask = k_ref[0], v_ref[0], mask_ref[...]
-    for n in range(bias_ref.shape[1]):
-        at = pl.ds(n * TILE, TILE)
-        wide = jnp.concatenate([q_ref[at, :]] * heads, axis=0) * mask
-        scores = dot(wide, keys, NT) * factor + bias_ref[0, n]
-        powers = jnp.exp(scores - jnp.max(scores, axis=-1, keepdims=True))
-        probs = powers * (1.0 / jnp.sum(powers, axis=-1, keepdims=True))
-        probs_ref[0, n] = probs
-        mixed = dot(probs.astype(BF16), values) * mask.astype(F32)
-        total = mixed[:TILE]
-        for h in range(1, heads):
-            total = total + mixed[h * TILE : (h + 1) * TILE]
-        out_ref[at, :] = total
+    mask = mask_ref[...]
+    shape = bias_ref.shape[1:]
+    bias = bias_ref[0].reshape(-1, shape[-1])
+    scores = dot(widen(q_ref, mask), k_ref[0], NT) * factor + bias
+    powers = jnp.exp(scores - jnp.max(scores, axis=-1, keepdims=True))
+    probs = powers * (1.0 / jnp.sum(powers, axis=-1, keepdims=True))
+    probs_ref[0] = probs.reshape(shape)
+    out_ref[...] = narrow(dot(probs.astype(BF16), v_ref[0]), mask)
 
 
 def attend(bias, queries, keys, values, mask, factor, group=4):
@@ -238,7 +261,6 @@
 
 def attend_back_kernel(factor, place_ref, probs_ref, q_ref, g_ref, k_ref, v_ref, mask_ref, ds_ref, dq_ref, dk_ref, dv_ref,
                        keep_ref, give_ref, dk_sum, dv_sum):
-    heads = mask_ref.shape[0] // TILE
     keys, values, mask = k_ref[0], v_ref[0], mask_ref[...]
 
     @pl.when(pl.program_id(1) == 0)
@@ -246,22 +268,16 @@
         dk_sum[...] = jnp.zeros_like(dk_sum)
         dv_sum[...] = jnp.zeros_like(dv_sum)
 
-    for n in range(probs_ref.shape[1]):
-        at = pl.ds(n * TILE, TILE)
-        probs = probs_ref[0, n]
-        queries = jnp.concatenate([q_ref[at, :]] * heads, axis=0) * mask
-        grads = jnp.concatenate([g_ref[at, :]] * heads, axis=0) * mask
-        probs_grad = dot(grads, values, NT)
-        inner = jnp.sum(probs_grad * probs, axis=-1, keepdims=True)
-        scores_grad = (probs * (probs_grad - inner)).astype(BF16)
-        ds_ref[0, n] = scores_grad
-        mixed = dot(scores_grad, keys) * mask.astype(F32)
-        total = mixed[:TILE]
-        for h in range(1, heads):
-            total = total + mixed[h * TILE : (h + 1) * TILE]
-        dq_ref[at, :] = (total * factor).astype(BF16)
-        dk_sum[...] += dot(scores_grad, queries, TN)
-        dv_sum[...] += dot(probs.astype(BF16), grads, TN)
+    shape = probs_ref.shape[1:]
+    probs = probs_ref[0].reshape(-1, shape[-1])
+    queries, grads = widen(q_ref, mask), widen(g_ref, mask)
+    probs_grad = dot(grads, values, NT)
+    inner = jnp.sum(probs_grad * probs, axis=-1, keepdims=True)
+    scores_grad = (probs * (probs_grad - inner)).astype(BF16)
+    ds_ref[0] = scores_grad.reshape(shape)
+    dq_ref[...] = (narrow(dot(scores_grad, keys), mask) * factor).astype(BF16)
+    dk_sum[...] += dot(scores_grad, queries, TN)
+    dv_sum[...] += dot(probs.astype(BF16), grads, TN)
 
     @pl.when(pl.program_id(1) == pl.num_programs(1) - 1)
     def _():
@@ -674,7 +690,8 @@
     for s in feed_sums:
         s.got = after(s.got, pair_sums[0])
         s.second()
-    pair_sums = more_pair(quarter, quarter, late_modes, *[s.give for s in feed_sums])
+    pair_sums = more_pair(quarter, quarter, *[s.give for s in feed_sums])
+    late_modes = after(late_modes, pair_sums[0])
     for s in in_sums:
         s.got = after(s.got, pair_sums[0])
         s.first()
@@ -691,13 +708,19 @@
     for s in feed_sums:
         s.got = after(s.got, normed_one_grad)
     feed_line = Line([s.third() for s in feed_sums], nz)
-    early_modes = share_modes(*early_halves, *feed_line.sent)
-    pair_sums = more_pair(2 * quarter, steps_all - 2 * quarter, *feed_line.sent, *early_halves)
+    early_modes = share_modes(*early_halves, feed_line.sent)
+    for s in in_sums:
+        s.got = after(s.got, feed_line.sent)
+        s.second()
+    pair_sums = more_pair(2 * quarter, quarter, feed_line.sent, *early_halves, *[s.give for s in in_sums])
+    feed_line.got = after(feed_line.got, pair_sums[0])
+    feed_line.next()
+    for s in in_sums:
+        s.got = after(s.got, feed_line.sent)
+    in_line = Line([s.third() for s in in_sums], nz)
+    pair_sums = more_pair(3 * quarter, steps_all - 3 * quarter, in_line.sent)
     tokens_grad = (middle_grad + normalise_back(normed_one_grad, scale_one, norm_one, root_one)).astype(BF16)
-    for s in in_sums:
-        s.got = after(s.got, pair_sums[0])
-        s.second()
-    early_modes = after(early_modes, *[s.give for s in in_sums]).reshape(ndp * chains, -1)
+    early_modes = after(early_modes, pair_sums[0]).reshape(ndp * chains, -1)
     late_modes = late_modes.reshape(ndp * chains, -1)
     pair_w_sum, pair_grad = pair_sums
     grad_pair_w = pair_w_sum[:heads].T
@@ -714,16 +737,17 @@
         [outer(features).reshape(devices, time_rows * own), grad_pair_w.reshape(devices, -1)], axis=1
     )
     time_got = lax.all_to_all(time_pack, ALL, split_axis=0, concat_axis=0, tiled=True)
-    for r in in_sums:
-        r.got = after(r.got, time_pack)
-    in_line = Line([r.third() for r in in_sums], nz)
-    feed_total = feed_line.total(time_pack, *in_line.sent)
+    in_line.got = after(in_line.got, time_pack)
+    in_line.next()
+    feed_total = feed_line.total(in_line.sent)
     early, late = jnp.split(feed_total, 2, axis=1)
     sum_gate, sum_up = early[:, :hidden_width], late[:, :hidden_width]
     sum_down = jnp.concatenate(
         [t[:, hidden_width + k * width : hidden_width + (k + 1) * width] for t in (early, late) for k in range(groups // 2)], axis=0
     )
-    sums = jnp.split(in_line.total(), 2, axis=1)
+    in_total = in_line.total(feed_total)
+    time_got = after(time_got, in_total)
+    sums = jnp.split(in_total, 2, axis=1)
     sum_out = jnp.concatenate([s[:, 2 * width :] for s in sums], axis=1)
     grad_time = time_got[:, :size_time].reshape(devices, time_rows, own).transpose(1, 0, 2).reshape(time_rows, width)
     grad_pair_own = jnp.sum(time_got[:, size_time:], axis=0).reshape(w_pair.shape)

time: 365 us -> 357 us (0.978)
  starting transfers between devices: 66 us -> 57.5 us
  Pallas kernels: 118 us -> 112 us
  waiting for transfers between devices: 56.9 us -> 62.4 us
    ppermute x9 -> x3, starting transfers between devices: 18.1 us -> 6.09 us  [shift(): lax.ppermute(value, axis, [(i, (i + by) % size) for i in range(size)])]
    ppermute x23, waiting for transfers between devices: 28.9 us -> 37.8 us  [swap(): return lax.ppermute(value, axis, [(0, 1), (1, 0)])]
    ppermute x0 -> x4, waiting for transfers between devices: none -> 8.14 us  [send(): lax.ppermute(sent, 'z', [(i, i ^ self.by) for i in range(self.nz)])]
    all_to_all x2, waiting for transfers between devices: 6.73 us -> 0.01 us  [share_modes(): return lax.all_to_all(mine, DP, split_axis=0, concat_axis=0, tiled=True)]
    ppermute x0 -> x4, starting transfers between devices: none -> 6.36 us  [send(): lax.ppermute(sent, 'z', [(i, i ^ self.by) for i in range(self.nz)])]
    convert_element_type x13 -> x15, other arithmetic: 27.9 us -> 33.3 us  [add_low(): return (left.astype(F32) + right.astype(F32)).astype(BF16)]
    ppermute x9 -> x3, waiting for transfers between devices: 4.62 us -> 0.01 us  [shift(): lax.ppermute(value, axis, [(i, (i + by) % size) for i in range(size)])]
    pallas_call x1, Pallas kernels: 15.8 us -> 12.1 us  [attend_back(): pl.pallas_call(functools.partial(attend_back_kernel, factor), grid=(chain...]
  transfers between devices with their start and end apart: 38 -> 36, of which waited for: 13 -> 9; matrix products, arithmetic and copies ran while one was open for 27% -> 27% of each run, Pallas kernels for 25% -> 24%
where the time goes in v4:
time: 357 us; the launch traced here: 352 us
  Pallas kernels  112 us (31%)
  other arithmetic  67.3 us (19%)
  waiting for transfers between devices  62.4 us (17%)
  starting transfers between devices  57.5 us (16%)
  local copies, waits for them, and re-layouts  21 us (6%)
  matrix products  16.4 us (5%)
  between operations  15.5 us (4%)
    ppermute x23, waiting for transfers between devices, swap(): return lax.ppermute(value, axis, [(0, 1), (1, 0)])  37.8 us
    convert_element_type x15, other arithmetic, add_low(): return (left.astype(F32) + right.astype(F32)).astype(BF16)  33.3 us
    pallas_call x4, Pallas kernels, pair_back(): pl.pallas_call(pair_back_kernel, grid=(count,), in_specs=[pl.BlockSpec((1...  32.5 us
    pallas_call x1, Pallas kernels, feed(): pl.pallas_call(functools.partial(feed_kernel, steps), grid=(steps + group...  26.8 us
    ppermute x23, starting transfers between devices, swap(): return lax.ppermute(value, axis, [(0, 1), (1, 0)])  21 us
    pallas_call x1, Pallas kernels, pair_bias(): pl.pallas_call(bias_kernel, grid=(chains, blocks // group), in_specs=[pl....  15.8 us
    pallas_call x1, Pallas kernels, attend_back(): pl.pallas_call(functools.partial(attend_back_kernel, factor), grid=(chain...  12.1 us
    dot_general x19, matrix products, dot(): lax.dot_general(left, right, (dims, ((), ())), preferred_element_type=F32)  11.9 us
  transfers between devices with their start and end apart: 36, of which 9 were waited for; matrix products, arithmetic and copies ran while one was open for 27% of the time, Pallas kernels for 24%

profile of v4, /device:TPU:0, one launch (start us, length us, event | category | flops | bytes accessed | tf_op | source)
XLA Modules:
  0.0 352.3 jit_solution(12464047000652504594)
XLA Ops:
  10.8 5.0 %collective-permute-start.1 = (bf16[24,3840]{1,0:T(8,128)(2,1)}, bf16[24,3840]{1,0:T(8,128)(2,1)S(1)}, u32[]{:S(2)}, u32[]{:S(2)}) collective-permute-start(bf16[24,3840]{1,0:T(8,128)(2,1)} %join.2), channel_id=1, source_target_pairs={{0,24},{8,0},{16,8},{24,16},{1,25},{9,1},{17,9},{25,17},{2,26},{10... | collective-permute-start | bytes 552968 | tf_op jit(solution)/shard_map/ppermute | solution.py:57
  20.9 5.0 %all-to-all-start = ((f32[32,1,296]{2,1,0:T(1,128)}), f32[32,1,296]{2,1,0:T(1,128)S(1)}, u32[]{:S(2)}, u32[]{:S(2)}) async-start(f32[32,1,296]{2,1,0:T(1,128)} %copy.90), calls=%async_computation | async-start | bytes 98304 | tf_op jit(solution)/shard_map/all_to_all | solution.py:573
  31.9 10.8 %all-to-all-done = f32[32,1,296]{2,1,0:T(1,128)S(1)} async-done(((f32[32,1,296]{2,1,0:T(1,128)}), f32[32,1,296]{2,1,0:T(1,128)S(1)}, u32[]{:S(2)}, u32[]{:S(2)}) %all-to-all-start) | async-done | bytes 37920 | tf_op jit(solution)/shard_map/all_to_all | solution.py:573
  47.6 6.8 %all-to-all-start.1 = ((f32[16,2,4608]{2,1,0:T(2,128)}), f32[16,2,4608]{2,1,0:T(2,128)}, u32[]{:S(2)}, u32[]{:S(2)}) async-start(f32[16,2,4608]{2,1,0:T(2,128)} %reshape.1068), calls=%async_computation.1 | async-start | bytes 1179648 | tf_op jit(solution)/shard_map/all_to_all | solution.py:590
  57.5 15.8 %pair_bias.1.bias_ref = f32[2,8,192,256]{3,2,1,0:T(8,128)} custom-call(bf16[2,128,256,256]{3,2,1,0:T(8,128)(2,1)} %pair_ref.8, bf16[256,192]{1,0:T(8,128)(2,1)} %copy.99.wide_ref), custom_call_target="tpu_custom_call" | custom-call | flops 6442450944 | bytes 33554432 | tf_op jit(solution)/shard_map/pair_bias/pallas_call | solution.py:191
  73.6 3.5 collective-permute-done.8
  85.1 21.0 %collective-permute-done = f32[2,4608]{1,0:T(2,128)S(1)} collective-permute-done((f32[2,4608]{1,0:T(2,128)S(1)}, f32[2,4608]{1,0:T(2,128)S(1)}, u32[]{:S(2)}, u32[]{:S(2)}) %collective-permute-start) | collective-permute-done | bytes 36896 | tf_op jit(solution)/shard_map/ppermute | solution.py:53
  112.3 4.7 %collective-permute-done.6 = bf16[4,2,24,1920]{3,2,0,1:T(8,128)(2,1)S(1)} collective-permute-done((bf16[4,2,24,1920]{3,2,0,1:T(8,128)(2,1)S(1)}, bf16[4,2,24,1920]{3,2,0,1:T(8,128)(2,1)S(1)}, u32[]{:S(2)}, u32[]{:S(2)}) %collective-permute-start.6) | collective-permute-done | bytes 737312 | tf_op jit(solution)/shard_map/ppermute | solution.py:53
  123.8 6.3 %project.1 = (bf16[256,768]{1,0:T(8,128)(2,1)}, bf16[512,768]{1,0:T(8,128)(2,1)}, bf16[512,768]{1,0:T(8,128)(2,1)}, f32[256,768]{1,0:T(8,128)}) custom-call(bf16[256,768]{1,0:T(8,128)(2,1)} %bitcast.226, bf16[512,768]{1,0:T(8,128)(2,1)} %bitcast.235, bf16[768,1920]{1,0:T(8,128)(2,1)} %bitcast.207, bf16[768,1920]{1,0:T(8,128)(2,1)} %bitcast.203), custom_call_target="tpu_custom_call" | custom-call | flops 1811939328 | bytes 7077888 | tf_op jit(solution)/shard_map/project/pallas_call | solution.py:496
  130.0 8.9 %attend.1 = (f32[2,8,192,256]{3,2,1,0:T(8,128)}, f32[256,768]{1,0:T(8,128)}) custom-call(f32[2,8,192,256]{3,2,1,0:T(8,128)} %pair_bias.1.bias_ref, bf16[256,768]{1,0:T(8,128)(2,1)} %get-tuple-element.77.q_ref, bf16[2,256,768]{2,1,0:T(8,128)(2,1)} %bitcast.270, bf16[2,256,768]{2,1,0:T(8,128)(2,1)} %bitcast.272, bf16[192,768]{1,0:T(8,128)(2,1)} %compare_convert_fusion.mask_ref), custom_call_target="tpu_custom_call" | custom-call | flops 2415919104 | bytes 7864320 | tf_op jit(solution)/shard_map/attend/pallas_call | solution.py:244
  146.1 26.8 %feed.1 = (f32[256,768]{1,0:T(8,128)}, f32[256,768]{1,0:T(8,128)}, bf16[4,4,24,4608]{3,2,1,0:T(8,128)(2,1)}, bf16[4,4,24,4608]{3,2,1,0:T(8,128)(2,1)}, bf16[4,4,...) custom-call(bf16[256,768]{1,0:T(8,128)(2,1)} %bitcast.256, bf16[2,768,256]{2,1,0:T(8,128)(2,1)} %pad_maximum_fusion.5.turned_ref, ...), custom_call_target="tpu_custom_call" | custom-call | flops 14495514624 | bytes 28311552 | tf_op jit(solution)/shard_map/feed/pallas_call | solution.py:437
  181.9 4.8 %add_convert_fusion = (bf16[2,4,24,4608]{3,2,1,0:T(8,128)(2,1)}, bf16[2,4,24,4608]{3,2,1,0:T(8,128)(2,1)}) fusion(bf16[4,4,24,4608]{3,2,1,0:T(8,128)(2,1)} %collective-permute-done.12, bf16[4,4,24,4608]{3,2,1,0:T(8,128)(2,1)S(1)} %copy-done.16), kind=kLoop, calls=%fused_computation | loop fusion | flops 7077888 | bytes 10616832 | tf_op jit(solution)/shard_map/convert_element_type | solution.py:61
  187.4 4.7 %add_convert_fusion.1 = (bf16[2,4,24,4608]{3,2,1,0:T(8,128)(2,1)}, bf16[2,4,24,4608]{3,2,1,0:T(8,128)(2,1)}) fusion(bf16[4,4,24,4608]{3,2,1,0:T(8,128)(2,1)} %collective-permute-done.11, bf16[4,4,24,4608]{3,2,1,0:T(8,128)(2,1)S(1)} %copy-done.15), kind=kLoop, calls=%fused_computation.1 | loop fusion | flops 7077888 | bytes 10616832 | tf_op jit(solution)/shard_map/convert_element_type | solution.py:61
  193.7 12.1 %attend_back.1 = (bf16[2,8,192,256]{3,2,1,0:T(8,128)(2,1)}, bf16[256,768]{1,0:T(8,128)(2,1)}, bf16[2,256,768]{2,1,0:T(8,128)(2,1)}, bf16[2,256,768]{2,1,0:T(8,12...) custom-call(s32[1]{0:T(128)} %bitcast.56.place_ref, ...), custom_call_target="tpu_custom_call" | custom-call | flops 6039797760 | bytes 4718592 | tf_op jit(solution)/shard_map/attend_back/pallas_call | solution.py:300
  205.8 6.4 %project_back.1 = (bf16[192,1920]{1,0:T(8,128)(2,1)}, bf16[192,1920]{1,0:T(8,128)(2,1)}, bf16[384,1920]{1,0:T(8,128)(2,1)}, bf16[192,1920]{1,0:T(8,128)(2,1)}, b...) custom-call(bf16[2,768,256]{2,1,0:T(8,128)(2,1)} %pad_maximum_fusion.7.own_ref, ...), custom_call_target="tpu_custom_call" | custom-call | flops 4831838208 | bytes 9437184 | tf_op jit(solution)/shard_map/project_back/pallas_call | solution.py:523
  214.8 4.7 %all-to-all-start.3 = ((f32[16,2,3072]{2,1,0:T(2,128)}), f32[16,2,3072]{2,1,0:T(2,128)}, u32[]{:S(2)}, u32[]{:S(2)}) async-start(f32[16,2,3072]{2,1,0:T(2,128)} %broadcast_in_dim.27), calls=%async_computation.3 | async-start | bytes 786432 | tf_op jit(solution)/shard_map/all_to_all | solution.py:651
  219.6 2.4 fusion.76
  222.6 8.1 %pair_back.4 = (bf16[2,128,256,256]{3,2,1,0:T(8,128)(2,1)}, f32[16,256]{1,0:T(8,128)}) custom-call(bf16[2,8,192,256]{3,2,1,0:T(8,128)(2,1)} %get-tuple-element.123.ds_ref, bf16[2,128,256,256]{3,2,1,0:T(8,128)(2,1)} %pair_ref.8, bf16[192,256]{1,0:T(8,128)(2,1)} %bitcast.219, bf16[256,192]{1,0:T(8,128)(2,1)} %and_convert_fusion.turn_ref, ...), custom_call_target="tpu_custom_call" | custom-call | flops 3221225472 | bytes 16777216 | tf_op jit(solution)/shard_map/pair_back/pallas_call | solution.py:357
  230.7 5.6 %collective-permute-done.15 = bf16[2,4,24,4608]{3,2,1,0:T(8,128)(2,1)} collective-permute-done((bf16[2,4,24,4608]{3,2,1,0:T(8,128)(2,1)}, bf16[2,4,24,4608]{3,2,1,0:T(8,128)(2,1)}, u32[]{:S(2)}, u32[]{:S(2)}) %collective-permute-start.15) | collective-permute-done | bytes 1769504 | tf_op jit(solution)/shard_map/ppermute | solution.py:53
  236.3 2.6 fusion.96
  240.6 2.3 fusion.95
  244.1 8.1 %pair_back.5 = (bf16[2,128,256,256]{3,2,1,0:T(8,128)(2,1)}, f32[16,256]{1,0:T(8,128)}) custom-call(bf16[2,8,192,256]{3,2,1,0:T(8,128)(2,1)} %get-tuple-element.123.ds_ref, bf16[2,128,256,256]{3,2,1,0:T(8,128)(2,1)} %pair_ref.8, bf16[192,256]{1,0:T(8,128)(2,1)} %bitcast.220, ...), custom_call_target="tpu_custom_call", output_to_operand_aliasing={{0}: (5, {})} | custom-call | flops 3221225472 | bytes 16777216 | tf_op jit(solution)/shard_map/pair_back/pallas_call | solution.py:357
  252.2 3.4 fusion.22
  256.1 3.0 add_convert_fusion.10
  276.3 2.9 collective-permute-done.18
  286.0 4.6 %all-to-all-start.2 = ((f32[16,2,1536]{2,1,0:T(2,128)}), f32[16,2,1536]{2,1,0:T(2,128)S(1)}, u32[]{:S(2)}, u32[]{:S(2)}) async-start(f32[16,2,1536]{2,1,0:T(2,128)} %broadcast_in_dim.26), calls=%async_computation.2 | async-start | bytes 393216 | tf_op jit(solution)/shard_map/all_to_all | solution.py:651
  290.6 8.2 %pair_back.6 = (bf16[2,128,256,256]{3,2,1,0:T(8,128)(2,1)}, f32[16,256]{1,0:T(8,128)}) custom-call(bf16[2,8,192,256]{3,2,1,0:T(8,128)(2,1)} %get-tuple-element.123.ds_ref, bf16[2,128,256,256]{3,2,1,0:T(8,128)(2,1)} %pair_ref.8, bf16[192,256]{1,0:T(8,128)(2,1)} %bitcast.221, ...), custom_call_target="tpu_custom_call", output_to_operand_aliasing={{0}: (5, {})} | custom-call | flops 3221225472 | bytes 16777216 | tf_op jit(solution)/shard_map/pair_back/pallas_call | solution.py:357
  301.0 2.9 collective-permute-start.29
  308.1 8.1 %pair_back.7 = (bf16[2,128,256,256]{3,2,1,0:T(8,128)(2,1)}, f32[16,256]{1,0:T(8,128)}) custom-call(bf16[2,8,192,256]{3,2,1,0:T(8,128)(2,1)} %get-tuple-element.123.ds_ref, bf16[2,128,256,256]{3,2,1,0:T(8,128)(2,1)} %pair_ref.8, bf16[192,256]{1,0:T(8,128)(2,1)} %bitcast.222, ...), custom_call_target="tpu_custom_call", output_to_operand_aliasing={{0}: (5, {})} | custom-call | flops 3221225472 | bytes 16777216 | tf_op jit(solution)/shard_map/pair_back/pallas_call | solution.py:357
  319.9 2.8 all-to-all-start.4
  325.1 5.0 %all-to-all-done.4 = f32[32,1,288]{2,1,0:T(1,128)S(1)} async-done(((f32[32,1,288]{2,1,0:T(1,128)}), f32[32,1,288]{2,1,0:T(1,128)S(1)}, u32[]{:S(2)}, u32[]{:S(2)}) %all-to-all-start.4) | async-done | bytes 36896 | tf_op jit(solution)/shard_map/all_to_all | solution.py:739
  333.3 8.1 %collective-permute-done.28 = bf16[1,24,3840]{2,1,0:T(8,128)(2,1)S(1)} collective-permute-done((bf16[1,24,3840]{2,1,0:T(8,128)(2,1)S(1)}, bf16[1,24,3840]{2,1,0:T(8,128)(2,1)S(1)}, u32[]{:S(2)}, u32[]{:S(2)}) %collective-permute-start.28) | collective-permute-done | bytes 184352 | tf_op jit(solution)/shard_map/ppermute | solution.py:164
  (357 shorter events, 111.2 us)
Async XLA Ops:
  7.2 138.9 %all-gather.2.cloned.1.call-start = ((), (), s32[]{:S(2)}) async-start(), calls=%async_computation.5 | async-start | bytes 14598144 | tf_op jit(solution)/shard_map/all_gather | solution.py:555
  10.8 43.6 %collective-permute-start.1 = (bf16[24,3840]{1,0:T(8,128)(2,1)}, bf16[24,3840]{1,0:T(8,128)(2,1)S(1)}, u32[]{:S(2)}, u32[]{:S(2)}) collective-permute-start(bf16[24,3840]{1,0:T(8,128)(2,1)} %join.2), channel_id=1, source_target_pairs={{0,24},{8,0},{16,8},{24,16},{1,25},{9,1},{17,9},{25,17},{2,26},{10... | collective-permute-start | bytes 552968 | tf_op jit(solution)/shard_map/ppermute | solution.py:57
  15.9 38.6 %collective-permute-start.2 = (bf16[24,3840]{1,0:T(8,128)(2,1)}, bf16[24,3840]{1,0:T(8,128)(2,1)S(1)}, u32[]{:S(2)}, u32[]{:S(2)}) collective-permute-start(bf16[24,3840]{1,0:T(8,128)(2,1)} %join.2), channel_id=1, source_target_pairs={{0,16},{8,24},{16,0},{24,8},{1,17},{9,25},{17,1},{25,9},{2,18},{10... | collective-permute-start | bytes 552968 | tf_op jit(solution)/shard_map/ppermute | solution.py:57
  15.9 38.6 %collective-permute-start.3 = (bf16[24,3840]{1,0:T(8,128)(2,1)}, bf16[24,3840]{1,0:T(8,128)(2,1)S(1)}, u32[]{:S(2)}, u32[]{:S(2)}) collective-permute-start(bf16[24,3840]{1,0:T(8,128)(2,1)} %join.2), channel_id=1, source_target_pairs={{0,8},{8,16},{16,24},{24,0},{1,9},{9,17},{17,25},{25,1},{2,10},{10... | collective-permute-start | bytes 552968 | tf_op jit(solution)/shard_map/ppermute | solution.py:57
  20.9 21.7 %all-to-all-start = ((f32[32,1,296]{2,1,0:T(1,128)}), f32[32,1,296]{2,1,0:T(1,128)S(1)}, u32[]{:S(2)}, u32[]{:S(2)}) async-start(f32[32,1,296]{2,1,0:T(1,128)} %copy.90), calls=%async_computation | async-start | bytes 98304 | tf_op jit(solution)/shard_map/all_to_all | solution.py:573
  26.0 47.3 %collective-permute-start.4 = (bf16[2,128,768]{2,1,0:T(8,128)(2,1)S(1)}, bf16[2,128,768]{2,1,0:T(8,128)(2,1)S(1)}, u32[]{:S(2)}, u32[]{:S(2)}) collective-permute-start(bf16[2,128,768]{2,1,0:T(8,128)(2,1)S(1)} %copy-done.6), channel_id=1, source_target_pairs={{0,1},{1,0},{2,3},{3,2},{4,5},{5,4},{6,7},{7,6},{8,9},{9,8},{10,11... | collective-permute-start | bytes 1179656 | tf_op jit(solution)/shard_map/ppermute | solution.py:53
  47.6 35.1 %all-to-all-start.1 = ((f32[16,2,4608]{2,1,0:T(2,128)}), f32[16,2,4608]{2,1,0:T(2,128)}, u32[]{:S(2)}, u32[]{:S(2)}) async-start(f32[16,2,4608]{2,1,0:T(2,128)} %reshape.1068), calls=%async_computation.1 | async-start | bytes 1179648 | tf_op jit(solution)/shard_map/all_to_all | solution.py:590
  54.7 22.4 %collective-permute-start.8 = (bf16[4,24,1920]{2,1,0:T(8,128)(2,1)S(1)}, bf16[4,24,1920]{2,1,0:T(8,128)(2,1)S(1)}, u32[]{:S(2)}, u32[]{:S(2)}) collective-permute-start(bf16[4,24,1920]{2,1,0:T(8,128)(2,1)S(1)} %get-tuple-element.161), channel_id=1, source_target_pairs={{0,4},{4,0},{1,5},{5,1},{2,6},{6,2},{3,7},{7,3},{8,12},{12,8},{9,1... | collective-permute-start | bytes 1105928 | tf_op jit(solution)/shard_map/ppermute | solution.py:53
  56.8 22.8 %collective-permute-start.5 = (bf16[4,24,1920]{2,1,0:T(8,128)(2,1)S(1)}, bf16[4,24,1920]{2,1,0:T(8,128)(2,1)S(1)}, u32[]{:S(2)}, u32[]{:S(2)}) collective-permute-start(bf16[4,24,1920]{2,1,0:T(8,128)(2,1)S(1)} %get-tuple-element.162), channel_id=1, source_target_pairs={{0,1},{1,0},{2,3},{3,2},{4,5},{5,4},{6,7},{7,6},{8,9},{9,8},{10,11... | collective-permute-start | bytes 1105928 | tf_op jit(solution)/shard_map/ppermute | solution.py:53
  78.1 33.9 %collective-permute-start.9 = (bf16[4,2,24,1920]{3,2,0,1:T(8,128)(2,1)}, bf16[4,2,24,1920]{3,2,0,1:T(8,128)(2,1)S(1)}, u32[]{:S(2)}, u32[]{:S(2)}) collective-permute-start(bf16[4,2,24,1920]{3,2,0,1:T(8,128)(2,1)} %maximum_select_fusion.8), channel_id=1, source_target_pairs={{0,1},{1,0},{2,3},{3,2},{4,5},{5,4},{6,7},{7,6},{8,9},{9,8},{10,11... | collective-permute-start | bytes 2211848 | tf_op jit(solution)/shard_map/ppermute | solution.py:53
  84.0 22.2 %collective-permute-start = (f32[2,4608]{1,0:T(2,128)S(1)}, f32[2,4608]{1,0:T(2,128)S(1)}, u32[]{:S(2)}, u32[]{:S(2)}) collective-permute-start(f32[2,4608]{1,0:T(2,128)S(1)} %reduce_sum.162), channel_id=1, source_target_pairs={{0,1},{1,0},{2,3},{3,2},{4,5},{5,4},{6,7},{7,6},{8,9},{9,8},{10,11... | collective-permute-start | bytes 110600 | tf_op jit(solution)/shard_map/ppermute | solution.py:53
  84.8 32.3 %collective-permute-start.6 = (bf16[4,2,24,1920]{3,2,0,1:T(8,128)(2,1)S(1)}, bf16[4,2,24,1920]{3,2,0,1:T(8,128)(2,1)S(1)}, u32[]{:S(2)}, u32[]{:S(2)}) collective-permute-start(bf16[4,2,24,1920]{3,2,0,1:T(8,128)(2,1)S(1)} %maximum_select_fusion.6), channel_id=1, source_target_pairs={{0,4},{4,0},{1,5},{5,1},{2,6},{6,2},{3,7},{7,3},{8,12},{12,8},{9,1... | collective-permute-start | bytes 2211848 | tf_op jit(solution)/shard_map/ppermute | solution.py:53
  173.3 14.2 %collective-permute-start.11 = (bf16[4,4,24,4608]{3,2,1,0:T(8,128)(2,1)}, bf16[4,4,24,4608]{3,2,1,0:T(8,128)(2,1)}, u32[]{:S(2)}, u32[]{:S(2)}) collective-permute-start(bf16[4,4,24,4608]{3,2,1,0:T(8,128)(2,1)} %get-tuple-element.87), channel_id=1, source_target_pairs={{0,2},{2,0},{1,3},{3,1},{4,6},{6,4},{5,7},{7,5},{8,10},{10,8},{9,1... | collective-permute-start | bytes 10616840 | tf_op jit(solution)/shard_map/ppermute | solution.py:53
  178.0 34.7 %collective-permute-start.26 = (f32[2,3072]{1,0:T(2,128)S(1)}, f32[2,3072]{1,0:T(2,128)S(1)}, u32[]{:S(2)}, u32[]{:S(2)}) collective-permute-start(f32[2,3072]{1,0:T(2,128)S(1)} %pad_maximum_fusion.16), channel_id=1, source_target_pairs={{0,1},{1,0},{2,3},{3,2},{4,5},{5,4},{6,7},{7,6},{8,9},{9,8},{10,11... | collective-permute-start | bytes 73736 | tf_op jit(solution)/shard_map/ppermute | solution.py:53
  186.7 44.0 %collective-permute-start.16 = (bf16[2,4,24,4608]{3,2,1,0:T(8,128)(2,1)}, bf16[2,4,24,4608]{3,2,1,0:T(8,128)(2,1)}, u32[]{:S(2)}, u32[]{:S(2)}) collective-permute-start(bf16[2,4,24,4608]{3,2,1,0:T(8,128)(2,1)} %get-tuple-element.146), channel_id=1, source_target_pairs={{0,1},{1,0},{2,3},{3,2},{4,5},{5,4},{6,7},{7,6},{8,9},{9,8},{10,11... | collective-permute-start | bytes 5308424 | tf_op jit(solution)/shard_map/ppermute | solution.py:53
  192.1 44.2 %collective-permute-start.15 = (bf16[2,4,24,4608]{3,2,1,0:T(8,128)(2,1)}, bf16[2,4,24,4608]{3,2,1,0:T(8,128)(2,1)}, u32[]{:S(2)}, u32[]{:S(2)}) collective-permute-start(bf16[2,4,24,4608]{3,2,1,0:T(8,128)(2,1)} %get-tuple-element.148), channel_id=1, source_target_pairs={{0,4},{4,0},{1,5},{5,1},{2,6},{6,2},{3,7},{7,3},{8,12},{12,8},{9,1... | collective-permute-start | bytes 5308424 | tf_op jit(solution)/shard_map/ppermute | solution.py:53
  212.2 40.0 %collective-permute-start.17 = (bf16[4,4,24,1920]{3,2,1,0:T(8,128)(2,1)}, bf16[4,4,24,1920]{3,2,1,0:T(8,128)(2,1)}, u32[]{:S(2)}, u32[]{:S(2)}) collective-permute-start(bf16[4,4,24,1920]{3,2,1,0:T(8,128)(2,1)} %bitcast.269), channel_id=1, source_target_pairs={{0,2},{2,0},{1,3},{3,1},{4,6},{6,4},{5,7},{7,5},{8,10},{10,8},{9,1... | collective-permute-start | bytes 4423688 | tf_op jit(solution)/shard_map/ppermute | solution.py:53
  212.2 43.4 %collective-permute-start.14 = (bf16[4,4,24,1920]{3,2,1,0:T(8,128)(2,1)}, bf16[4,4,24,1920]{3,2,1,0:T(8,128)(2,1)}, u32[]{:S(2)}, u32[]{:S(2)}) collective-permute-start(bf16[4,4,24,1920]{3,2,1,0:T(8,128)(2,1)} %bitcast.268), channel_id=1, source_target_pairs={{0,2},{2,0},{1,3},{3,1},{4,6},{6,4},{5,7},{7,5},{8,10},{10,8},{9,1... | collective-permute-start | bytes 4423688 | tf_op jit(solution)/shard_map/ppermute | solution.py:53
  212.7 47.1 %collective-permute-start.13 = (bf16[2,128,1536]{2,1,0:T(8,128)(2,1)}, bf16[2,128,1536]{2,1,0:T(8,128)(2,1)}, u32[]{:S(2)}, u32[]{:S(2)}) collective-permute-start(bf16[2,128,1536]{2,1,0:T(8,128)(2,1)} %get-tuple-element.93), channel_id=1, source_target_pairs={{0,1},{1,0},{2,3},{3,2},{4,5},{5,4},{6,7},{7,6},{8,9},{9,8},{10,11... | collective-permute-start | bytes 2359304 | tf_op jit(solution)/shard_map/ppermute | solution.py:53
  214.8 51.5 %all-to-all-start.3 = ((f32[16,2,3072]{2,1,0:T(2,128)}), f32[16,2,3072]{2,1,0:T(2,128)}, u32[]{:S(2)}, u32[]{:S(2)}) async-start(f32[16,2,3072]{2,1,0:T(2,128)} %broadcast_in_dim.27), calls=%async_computation.3 | async-start | bytes 786432 | tf_op jit(solution)/shard_map/all_to_all | solution.py:651
  238.9 31.0 %collective-permute-start.20 = (bf16[4,24,4608]{2,1,0:T(8,128)(2,1)}, bf16[4,24,4608]{2,1,0:T(8,128)(2,1)}, u32[]{:S(2)}, u32[]{:S(2)}) collective-permute-start(bf16[4,24,4608]{2,1,0:T(8,128)(2,1)} %fusion.96), channel_id=1, source_target_pairs={{0,4},{4,0},{1,5},{5,1},{2,6},{6,2},{3,7},{7,3},{8,12},{12,8},{9,1... | collective-permute-start | bytes 2654216 | tf_op jit(solution)/shard_map/ppermute | solution.py:53
  242.9 29.0 %collective-permute-start.19 = (bf16[4,24,4608]{2,1,0:T(8,128)(2,1)}, bf16[4,24,4608]{2,1,0:T(8,128)(2,1)}, u32[]{:S(2)}, u32[]{:S(2)}) collective-permute-start(bf16[4,24,4608]{2,1,0:T(8,128)(2,1)} %fusion.95), channel_id=1, source_target_pairs={{0,1},{1,0},{2,3},{3,2},{4,5},{5,4},{6,7},{7,6},{8,9},{9,8},{10,11... | collective-permute-start | bytes 2654216 | tf_op jit(solution)/shard_map/ppermute | solution.py:53
  255.6 20.7 %collective-permute-start.24 = (bf16[2,4,24,1920]{3,2,1,0:T(8,128)(2,1)}, bf16[2,4,24,1920]{3,2,1,0:T(8,128)(2,1)}, u32[]{:S(2)}, u32[]{:S(2)}) collective-permute-start(bf16[2,4,24,1920]{3,2,1,0:T(8,128)(2,1)} %get-tuple-element.156), channel_id=1, source_target_pairs={{0,4},{4,0},{1,5},{5,1},{2,6},{6,2},{3,7},{7,3},{8,12},{12,8},{9,1... | collective-permute-start | bytes 2211848 | tf_op jit(solution)/shard_map/ppermute | solution.py:53
  259.0 20.2 %collective-permute-start.18 = (bf16[2,4,24,1920]{3,2,1,0:T(8,128)(2,1)}, bf16[2,4,24,1920]{3,2,1,0:T(8,128)(2,1)}, u32[]{:S(2)}, u32[]{:S(2)}) collective-permute-start(bf16[2,4,24,1920]{3,2,1,0:T(8,128)(2,1)} %get-tuple-element.158), channel_id=1, source_target_pairs={{0,1},{1,0},{2,3},{3,2},{4,5},{5,4},{6,7},{7,6},{8,9},{9,8},{10,11... | collective-permute-start | bytes 2211848 | tf_op jit(solution)/shard_map/ppermute | solution.py:53
  265.0 20.2 %collective-permute-start.23 = (f32[2,1536]{1,0:T(2,128)S(1)}, f32[2,1536]{1,0:T(2,128)S(1)}, u32[]{:S(2)}, u32[]{:S(2)}) collective-permute-start(f32[2,1536]{1,0:T(2,128)S(1)} %pad_maximum_fusion.18), channel_id=1, source_target_pairs={{0,1},{1,0},{2,3},{3,2},{4,5},{5,4},{6,7},{7,6},{8,9},{9,8},{10,11... | collective-permute-start | bytes 36872 | tf_op jit(solution)/shard_map/ppermute | solution.py:53
  274.7 24.1 %collective-permute-start.22 = (bf16[2,24,9216]{2,1,0:T(8,128)(2,1)S(1)}, bf16[2,24,9216]{2,1,0:T(8,128)(2,1)}, u32[]{:S(2)}, u32[]{:S(2)}) collective-permute-start(bf16[2,24,9216]{2,1,0:T(8,128)(2,1)S(1)} %pad_maximum_fusion.4), channel_id=1, source_target_pairs={{0,8},{8,0},{16,24},{24,16},{1,9},{9,1},{17,25},{25,17},{2,10},{10... | collective-permute-start | bytes 2654216 | tf_op jit(solution)/shard_map/ppermute | solution.py:164
  281.0 22.9 %collective-permute-start.25 = (bf16[4,24,1920]{2,1,0:T(8,128)(2,1)}, bf16[4,24,1920]{2,1,0:T(8,128)(2,1)}, u32[]{:S(2)}, u32[]{:S(2)}) collective-permute-start(bf16[4,24,1920]{2,1,0:T(8,128)(2,1)} %fusion.133), channel_id=1, source_target_pairs={{0,1},{1,0},{2,3},{3,2},{4,5},{5,4},{6,7},{7,6},{8,9},{9,8},{10,11... | collective-permute-start | bytes 1105928 | tf_op jit(solution)/shard_map/ppermute | solution.py:53
  283.6 21.6 %collective-permute-start.21 = (bf16[4,24,1920]{2,1,0:T(8,128)(2,1)}, bf16[4,24,1920]{2,1,0:T(8,128)(2,1)}, u32[]{:S(2)}, u32[]{:S(2)}) collective-permute-start(bf16[4,24,1920]{2,1,0:T(8,128)(2,1)} %fusion.132), channel_id=1, source_target_pairs={{0,4},{4,0},{1,5},{5,1},{2,6},{6,2},{3,7},{7,3},{8,12},{12,8},{9,1... | collective-permute-start | bytes 1105928 | tf_op jit(solution)/shard_map/ppermute | solution.py:53
  286.0 31.0 %all-to-all-start.2 = ((f32[16,2,1536]{2,1,0:T(2,128)}), f32[16,2,1536]{2,1,0:T(2,128)S(1)}, u32[]{:S(2)}, u32[]{:S(2)}) async-start(f32[16,2,1536]{2,1,0:T(2,128)} %broadcast_in_dim.26), calls=%async_computation.2 | async-start | bytes 393216 | tf_op jit(solution)/shard_map/all_to_all | solution.py:651
  301.0 29.6 %collective-permute-start.29 = (bf16[1,24,9216]{2,1,0:T(8,128)(2,1)}, bf16[1,24,9216]{2,1,0:T(8,128)(2,1)}, u32[]{:S(2)}, u32[]{:S(2)}) collective-permute-start(bf16[1,24,9216]{2,1,0:T(8,128)(2,1)} %slice.318), channel_id=1, source_target_pairs={{0,16},{8,24},{16,0},{24,8},{1,17},{9,25},{17,1},{25,9},{2,18},{10... | collective-permute-start | bytes 1327112 | tf_op jit(solution)/shard_map/ppermute | solution.py:164
  306.5 23.6 %collective-permute-start.27 = (bf16[2,24,3840]{2,1,0:T(8,128)(2,1)S(1)}, bf16[2,24,3840]{2,1,0:T(8,128)(2,1)S(1)}, u32[]{:S(2)}, u32[]{:S(2)}) collective-permute-start(bf16[2,24,3840]{2,1,0:T(8,128)(2,1)S(1)} %pad_maximum_fusion.11), channel_id=1, source_target_pairs={{0,8},{8,0},{16,24},{24,16},{1,9},{9,1},{17,25},{25,17},{2,10},{10... | collective-permute-start | bytes 1105928 | tf_op jit(solution)/shard_map/ppermute | solution.py:164
  330.3 11.2 %collective-permute-start.28 = (bf16[1,24,3840]{2,1,0:T(8,128)(2,1)S(1)}, bf16[1,24,3840]{2,1,0:T(8,128)(2,1)S(1)}, u32[]{:S(2)}, u32[]{:S(2)}) collective-permute-start(bf16[1,24,3840]{2,1,0:T(8,128)(2,1)S(1)} %slice.321), channel_id=1, source_target_pairs={{0,16},{8,24},{16,0},{24,8},{1,17},{9,25},{17,1},{25,9},{2,18},{10... | collective-permute-start | bytes 552968 | tf_op jit(solution)/shard_map/ppermute | solution.py:164
  (61 other events, 401.9 us)
Sparse Core Ops, SparseCore 0:
  11.5 134.4 all-gather.1

commit v5 on v4

--- a/solution.py
+++ b/solution.py
@@ -680,17 +680,18 @@
     pair_sums = (jnp.zeros((TILE, pair.shape[3]), F32),)
     steps_all = chains * (local // TILE) // 2
     quarter = steps_all // 4
+    ahead = quarter + quarter // 2
 
     def more_pair(start, count, *needed):
         new_grad, new_sum = pair_back(after(scores_grad, *needed), pair, tall_pair, turn, start, count, *pair_sums)
         return (new_sum, new_grad)
 
     late_modes = share_modes(*late_halves, kept_sent[0])
-    pair_sums = more_pair(0, quarter, kept_sent[0])
+    pair_sums = more_pair(0, ahead, kept_sent[0])
     for s in feed_sums:
         s.got = after(s.got, pair_sums[0])
         s.second()
-    pair_sums = more_pair(quarter, quarter, *[s.give for s in feed_sums])
+    pair_sums = more_pair(ahead, 2 * quarter - ahead, *[s.give for s in feed_sums])
     late_modes = after(late_modes, pair_sums[0])
     for s in in_sums:
         s.got = after(s.got, pair_sums[0])
@@ -736,9 +737,10 @@
     time_pack = jnp.concatenate(
         [outer(features).reshape(devices, time_rows * own), grad_pair_w.reshape(devices, -1)], axis=1
     )
-    time_got = lax.all_to_all(time_pack, ALL, split_axis=0, concat_axis=0, tiled=True)
     in_line.got = after(in_line.got, time_pack)
     in_line.next()
+    time_pack = after(time_pack, in_line.sent)
+    time_got = lax.all_to_all(time_pack, ALL, split_axis=0, concat_axis=0, tiled=True)
     feed_total = feed_line.total(in_line.sent)
     early, late = jnp.split(feed_total, 2, axis=1)
     sum_gate, sum_up = early[:, :hidden_width], late[:, :hidden_width]

time: 357 us -> 356 us (level)
  waiting for transfers between devices: 62.4 us -> 56.8 us
  transfers between devices with their start and end apart: 36 -> 36, of which waited for: 9 -> 9; matrix products, arithmetic and copies ran while one was open for 27% -> 27% of each run, Pallas kernels for 24% -> 25%
where the time goes in v5:
time: 356 us; the launch traced here: 351 us
  Pallas kernels  115 us (32%)
  other arithmetic  67.2 us (19%)
  starting transfers between devices  60.2 us (17%)
  waiting for transfers between devices  56.8 us (16%)
  local copies, waits for them, and re-layouts  21 us (6%)
  between operations  15.5 us (4%)
  matrix products  15.3 us (4%)
    ppermute x23, waiting for transfers between devices, swap(): return lax.ppermute(value, axis, [(0, 1), (1, 0)])  36.3 us
    pallas_call x4, Pallas kernels, pair_back(): pl.pallas_call(pair_back_kernel, grid=(count,), in_specs=[pl.BlockSpec((1...  35.7 us
    convert_element_type x15, other arithmetic, add_low(): return (left.astype(F32) + right.astype(F32)).astype(BF16)  33.4 us
    pallas_call x1, Pallas kernels, feed(): pl.pallas_call(functools.partial(feed_kernel, steps), grid=(steps + group...  26.8 us
    ppermute x23, starting transfers between devices, swap(): return lax.ppermute(value, axis, [(0, 1), (1, 0)])  20.4 us
    pallas_call x1, Pallas kernels, pair_bias(): pl.pallas_call(bias_kernel, grid=(chains, blocks // group), in_specs=[pl....  15.8 us
    pallas_call x1, Pallas kernels, attend_back(): pl.pallas_call(functools.partial(attend_back_kernel, factor), grid=(chain...  12.1 us
    dot_general x19, matrix products, dot(): lax.dot_general(left, right, (dims, ((), ())), preferred_element_type=F32)  10.8 us
  transfers between devices with their start and end apart: 36, of which 9 were waited for; matrix products, arithmetic and copies ran while one was open for 27% of the time, Pallas kernels for 25%

profile of v5, /device:TPU:0, one launch (start us, length us, event | category | flops | bytes accessed | tf_op | source)
XLA Modules:
  0.0 351.4 jit_solution(18398445977675197835)
XLA Ops:
  10.8 5.0 %collective-permute-start.1 = (bf16[24,3840]{1,0:T(8,128)(2,1)}, bf16[24,3840]{1,0:T(8,128)(2,1)S(1)}, u32[]{:S(2)}, u32[]{:S(2)}) collective-permute-start(bf16[24,3840]{1,0:T(8,128)(2,1)} %join.2), channel_id=1, source_target_pairs={{0,24},{8,0},{16,8},{24,16},{1,25},{9,1},{17,9},{25,17},{2,26},{10... | collective-permute-start | bytes 552968 | tf_op jit(solution)/shard_map/ppermute | solution.py:57
  20.9 5.0 %all-to-all-start = ((f32[32,1,296]{2,1,0:T(1,128)}), f32[32,1,296]{2,1,0:T(1,128)S(1)}, u32[]{:S(2)}, u32[]{:S(2)}) async-start(f32[32,1,296]{2,1,0:T(1,128)} %copy.90), calls=%async_computation | async-start | bytes 98304 | tf_op jit(solution)/shard_map/all_to_all | solution.py:573
  31.8 10.8 %all-to-all-done = f32[32,1,296]{2,1,0:T(1,128)S(1)} async-done(((f32[32,1,296]{2,1,0:T(1,128)}), f32[32,1,296]{2,1,0:T(1,128)S(1)}, u32[]{:S(2)}, u32[]{:S(2)}) %all-to-all-start) | async-done | bytes 37920 | tf_op jit(solution)/shard_map/all_to_all | solution.py:573
  47.6 6.8 %all-to-all-start.1 = ((f32[16,2,4608]{2,1,0:T(2,128)}), f32[16,2,4608]{2,1,0:T(2,128)}, u32[]{:S(2)}, u32[]{:S(2)}) async-start(f32[16,2,4608]{2,1,0:T(2,128)} %reshape.1068), calls=%async_computation.1 | async-start | bytes 1179648 | tf_op jit(solution)/shard_map/all_to_all | solution.py:590
  54.7 2.1 collective-permute-start.8
  57.5 15.8 %pair_bias.1.bias_ref = f32[2,8,192,256]{3,2,1,0:T(8,128)} custom-call(bf16[2,128,256,256]{3,2,1,0:T(8,128)(2,1)} %pair_ref.8, bf16[256,192]{1,0:T(8,128)(2,1)} %copy.99.wide_ref), custom_call_target="tpu_custom_call" | custom-call | flops 6442450944 | bytes 33554432 | tf_op jit(solution)/shard_map/pair_bias/pallas_call | solution.py:191
  73.6 3.5 collective-permute-done.8
  85.1 21.0 %collective-permute-done = f32[2,4608]{1,0:T(2,128)S(1)} collective-permute-done((f32[2,4608]{1,0:T(2,128)S(1)}, f32[2,4608]{1,0:T(2,128)S(1)}, u32[]{:S(2)}, u32[]{:S(2)}) %collective-permute-start) | collective-permute-done | bytes 36896 | tf_op jit(solution)/shard_map/ppermute | solution.py:53
  112.4 4.7 %collective-permute-done.6 = bf16[4,2,24,1920]{3,2,0,1:T(8,128)(2,1)S(1)} collective-permute-done((bf16[4,2,24,1920]{3,2,0,1:T(8,128)(2,1)S(1)}, bf16[4,2,24,1920]{3,2,0,1:T(8,128)(2,1)S(1)}, u32[]{:S(2)}, u32[]{:S(2)}) %collective-permute-start.6) | collective-permute-done | bytes 737312 | tf_op jit(solution)/shard_map/ppermute | solution.py:53
  123.7 6.2 %project.1 = (bf16[256,768]{1,0:T(8,128)(2,1)}, bf16[512,768]{1,0:T(8,128)(2,1)}, bf16[512,768]{1,0:T(8,128)(2,1)}, f32[256,768]{1,0:T(8,128)}) custom-call(bf16[256,768]{1,0:T(8,128)(2,1)} %bitcast.225, bf16[512,768]{1,0:T(8,128)(2,1)} %bitcast.234, bf16[768,1920]{1,0:T(8,128)(2,1)} %bitcast.206, bf16[768,1920]{1,0:T(8,128)(2,1)} %bitcast.202), custom_call_target="tpu_custom_call" | custom-call | flops 1811939328 | bytes 7077888 | tf_op jit(solution)/shard_map/project/pallas_call | solution.py:496
  130.0 8.9 %attend.1 = (f32[2,8,192,256]{3,2,1,0:T(8,128)}, f32[256,768]{1,0:T(8,128)}) custom-call(f32[2,8,192,256]{3,2,1,0:T(8,128)} %pair_bias.1.bias_ref, bf16[256,768]{1,0:T(8,128)(2,1)} %get-tuple-element.78.q_ref, bf16[2,256,768]{2,1,0:T(8,128)(2,1)} %bitcast.270, bf16[2,256,768]{2,1,0:T(8,128)(2,1)} %bitcast.272, bf16[192,768]{1,0:T(8,128)(2,1)} %compare_convert_fusion.mask_ref), custom_call_target="tpu_custom_call" | custom-call | flops 2415919104 | bytes 7864320 | tf_op jit(solution)/shard_map/attend/pallas_call | solution.py:244
  146.0 26.8 %feed.1 = (f32[256,768]{1,0:T(8,128)}, f32[256,768]{1,0:T(8,128)}, bf16[4,4,24,4608]{3,2,1,0:T(8,128)(2,1)}, bf16[4,4,24,4608]{3,2,1,0:T(8,128)(2,1)}, bf16[4,4,...) custom-call(bf16[256,768]{1,0:T(8,128)(2,1)} %bitcast.255, bf16[2,768,256]{2,1,0:T(8,128)(2,1)} %pad_maximum_fusion.5.turned_ref, ...), custom_call_target="tpu_custom_call" | custom-call | flops 14495514624 | bytes 28311552 | tf_op jit(solution)/shard_map/feed/pallas_call | solution.py:437
  181.8 4.8 %add_convert_fusion = (bf16[2,4,24,4608]{3,2,1,0:T(8,128)(2,1)}, bf16[2,4,24,4608]{3,2,1,0:T(8,128)(2,1)}) fusion(bf16[4,4,24,4608]{3,2,1,0:T(8,128)(2,1)} %collective-permute-done.12, bf16[4,4,24,4608]{3,2,1,0:T(8,128)(2,1)S(1)} %copy-done.16), kind=kLoop, calls=%fused_computation | loop fusion | flops 7077888 | bytes 10616832 | tf_op jit(solution)/shard_map/convert_element_type | solution.py:61
  187.3 4.7 %add_convert_fusion.1 = (bf16[2,4,24,4608]{3,2,1,0:T(8,128)(2,1)}, bf16[2,4,24,4608]{3,2,1,0:T(8,128)(2,1)}) fusion(bf16[4,4,24,4608]{3,2,1,0:T(8,128)(2,1)} %collective-permute-done.11, bf16[4,4,24,4608]{3,2,1,0:T(8,128)(2,1)S(1)} %copy-done.15), kind=kLoop, calls=%fused_computation.1 | loop fusion | flops 7077888 | bytes 10616832 | tf_op jit(solution)/shard_map/convert_element_type | solution.py:61
  193.7 12.1 %attend_back.1 = (bf16[2,8,192,256]{3,2,1,0:T(8,128)(2,1)}, bf16[256,768]{1,0:T(8,128)(2,1)}, bf16[2,256,768]{2,1,0:T(8,128)(2,1)}, bf16[2,256,768]{2,1,0:T(8,12...) custom-call(s32[1]{0:T(128)} %bitcast.56.place_ref, ...), custom_call_target="tpu_custom_call" | custom-call | flops 6039797760 | bytes 4718592 | tf_op jit(solution)/shard_map/attend_back/pallas_call | solution.py:300
  205.8 6.4 %project_back.1 = (bf16[192,1920]{1,0:T(8,128)(2,1)}, bf16[192,1920]{1,0:T(8,128)(2,1)}, bf16[384,1920]{1,0:T(8,128)(2,1)}, bf16[192,1920]{1,0:T(8,128)(2,1)}, b...) custom-call(bf16[2,768,256]{2,1,0:T(8,128)(2,1)} %pad_maximum_fusion.7.own_ref, ...), custom_call_target="tpu_custom_call" | custom-call | flops 4831838208 | bytes 9437184 | tf_op jit(solution)/shard_map/project_back/pallas_call | solution.py:523
  216.2 4.7 %all-to-all-start.3 = ((f32[16,2,3072]{2,1,0:T(2,128)}), f32[16,2,3072]{2,1,0:T(2,128)}, u32[]{:S(2)}, u32[]{:S(2)}) async-start(f32[16,2,3072]{2,1,0:T(2,128)} %broadcast_in_dim.27), calls=%async_computation.3 | async-start | bytes 786432 | tf_op jit(solution)/shard_map/all_to_all | solution.py:651
  221.5 13.3 %pair_back.4 = (bf16[2,128,256,256]{3,2,1,0:T(8,128)(2,1)}, f32[16,256]{1,0:T(8,128)}) custom-call(bf16[2,8,192,256]{3,2,1,0:T(8,128)(2,1)} %get-tuple-element.124.ds_ref, bf16[2,128,256,256]{3,2,1,0:T(8,128)(2,1)} %pair_ref.8, bf16[192,256]{1,0:T(8,128)(2,1)} %bitcast.218, bf16[256,192]{1,0:T(8,128)(2,1)} %and_convert_fusion.turn_ref, ...), custom_call_target="tpu_custom_call" | custom-call | flops 4831838208 | bytes 25165824 | tf_op jit(solution)/shard_map/pair_back/pallas_call | solution.py:357
  234.8 2.7 fusion.96
  239.5 2.3 fusion.95
  242.1 6.1 %pair_back.5 = (bf16[2,128,256,256]{3,2,1,0:T(8,128)(2,1)}, f32[16,256]{1,0:T(8,128)}) custom-call(bf16[2,8,192,256]{3,2,1,0:T(8,128)(2,1)} %get-tuple-element.124.ds_ref, bf16[2,128,256,256]{3,2,1,0:T(8,128)(2,1)} %pair_ref.8, bf16[192,256]{1,0:T(8,128)(2,1)} %bitcast.219, ...), custom_call_target="tpu_custom_call", output_to_operand_aliasing={{0}: (5, {})} | custom-call | flops 1610612736 | bytes 8388608 | tf_op jit(solution)/shard_map/pair_back/pallas_call | solution.py:357
  248.3 3.4 fusion.22
  251.9 2.9 add_convert_fusion.10
  272.4 7.0 %collective-permute-done.23 = f32[2,1536]{1,0:T(2,128)S(1)} collective-permute-done((f32[2,1536]{1,0:T(2,128)S(1)}, f32[2,1536]{1,0:T(2,128)S(1)}, u32[]{:S(2)}, u32[]{:S(2)}) %collective-permute-start.23) | collective-permute-done | bytes 12320 | tf_op jit(solution)/shard_map/ppermute | solution.py:53
  280.2 4.9 %all-to-all-start.2 = ((f32[16,2,1536]{2,1,0:T(2,128)}), f32[16,2,1536]{2,1,0:T(2,128)S(1)}, u32[]{:S(2)}, u32[]{:S(2)}) async-start(f32[16,2,1536]{2,1,0:T(2,128)} %broadcast_in_dim.26), calls=%async_computation.2 | async-start | bytes 393216 | tf_op jit(solution)/shard_map/all_to_all | solution.py:651
  291.3 8.1 %pair_back.6 = (bf16[2,128,256,256]{3,2,1,0:T(8,128)(2,1)}, f32[16,256]{1,0:T(8,128)}) custom-call(bf16[2,8,192,256]{3,2,1,0:T(8,128)(2,1)} %get-tuple-element.124.ds_ref, bf16[2,128,256,256]{3,2,1,0:T(8,128)(2,1)} %pair_ref.8, bf16[192,256]{1,0:T(8,128)(2,1)} %bitcast.220, ...), custom_call_target="tpu_custom_call", output_to_operand_aliasing={{0}: (5, {})} | custom-call | flops 3221225472 | bytes 16777216 | tf_op jit(solution)/shard_map/pair_back/pallas_call | solution.py:357
  306.5 2.4 collective-permute-start.29
  308.9 8.1 %pair_back.7 = (bf16[2,128,256,256]{3,2,1,0:T(8,128)(2,1)}, f32[16,256]{1,0:T(8,128)}) custom-call(bf16[2,8,192,256]{3,2,1,0:T(8,128)(2,1)} %get-tuple-element.124.ds_ref, bf16[2,128,256,256]{3,2,1,0:T(8,128)(2,1)} %pair_ref.8, bf16[192,256]{1,0:T(8,128)(2,1)} %bitcast.221, ...), custom_call_target="tpu_custom_call", output_to_operand_aliasing={{0}: (5, {})} | custom-call | flops 3221225472 | bytes 16777216 | tf_op jit(solution)/shard_map/pair_back/pallas_call | solution.py:357
  323.8 3.7 %all-to-all-start.4 = ((f32[32,1,288]{2,1,0:T(1,128)}), f32[32,1,288]{2,1,0:T(1,128)S(1)}, u32[]{:S(2)}, u32[]{:S(2)}) async-start(f32[32,1,288]{2,1,0:T(1,128)} %copy.109), calls=%async_computation.4 | async-start | bytes 98304 | tf_op jit(solution)/shard_map/all_to_all | solution.py:743
  328.4 2.7 collective-permute-start.28
  331.1 3.9 %all-to-all-done.4 = f32[32,1,288]{2,1,0:T(1,128)S(1)} async-done(((f32[32,1,288]{2,1,0:T(1,128)}), f32[32,1,288]{2,1,0:T(1,128)S(1)}, u32[]{:S(2)}, u32[]{:S(2)}) %all-to-all-start.4) | async-done | bytes 36896 | tf_op jit(solution)/shard_map/all_to_all | solution.py:743
  336.8 3.8 %collective-permute-done.28 = bf16[1,24,3840]{2,1,0:T(8,128)(2,1)S(1)} collective-permute-done((bf16[1,24,3840]{2,1,0:T(8,128)(2,1)S(1)}, bf16[1,24,3840]{2,1,0:T(8,128)(2,1)S(1)}, u32[]{:S(2)}, u32[]{:S(2)}) %collective-permute-start.28) | collective-permute-done | bytes 184352 | tf_op jit(solution)/shard_map/ppermute | solution.py:164
  (359 shorter events, 111.1 us)
Async XLA Ops:
  7.2 138.8 %all-gather.2.cloned.1.call-start = ((), (), s32[]{:S(2)}) async-start(), calls=%async_computation.5 | async-start | bytes 14598144 | tf_op jit(solution)/shard_map/all_gather | solution.py:555
  10.8 43.6 %collective-permute-start.1 = (bf16[24,3840]{1,0:T(8,128)(2,1)}, bf16[24,3840]{1,0:T(8,128)(2,1)S(1)}, u32[]{:S(2)}, u32[]{:S(2)}) collective-permute-start(bf16[24,3840]{1,0:T(8,128)(2,1)} %join.2), channel_id=1, source_target_pairs={{0,24},{8,0},{16,8},{24,16},{1,25},{9,1},{17,9},{25,17},{2,26},{10... | collective-permute-start | bytes 552968 | tf_op jit(solution)/shard_map/ppermute | solution.py:57
  15.9 38.6 %collective-permute-start.2 = (bf16[24,3840]{1,0:T(8,128)(2,1)}, bf16[24,3840]{1,0:T(8,128)(2,1)S(1)}, u32[]{:S(2)}, u32[]{:S(2)}) collective-permute-start(bf16[24,3840]{1,0:T(8,128)(2,1)} %join.2), channel_id=1, source_target_pairs={{0,16},{8,24},{16,0},{24,8},{1,17},{9,25},{17,1},{25,9},{2,18},{10... | collective-permute-start | bytes 552968 | tf_op jit(solution)/shard_map/ppermute | solution.py:57
  15.9 38.6 %collective-permute-start.3 = (bf16[24,3840]{1,0:T(8,128)(2,1)}, bf16[24,3840]{1,0:T(8,128)(2,1)S(1)}, u32[]{:S(2)}, u32[]{:S(2)}) collective-permute-start(bf16[24,3840]{1,0:T(8,128)(2,1)} %join.2), channel_id=1, source_target_pairs={{0,8},{8,16},{16,24},{24,0},{1,9},{9,17},{17,25},{25,1},{2,10},{10... | collective-permute-start | bytes 552968 | tf_op jit(solution)/shard_map/ppermute | solution.py:57
  20.9 21.7 %all-to-all-start = ((f32[32,1,296]{2,1,0:T(1,128)}), f32[32,1,296]{2,1,0:T(1,128)S(1)}, u32[]{:S(2)}, u32[]{:S(2)}) async-start(f32[32,1,296]{2,1,0:T(1,128)} %copy.90), calls=%async_computation | async-start | bytes 98304 | tf_op jit(solution)/shard_map/all_to_all | solution.py:573
  26.0 47.3 %collective-permute-start.4 = (bf16[2,128,768]{2,1,0:T(8,128)(2,1)S(1)}, bf16[2,128,768]{2,1,0:T(8,128)(2,1)S(1)}, u32[]{:S(2)}, u32[]{:S(2)}) collective-permute-start(bf16[2,128,768]{2,1,0:T(8,128)(2,1)S(1)} %copy-done.6), channel_id=1, source_target_pairs={{0,1},{1,0},{2,3},{3,2},{4,5},{5,4},{6,7},{7,6},{8,9},{9,8},{10,11... | collective-permute-start | bytes 1179656 | tf_op jit(solution)/shard_map/ppermute | solution.py:53
  47.6 35.1 %all-to-all-start.1 = ((f32[16,2,4608]{2,1,0:T(2,128)}), f32[16,2,4608]{2,1,0:T(2,128)}, u32[]{:S(2)}, u32[]{:S(2)}) async-start(f32[16,2,4608]{2,1,0:T(2,128)} %reshape.1068), calls=%async_computation.1 | async-start | bytes 1179648 | tf_op jit(solution)/shard_map/all_to_all | solution.py:590
  54.7 22.4 %collective-permute-start.8 = (bf16[4,24,1920]{2,1,0:T(8,128)(2,1)S(1)}, bf16[4,24,1920]{2,1,0:T(8,128)(2,1)S(1)}, u32[]{:S(2)}, u32[]{:S(2)}) collective-permute-start(bf16[4,24,1920]{2,1,0:T(8,128)(2,1)S(1)} %get-tuple-element.163), channel_id=1, source_target_pairs={{0,4},{4,0},{1,5},{5,1},{2,6},{6,2},{3,7},{7,3},{8,12},{12,8},{9,1... | collective-permute-start | bytes 1105928 | tf_op jit(solution)/shard_map/ppermute | solution.py:53
  56.8 22.8 %collective-permute-start.5 = (bf16[4,24,1920]{2,1,0:T(8,128)(2,1)S(1)}, bf16[4,24,1920]{2,1,0:T(8,128)(2,1)S(1)}, u32[]{:S(2)}, u32[]{:S(2)}) collective-permute-start(bf16[4,24,1920]{2,1,0:T(8,128)(2,1)S(1)} %get-tuple-element.164), channel_id=1, source_target_pairs={{0,1},{1,0},{2,3},{3,2},{4,5},{5,4},{6,7},{7,6},{8,9},{9,8},{10,11... | collective-permute-start | bytes 1105928 | tf_op jit(solution)/shard_map/ppermute | solution.py:53
  78.1 33.9 %collective-permute-start.9 = (bf16[4,2,24,1920]{3,2,0,1:T(8,128)(2,1)}, bf16[4,2,24,1920]{3,2,0,1:T(8,128)(2,1)S(1)}, u32[]{:S(2)}, u32[]{:S(2)}) collective-permute-start(bf16[4,2,24,1920]{3,2,0,1:T(8,128)(2,1)} %maximum_select_fusion.8), channel_id=1, source_target_pairs={{0,1},{1,0},{2,3},{3,2},{4,5},{5,4},{6,7},{7,6},{8,9},{9,8},{10,11... | collective-permute-start | bytes 2211848 | tf_op jit(solution)/shard_map/ppermute | solution.py:53
  84.0 22.2 %collective-permute-start = (f32[2,4608]{1,0:T(2,128)S(1)}, f32[2,4608]{1,0:T(2,128)S(1)}, u32[]{:S(2)}, u32[]{:S(2)}) collective-permute-start(f32[2,4608]{1,0:T(2,128)S(1)} %reduce_sum.162), channel_id=1, source_target_pairs={{0,1},{1,0},{2,3},{3,2},{4,5},{5,4},{6,7},{7,6},{8,9},{9,8},{10,11... | collective-permute-start | bytes 110600 | tf_op jit(solution)/shard_map/ppermute | solution.py:53
  84.7 32.3 %collective-permute-start.6 = (bf16[4,2,24,1920]{3,2,0,1:T(8,128)(2,1)S(1)}, bf16[4,2,24,1920]{3,2,0,1:T(8,128)(2,1)S(1)}, u32[]{:S(2)}, u32[]{:S(2)}) collective-permute-start(bf16[4,2,24,1920]{3,2,0,1:T(8,128)(2,1)S(1)} %maximum_select_fusion.6), channel_id=1, source_target_pairs={{0,4},{4,0},{1,5},{5,1},{2,6},{6,2},{3,7},{7,3},{8,12},{12,8},{9,1... | collective-permute-start | bytes 2211848 | tf_op jit(solution)/shard_map/ppermute | solution.py:53
  173.2 14.2 %collective-permute-start.11 = (bf16[4,4,24,4608]{3,2,1,0:T(8,128)(2,1)}, bf16[4,4,24,4608]{3,2,1,0:T(8,128)(2,1)}, u32[]{:S(2)}, u32[]{:S(2)}) collective-permute-start(bf16[4,4,24,4608]{3,2,1,0:T(8,128)(2,1)} %get-tuple-element.88), channel_id=1, source_target_pairs={{0,2},{2,0},{1,3},{3,1},{4,6},{6,4},{5,7},{7,5},{8,10},{10,8},{9,1... | collective-permute-start | bytes 10616840 | tf_op jit(solution)/shard_map/ppermute | solution.py:53
  177.9 34.7 %collective-permute-start.26 = (f32[2,3072]{1,0:T(2,128)S(1)}, f32[2,3072]{1,0:T(2,128)S(1)}, u32[]{:S(2)}, u32[]{:S(2)}) collective-permute-start(f32[2,3072]{1,0:T(2,128)S(1)} %pad_maximum_fusion.16), channel_id=1, source_target_pairs={{0,1},{1,0},{2,3},{3,2},{4,5},{5,4},{6,7},{7,6},{8,9},{9,8},{10,11... | collective-permute-start | bytes 73736 | tf_op jit(solution)/shard_map/ppermute | solution.py:53
  186.6 48.2 %collective-permute-start.16 = (bf16[2,4,24,4608]{3,2,1,0:T(8,128)(2,1)}, bf16[2,4,24,4608]{3,2,1,0:T(8,128)(2,1)}, u32[]{:S(2)}, u32[]{:S(2)}) collective-permute-start(bf16[2,4,24,4608]{3,2,1,0:T(8,128)(2,1)} %get-tuple-element.148), channel_id=1, source_target_pairs={{0,1},{1,0},{2,3},{3,2},{4,5},{5,4},{6,7},{7,6},{8,9},{9,8},{10,11... | collective-permute-start | bytes 5308424 | tf_op jit(solution)/shard_map/ppermute | solution.py:53
  192.0 45.4 %collective-permute-start.15 = (bf16[2,4,24,4608]{3,2,1,0:T(8,128)(2,1)}, bf16[2,4,24,4608]{3,2,1,0:T(8,128)(2,1)}, u32[]{:S(2)}, u32[]{:S(2)}) collective-permute-start(bf16[2,4,24,4608]{3,2,1,0:T(8,128)(2,1)} %get-tuple-element.150), channel_id=1, source_target_pairs={{0,4},{4,0},{1,5},{5,1},{2,6},{6,2},{3,7},{7,3},{8,12},{12,8},{9,1... | collective-permute-start | bytes 5308424 | tf_op jit(solution)/shard_map/ppermute | solution.py:53
  212.1 36.1 %collective-permute-start.17 = (bf16[4,4,24,1920]{3,2,1,0:T(8,128)(2,1)}, bf16[4,4,24,1920]{3,2,1,0:T(8,128)(2,1)}, u32[]{:S(2)}, u32[]{:S(2)}) collective-permute-start(bf16[4,4,24,1920]{3,2,1,0:T(8,128)(2,1)} %bitcast.269), channel_id=1, source_target_pairs={{0,2},{2,0},{1,3},{3,1},{4,6},{6,4},{5,7},{7,5},{8,10},{10,8},{9,1... | collective-permute-start | bytes 4423688 | tf_op jit(solution)/shard_map/ppermute | solution.py:53
  212.1 39.6 %collective-permute-start.14 = (bf16[4,4,24,1920]{3,2,1,0:T(8,128)(2,1)}, bf16[4,4,24,1920]{3,2,1,0:T(8,128)(2,1)}, u32[]{:S(2)}, u32[]{:S(2)}) collective-permute-start(bf16[4,4,24,1920]{3,2,1,0:T(8,128)(2,1)} %bitcast.268), channel_id=1, source_target_pairs={{0,2},{2,0},{1,3},{3,1},{4,6},{6,4},{5,7},{7,5},{8,10},{10,8},{9,1... | collective-permute-start | bytes 4423688 | tf_op jit(solution)/shard_map/ppermute | solution.py:53
  212.7 43.6 %collective-permute-start.13 = (bf16[2,128,1536]{2,1,0:T(8,128)(2,1)}, bf16[2,128,1536]{2,1,0:T(8,128)(2,1)}, u32[]{:S(2)}, u32[]{:S(2)}) collective-permute-start(bf16[2,128,1536]{2,1,0:T(8,128)(2,1)} %get-tuple-element.94), channel_id=1, source_target_pairs={{0,1},{1,0},{2,3},{3,2},{4,5},{5,4},{6,7},{7,6},{8,9},{9,8},{10,11... | collective-permute-start | bytes 2359304 | tf_op jit(solution)/shard_map/ppermute | solution.py:53
  216.2 45.9 %all-to-all-start.3 = ((f32[16,2,3072]{2,1,0:T(2,128)}), f32[16,2,3072]{2,1,0:T(2,128)}, u32[]{:S(2)}, u32[]{:S(2)}) async-start(f32[16,2,3072]{2,1,0:T(2,128)} %broadcast_in_dim.27), calls=%async_computation.3 | async-start | bytes 786432 | tf_op jit(solution)/shard_map/all_to_all | solution.py:651
  237.5 28.2 %collective-permute-start.20 = (bf16[4,24,4608]{2,1,0:T(8,128)(2,1)}, bf16[4,24,4608]{2,1,0:T(8,128)(2,1)}, u32[]{:S(2)}, u32[]{:S(2)}) collective-permute-start(bf16[4,24,4608]{2,1,0:T(8,128)(2,1)} %fusion.96), channel_id=1, source_target_pairs={{0,4},{4,0},{1,5},{5,1},{2,6},{6,2},{3,7},{7,3},{8,12},{12,8},{9,1... | collective-permute-start | bytes 2654216 | tf_op jit(solution)/shard_map/ppermute | solution.py:53
  241.8 25.8 %collective-permute-start.19 = (bf16[4,24,4608]{2,1,0:T(8,128)(2,1)}, bf16[4,24,4608]{2,1,0:T(8,128)(2,1)}, u32[]{:S(2)}, u32[]{:S(2)}) collective-permute-start(bf16[4,24,4608]{2,1,0:T(8,128)(2,1)} %fusion.95), channel_id=1, source_target_pairs={{0,1},{1,0},{2,3},{3,2},{4,5},{5,4},{6,7},{7,6},{8,9},{9,8},{10,11... | collective-permute-start | bytes 2654216 | tf_op jit(solution)/shard_map/ppermute | solution.py:53
  251.7 33.4 %collective-permute-start.24 = (bf16[2,4,24,1920]{3,2,1,0:T(8,128)(2,1)}, bf16[2,4,24,1920]{3,2,1,0:T(8,128)(2,1)}, u32[]{:S(2)}, u32[]{:S(2)}) collective-permute-start(bf16[2,4,24,1920]{3,2,1,0:T(8,128)(2,1)} %get-tuple-element.158), channel_id=1, source_target_pairs={{0,4},{4,0},{1,5},{5,1},{2,6},{6,2},{3,7},{7,3},{8,12},{12,8},{9,1... | collective-permute-start | bytes 2211848 | tf_op jit(solution)/shard_map/ppermute | solution.py:53
  254.8 32.2 %collective-permute-start.18 = (bf16[2,4,24,1920]{3,2,1,0:T(8,128)(2,1)}, bf16[2,4,24,1920]{3,2,1,0:T(8,128)(2,1)}, u32[]{:S(2)}, u32[]{:S(2)}) collective-permute-start(bf16[2,4,24,1920]{3,2,1,0:T(8,128)(2,1)} %get-tuple-element.160), channel_id=1, source_target_pairs={{0,1},{1,0},{2,3},{3,2},{4,5},{5,4},{6,7},{7,6},{8,9},{9,8},{10,11... | collective-permute-start | bytes 2211848 | tf_op jit(solution)/shard_map/ppermute | solution.py:53
  261.5 18.0 %collective-permute-start.23 = (f32[2,1536]{1,0:T(2,128)S(1)}, f32[2,1536]{1,0:T(2,128)S(1)}, u32[]{:S(2)}, u32[]{:S(2)}) collective-permute-start(f32[2,1536]{1,0:T(2,128)S(1)} %pad_maximum_fusion.18), channel_id=1, source_target_pairs={{0,1},{1,0},{2,3},{3,2},{4,5},{5,4},{6,7},{7,6},{8,9},{9,8},{10,11... | collective-permute-start | bytes 36872 | tf_op jit(solution)/shard_map/ppermute | solution.py:53
  270.5 29.0 %collective-permute-start.22 = (bf16[2,24,9216]{2,1,0:T(8,128)(2,1)S(1)}, bf16[2,24,9216]{2,1,0:T(8,128)(2,1)}, u32[]{:S(2)}, u32[]{:S(2)}) collective-permute-start(bf16[2,24,9216]{2,1,0:T(8,128)(2,1)S(1)} %pad_maximum_fusion.4), channel_id=1, source_target_pairs={{0,8},{8,0},{16,24},{24,16},{1,9},{9,1},{17,25},{25,17},{2,10},{10... | collective-permute-start | bytes 2654216 | tf_op jit(solution)/shard_map/ppermute | solution.py:164
  280.2 37.6 %all-to-all-start.2 = ((f32[16,2,1536]{2,1,0:T(2,128)}), f32[16,2,1536]{2,1,0:T(2,128)S(1)}, u32[]{:S(2)}, u32[]{:S(2)}) async-start(f32[16,2,1536]{2,1,0:T(2,128)} %broadcast_in_dim.26), calls=%async_computation.2 | async-start | bytes 393216 | tf_op jit(solution)/shard_map/all_to_all | solution.py:651
  287.0 14.7 %collective-permute-start.25 = (bf16[4,24,1920]{2,1,0:T(8,128)(2,1)}, bf16[4,24,1920]{2,1,0:T(8,128)(2,1)}, u32[]{:S(2)}, u32[]{:S(2)}) collective-permute-start(bf16[4,24,1920]{2,1,0:T(8,128)(2,1)} %fusion.133), channel_id=1, source_target_pairs={{0,1},{1,0},{2,3},{3,2},{4,5},{5,4},{6,7},{7,6},{8,9},{9,8},{10,11... | collective-permute-start | bytes 1105928 | tf_op jit(solution)/shard_map/ppermute | solution.py:53
  289.3 13.7 %collective-permute-start.21 = (bf16[4,24,1920]{2,1,0:T(8,128)(2,1)}, bf16[4,24,1920]{2,1,0:T(8,128)(2,1)}, u32[]{:S(2)}, u32[]{:S(2)}) collective-permute-start(bf16[4,24,1920]{2,1,0:T(8,128)(2,1)} %fusion.132), channel_id=1, source_target_pairs={{0,4},{4,0},{1,5},{5,1},{2,6},{6,2},{3,7},{7,3},{8,12},{12,8},{9,1... | collective-permute-start | bytes 1105928 | tf_op jit(solution)/shard_map/ppermute | solution.py:53
  305.1 18.0 %collective-permute-start.27 = (bf16[2,24,3840]{2,1,0:T(8,128)(2,1)}, bf16[2,24,3840]{2,1,0:T(8,128)(2,1)S(1)}, u32[]{:S(2)}, u32[]{:S(2)}) collective-permute-start(bf16[2,24,3840]{2,1,0:T(8,128)(2,1)} %pad_maximum_fusion.11), channel_id=1, source_target_pairs={{0,8},{8,0},{16,24},{24,16},{1,9},{9,1},{17,25},{25,17},{2,10},{10... | collective-permute-start | bytes 1105928 | tf_op jit(solution)/shard_map/ppermute | solution.py:164
  306.5 28.5 %collective-permute-start.29 = (bf16[1,24,9216]{2,1,0:T(8,128)(2,1)}, bf16[1,24,9216]{2,1,0:T(8,128)(2,1)S(1)}, u32[]{:S(2)}, u32[]{:S(2)}) collective-permute-start(bf16[1,24,9216]{2,1,0:T(8,128)(2,1)} %slice.318), channel_id=1, source_target_pairs={{0,16},{8,24},{16,0},{24,8},{1,17},{9,25},{17,1},{25,9},{2,18},{10... | collective-permute-start | bytes 1327112 | tf_op jit(solution)/shard_map/ppermute | solution.py:164
  328.4 12.2 %collective-permute-start.28 = (bf16[1,24,3840]{2,1,0:T(8,128)(2,1)S(1)}, bf16[1,24,3840]{2,1,0:T(8,128)(2,1)S(1)}, u32[]{:S(2)}, u32[]{:S(2)}) collective-permute-start(bf16[1,24,3840]{2,1,0:T(8,128)(2,1)S(1)} %slice.320), channel_id=1, source_target_pairs={{0,16},{8,24},{16,0},{24,8},{1,17},{9,25},{17,1},{25,9},{2,18},{10... | collective-permute-start | bytes 552968 | tf_op jit(solution)/shard_map/ppermute | solution.py:164
  (62 other events, 405.4 us)
Sparse Core Ops, SparseCore 0:
  11.5 134.4 all-gather.1
